TPU v7x, 128 devices: a whole 4x4x4 slice. The times are simulated.
128 devices in a mesh: lat: 8 (over x, core), lon: 16 (over z, y).
Axes of the slice: x: 4, y: 4, z: 4, core: 2. Of those that a mesh axis runs over, the one named last changes fastest.
Arguments:
- noisy: bfloat16 [64, 128, 20480], P(None, 'lat', 'lon'), may hold values from -6 to 6
- coarse: bfloat16 [8, 64, 30, 128], P('lat', 'lon'), may hold values from -6 to 6
- owner: int32 [8, 16, 4, 4], P('lat', 'lon'), may hold values from 0 to 15, as said below
- local_slot: int32 [8, 16, 4, 4], P('lat', 'lon'), may hold values from 0 to 3
- weight_id: int32 [8, 16, 4, 4], P('lat', 'lon'), may hold values from 0 to 3
- counts: int32 [8, 16, 4], P('lat', 'lon'), may hold values from 1 to 4, 12 in all within a row
- interp_table: bfloat16 [4, 128, 5120], replicated, may hold values from -0.3125 to 0.3125
- conv_in: bfloat16 [3, 3, 64, 64], replicated, may hold values from -0.25 to 0.25
- conv_cond: bfloat16 [3, 3, 64, 30], replicated, may hold values from -0.375 to 0.375
- bias_in: float32 [64], replicated, may hold values from -4 to 4
- conv_out: bfloat16 [3, 3, 64, 64], replicated, may hold values from -0.25 to 0.25
- bias_out: float32 [64], replicated, may hold values from -4 to 4
Outputs:
- updated: bfloat16 [64, 128, 20480], P(None, 'lat', 'lon')
Inputs may be any that keep to these rules, and one draw needn't show every extreme that they name: `owner`: in the lists of one device (its 4 x 4 slots, live or not) no lon index is named by more than 6 slots, and some is named by exactly 6. The 4 counts of one device sum to 12, and the largest is 4.
All inputs are finite; a program needn't handle non-finite values.
Results may differ from a plain program's by a relative error of at most 0.0041.
Values may be sent and summed in bfloat16 or wider, within the bound.
No kernel may reach another device: no remote copies, remote signals or barrier semaphores. Data moves between devices by JAX's collectives and lax.ppermute only.
A program may use at most 256 MiB of HBM per device.

v0:
```python
import jax
import jax.numpy as jnp
from jax import lax
from jax.sharding import PartitionSpec as P

CAP = 6


def padded_2(cells, sides, width):
    for axis, dim in sides:
        count = lax.axis_size(axis)
        head = lax.slice_in_dim(cells, 0, width, axis=dim)
        tail = lax.slice_in_dim(cells, cells.shape[dim] - width, cells.shape[dim], axis=dim)
        cells = jnp.concatenate(
            [
                lax.ppermute(tail, axis, [(i, (i + 1) % count) for i in range(count)]),
                cells,
                lax.ppermute(head, axis, [((i + 1) % count, i) for i in range(count)]),
            ],
            axis=dim,
        )
    return cells


def conv_sum(padded, kernel, rows, cols):
    total = jnp.zeros((kernel.shape[2], rows, cols), jnp.float32)
    for shift_r in range(3):
        for shift_c in range(3):
            window = padded[:, shift_r : shift_r + rows, shift_c : shift_c + cols]
            total = total + jnp.einsum(
                "oc,crw->orw", kernel[shift_r, shift_c], window, preferred_element_type=jnp.float32
            )
    return total


def clear_edges(padded, width, tile_rows):
    lat_pos = lax.axis_index("lat")
    lat_count = lax.axis_size("lat")
    row_ids = lax.broadcasted_iota(jnp.int32, (1, padded.shape[1], 1), 1)
    upper = (row_ids < width) & (lat_pos == 0)
    lower = (row_ids >= tile_rows + width) & (lat_pos == lat_count - 1)
    return jnp.where(upper | lower, jnp.zeros_like(padded), padded)


def local(
    noisy,
    coarse,
    owner,
    local_slot,
    weight_id,
    counts,
    interp_table,
    conv_in,
    conv_cond,
    bias_in,
    conv_out,
    bias_out,
):
    channels, tile_rows, tile_cols = noisy.shape
    subs = owner.shape[2]
    slots = owner.shape[3]
    cc_count = coarse.shape[2]
    cells = coarse.shape[3]
    held = coarse.shape[1]
    kinds = interp_table.shape[0]
    total_slots = subs * slots
    peers = lax.axis_size("lon")
    owned = owner.reshape(total_slots)
    within = local_slot.reshape(total_slots)
    live = (lax.broadcasted_iota(jnp.int32, (subs, slots), 1) < counts.reshape(subs, 1)).reshape(
        total_slots
    )
    hits = (
        (owned[:, None] == lax.broadcasted_iota(jnp.int32, (1, peers), 1)) & live[:, None]
    ).astype(jnp.int32)
    before = jnp.cumsum(hits, axis=0) - hits
    place = jnp.sum(before * hits, axis=1)
    placing = hits[:, :, None] * (
        place[:, None, None] == lax.broadcasted_iota(jnp.int32, (1, 1, CAP), 2)
    ).astype(jnp.int32)
    wanted = jnp.sum(placing * (within[:, None, None] + 1), axis=0) - 1
    picks = (
        lax.all_to_all(wanted, "lon", split_axis=0, concat_axis=0, tiled=True)[:, :, None]
        == lax.broadcasted_iota(jnp.int32, (1, 1, held), 2)
    ).astype(jnp.bfloat16)
    found = jnp.einsum(
        "pnb,bcx->pncx", picks, coarse[0], preferred_element_type=jnp.float32
    ).astype(jnp.bfloat16)
    arrived = lax.all_to_all(found, "lon", split_axis=0, concat_axis=0, tiled=True)
    slot_blocks = jnp.einsum(
        "lpn,pncx->lcx", placing.astype(jnp.bfloat16), arrived, preferred_element_type=jnp.float32
    ).astype(jnp.bfloat16)
    slot_blocks = slot_blocks.reshape(subs, slots, cc_count, cells)
    onehot = (
        weight_id.reshape(subs, slots)[:, :, None]
        == lax.broadcasted_iota(jnp.int32, (1, 1, kinds), 2)
    ).astype(jnp.bfloat16)
    grouped = jnp.einsum(
        "skw,skcb->scwb", onehot, slot_blocks, preferred_element_type=jnp.float32
    ).astype(jnp.bfloat16)
    grouped = grouped.reshape(subs, cc_count, kinds * cells)
    table = interp_table.reshape(kinds * cells, interp_table.shape[2])
    tiles = jnp.einsum("scj,jf->scf", grouped, table, preferred_element_type=jnp.float32).astype(
        jnp.bfloat16
    )
    cond = jnp.transpose(
        tiles.reshape(subs, cc_count, tile_rows // subs, tile_cols), (1, 0, 2, 3)
    ).reshape(cc_count, tile_rows, tile_cols)
    stacked = jnp.concatenate([noisy, cond], axis=0)
    padded = padded_2(stacked, (("lat", 1), ("lon", 2)), 1)
    padded = clear_edges(padded, 1, tile_rows)
    hidden = conv_sum(padded[:channels], conv_in, tile_rows, tile_cols) + conv_sum(
        padded[channels:], conv_cond, tile_rows, tile_cols
    )
    act = jax.nn.silu(hidden + bias_in[:, None, None]).astype(jnp.bfloat16)
    act_padded = padded_2(act, (("lat", 1), ("lon", 2)), 1)
    act_padded = clear_edges(act_padded, 1, tile_rows)
    result = (
        noisy.astype(jnp.float32)
        + conv_sum(act_padded, conv_out, tile_rows, tile_cols)
        + bias_out[:, None, None]
    )
    return result.astype(jnp.bfloat16)


def solution(mesh):
    in_specs = (
        P(None, "lat", "lon"),
        P("lat", "lon", None, None),
        P("lat", "lon", None, None),
        P("lat", "lon", None, None),
        P("lat", "lon", None, None),
        P("lat", "lon", None),
        P(),
        P(),
        P(),
        P(),
        P(),
        P(),
    )
    out_specs = P(None, "lat", "lon")
    return jax.shard_map(local, mesh=mesh, in_specs=in_specs, out_specs=out_specs, check_vma=False)
```

profile of v0, /device:TPU:1, one launch (start us, length us, event | category | flops | bytes accessed | tf_op | source)
XLA Modules:
  0.0 248.8 jit_solution(6555738713048006042)
XLA Ops:
  2.9 14.8 %all_to_all.11 = s32[16,1,6]{2,1,0:T(1,128)S(1)} all-to-all(s32[16,1,6]{2,1,0:T(1,128)S(1)} %copy.36), channel_id=1, replica_groups=mesh['lat'=8,'lon'=16] {'lon'}, dimensions={0} | all-to-all | bytes 768 | tf_op jit(solution)/shard_map/all_to_all | solution.py:83
  19.4 3.6 %all-to-all-start.1 = ((bf16[16,6,30,128]{3,2,1,0:T(8,128)(2,1)}), bf16[16,6,30,128]{3,2,1,0:T(8,128)(2,1)S(1)}, u32[]{:S(2)}, u32[]{:S(2)}) async-start(bf16[16,6,30,128]{3,2,1,0:T(8,128)(2,1)} %copy.38), calls=%async_computation.1 | async-start | bytes 1572864 | tf_op jit(solution)/shard_map/all_to_all | solution.py:89
  23.0 2.5 %copy.35 = bf16[64,16,1280]{2,0,1:T(8,128)(2,1)S(1)} copy(bf16[64,16,1280]{2,1,0:T(8,128)(2,1)} %param.12) | data formatting | bytes 5242880 | tf_op args[0]
  25.5 9.8 %all-to-all-done.1 = bf16[16,6,30,128]{3,2,1,0:T(8,128)(2,1)S(1)} async-done(((bf16[16,6,30,128]{3,2,1,0:T(8,128)(2,1)}), bf16[16,6,30,128]{3,2,1,0:T(8,128)(2,1)S(1)}, u32[]{:S(2)}, u32[]{:S(2)}) %all-to-all-start.1) | async-done | bytes 737312 | tf_op jit(solution)/shard_map/all_to_all | solution.py:89
  36.4 4.4 %fusion = bf16[4,30,5120]{2,1,0:T(8,128)(2,1)} fusion(bf16[4,128,5120]{2,1,0:T(8,128)(2,1)} %param.18, bf16[4,30,4,128]{3,2,1,0:T(4,128)(2,1)S(1)} %fusion.67), kind=kOutput, calls=%fused_computation.1 | convolution fusion | flops 629760000 | bytes 6594560 | tf_op jit(solution)/shard_map/scj,jf->scf/dot_general | solution.py:103
  40.8 2.6 %reshape.167 = bf16[4,30,4,1280]{3,2,1,0:T(4,128)(2,1)} reshape(bf16[4,30,5120]{2,1,0:T(8,128)(2,1)} %fusion) | data formatting | bytes 2457600 | tf_op jit(solution)/shard_map/reshape | solution.py:107
  46.7 4.0 %collective-permute-start = (bf16[94,1,1280]{2,0,1:T(8,128)(2,1)}, bf16[94,1,1280]{2,0,1:T(8,128)(2,1)S(1)}, u32[]{:S(2)}, u32[]{:S(2)}) collective-permute-start(bf16[94,1,1280]{2,0,1:T(8,128)(2,1)} %get-tuple-element.7), channel_id=1, source_target_pairs={{0,16},{16,32},{32,48},{48,64},{64,80},{80,96},{96,112},{112,0},{1... | collective-permute-start | bytes 721928 | tf_op jit(solution)/shard_map/ppermute | solution.py:16
  50.7 3.5 %collective-permute-done = bf16[94,1,1280]{2,0,1:T(8,128)(2,1)S(1)} collective-permute-done((bf16[94,1,1280]{2,0,1:T(8,128)(2,1)}, bf16[94,1,1280]{2,0,1:T(8,128)(2,1)S(1)}, u32[]{:S(2)}, u32[]{:S(2)}) %collective-permute-start) | collective-permute-done | bytes 240672 | tf_op jit(solution)/shard_map/ppermute | solution.py:16
  54.2 2.2 collective-permute-done.1
  61.9 10.0 %collective-permute-done.3 = bf16[94,18,1]{2,0,1:T(8,128)(2,1)S(1)} collective-permute-done((bf16[94,18,1]{2,0,1:T(8,128)(2,1)S(1)}, bf16[94,18,1]{2,0,1:T(8,128)(2,1)S(1)}, u32[]{:S(2)}, u32[]{:S(2)}) %collective-permute-start.3) | collective-permute-done | bytes 3416 | tf_op jit(solution)/shard_map/ppermute | solution.py:18
  71.8 3.8 %collective-permute-done.2 = bf16[94,18,1]{2,0,1:T(8,128)(2,1)S(1)} collective-permute-done((bf16[94,18,1]{2,0,1:T(8,128)(2,1)S(1)}, bf16[94,18,1]{2,0,1:T(8,128)(2,1)S(1)}, u32[]{:S(2)}, u32[]{:S(2)}) %collective-permute-start.2) | collective-permute-done | bytes 3416 | tf_op jit(solution)/shard_map/ppermute | solution.py:16
  75.7 9.4 %concatenate.17 = bf16[94,18,1282]{2,0,1:T(8,128)(2,1)} concatenate(bf16[94,18,1]{2,0,1:T(8,128)(2,1)S(1)} %collective-permute-done.2, bf16[94,18,1280]{2,0,1:T(8,128)(2,1)} %copy-done.2, bf16[94,18,1]{2,0,1:T(8,128)(2,1)S(1)} %collective-permute-done.3), dimensions={2} | concatenate | bytes 8676576 | tf_op jit(solution)/shard_map/concatenate | solution.py:14
  85.1 2.9 %broadcast_select_fusion = bf16[94,18,1282]{2,0,1:T(8,128)(2,1)S(1)} fusion(bf16[94,18,1282]{2,0,1:T(8,128)(2,1)} %concatenate.17, pred[18]{0:T(512)(128)(4,1)S(1)} %and_or_fusion), kind=kLoop, calls=%fused_computation.12 | loop fusion | flops 2169144 | bytes 8676594 | tf_op jit(solution)/shard_map/jit(_where)/select_n | solution.py:42
  88.0 3.2 %fusion.50 = f32[16,1280,64]{1,2,0:T(8,128)} fusion(bf16[94,18,1282]{2,0,1:T(8,128)(2,1)S(1)} %broadcast_select_fusion, bf16[3,3,64,30]{2,3,1,0:T(8,128)(2,1)S(1)} %copy-done.7), kind=kOutput, calls=%fused_computation.55 | convolution fusion | flops 78643200 | bytes 6561792 | tf_op jit(solution)/shard_map/oc,crw->orw/dot_general | solution.py:30
  91.2 3.2 %fusion.52 = f32[16,1280,64]{1,2,0:T(8,128)} fusion(bf16[94,18,1282]{2,0,1:T(8,128)(2,1)S(1)} %broadcast_select_fusion, bf16[3,3,64,30]{2,3,1,0:T(8,128)(2,1)S(1)} %copy-done.7), kind=kOutput, calls=%fused_computation.57 | convolution fusion | flops 78643200 | bytes 6561792 | tf_op jit(solution)/shard_map/oc,crw->orw/dot_general | solution.py:30
  94.5 3.3 %fusion.54 = f32[16,1280,64]{1,2,0:T(8,128)} fusion(bf16[94,18,1282]{2,0,1:T(8,128)(2,1)S(1)} %broadcast_select_fusion, bf16[3,3,64,30]{2,3,1,0:T(8,128)(2,1)S(1)} %copy-done.7), kind=kOutput, calls=%fused_computation.59 | convolution fusion | flops 78643200 | bytes 6561792 | tf_op jit(solution)/shard_map/oc,crw->orw/dot_general | solution.py:30
  97.7 3.2 %fusion.56 = f32[16,1280,64]{1,2,0:T(8,128)} fusion(bf16[94,18,1282]{2,0,1:T(8,128)(2,1)S(1)} %broadcast_select_fusion, bf16[3,3,64,30]{2,3,1,0:T(8,128)(2,1)S(1)} %copy-done.7), kind=kOutput, calls=%fused_computation.61 | convolution fusion | flops 78643200 | bytes 6561792 | tf_op jit(solution)/shard_map/oc,crw->orw/dot_general | solution.py:30
  100.9 3.2 %fusion.58 = f32[16,1280,64]{1,2,0:T(8,128)} fusion(bf16[94,18,1282]{2,0,1:T(8,128)(2,1)S(1)} %broadcast_select_fusion, bf16[3,3,64,30]{2,3,1,0:T(8,128)(2,1)S(1)} %copy-done.7), kind=kOutput, calls=%fused_computation.63 | convolution fusion | flops 78643200 | bytes 6561792 | tf_op jit(solution)/shard_map/oc,crw->orw/dot_general | solution.py:30
  104.1 3.3 %fusion.60 = f32[16,1280,64]{1,2,0:T(8,128)} fusion(bf16[94,18,1282]{2,0,1:T(8,128)(2,1)S(1)} %broadcast_select_fusion, bf16[3,3,64,30]{2,3,1,0:T(8,128)(2,1)S(1)} %copy-done.7), kind=kOutput, calls=%fused_computation.65 | convolution fusion | flops 78643200 | bytes 6561792 | tf_op jit(solution)/shard_map/oc,crw->orw/dot_general | solution.py:30
  107.5 3.2 %fusion.62 = f32[16,1280,64]{1,2,0:T(8,128)} fusion(bf16[94,18,1282]{2,0,1:T(8,128)(2,1)S(1)} %broadcast_select_fusion, bf16[3,3,64,30]{2,3,1,0:T(8,128)(2,1)S(1)} %copy-done.7), kind=kOutput, calls=%fused_computation.67 | convolution fusion | flops 78643200 | bytes 6561792 | tf_op jit(solution)/shard_map/oc,crw->orw/dot_general | solution.py:30
  110.7 3.2 %fusion.64 = f32[16,1280,64]{1,2,0:T(8,128)} fusion(bf16[94,18,1282]{2,0,1:T(8,128)(2,1)S(1)} %broadcast_select_fusion, bf16[3,3,64,30]{2,3,1,0:T(8,128)(2,1)S(1)} %copy-done.7), kind=kOutput, calls=%fused_computation.69 | convolution fusion | flops 78643200 | bytes 6561792 | tf_op jit(solution)/shard_map/oc,crw->orw/dot_general | solution.py:30
  113.8 3.4 %fusion.28 = f32[16,1280,64]{1,2,0:T(8,128)} fusion(bf16[94,18,1282]{2,0,1:T(8,128)(2,1)S(1)} %broadcast_select_fusion, bf16[3,3,64,64]{3,2,1,0:T(8,128)(2,1)S(1)} %copy-done.5), kind=kOutput, calls=%fused_computation.34 | convolution fusion | flops 167772160 | bytes 7880704 | tf_op jit(solution)/shard_map/oc,crw->orw/dot_general | solution.py:30
  117.2 3.2 %fusion.30 = f32[16,1280,64]{1,2,0:T(8,128)} fusion(bf16[94,18,1282]{2,0,1:T(8,128)(2,1)S(1)} %broadcast_select_fusion, bf16[3,3,64,64]{3,2,1,0:T(8,128)(2,1)S(1)} %copy-done.5), kind=kOutput, calls=%fused_computation.36 | convolution fusion | flops 167772160 | bytes 7880704 | tf_op jit(solution)/shard_map/oc,crw->orw/dot_general | solution.py:30
  120.5 3.1 %fusion.32 = f32[16,1280,64]{1,2,0:T(8,128)} fusion(bf16[94,18,1282]{2,0,1:T(8,128)(2,1)S(1)} %broadcast_select_fusion, bf16[3,3,64,64]{3,2,1,0:T(8,128)(2,1)S(1)} %copy-done.5), kind=kOutput, calls=%fused_computation.38 | convolution fusion | flops 167772160 | bytes 7880704 | tf_op jit(solution)/shard_map/oc,crw->orw/dot_general | solution.py:30
  123.6 3.3 %fusion.34 = f32[16,1280,64]{1,2,0:T(8,128)} fusion(bf16[94,18,1282]{2,0,1:T(8,128)(2,1)S(1)} %broadcast_select_fusion, bf16[3,3,64,64]{3,2,1,0:T(8,128)(2,1)S(1)} %copy-done.5), kind=kOutput, calls=%fused_computation.40 | convolution fusion | flops 167772160 | bytes 7880704 | tf_op jit(solution)/shard_map/oc,crw->orw/dot_general | solution.py:30
  126.8 3.3 %fusion.36 = f32[16,1280,64]{1,2,0:T(8,128)} fusion(bf16[94,18,1282]{2,0,1:T(8,128)(2,1)S(1)} %broadcast_select_fusion, bf16[3,3,64,64]{3,2,1,0:T(8,128)(2,1)S(1)} %copy-done.5), kind=kOutput, calls=%fused_computation.42 | convolution fusion | flops 167772160 | bytes 7880704 | tf_op jit(solution)/shard_map/oc,crw->orw/dot_general | solution.py:30
  130.1 3.4 %fusion.38 = f32[16,1280,64]{1,2,0:T(8,128)} fusion(bf16[94,18,1282]{2,0,1:T(8,128)(2,1)S(1)} %broadcast_select_fusion, bf16[3,3,64,64]{3,2,1,0:T(8,128)(2,1)S(1)} %copy-done.5), kind=kOutput, calls=%fused_computation.44 | convolution fusion | flops 167772160 | bytes 7880704 | tf_op jit(solution)/shard_map/oc,crw->orw/dot_general | solution.py:30
  133.6 3.3 %fusion.40 = f32[16,1280,64]{1,2,0:T(8,128)} fusion(bf16[94,18,1282]{2,0,1:T(8,128)(2,1)S(1)} %broadcast_select_fusion, bf16[3,3,64,64]{3,2,1,0:T(8,128)(2,1)S(1)} %copy-done.5), kind=kOutput, calls=%fused_computation.46 | convolution fusion | flops 167772160 | bytes 7880704 | tf_op jit(solution)/shard_map/oc,crw->orw/dot_general | solution.py:30
  136.8 3.3 %fusion.42 = f32[16,1280,64]{1,2,0:T(8,128)} fusion(bf16[94,18,1282]{2,0,1:T(8,128)(2,1)S(1)} %broadcast_select_fusion, bf16[3,3,64,64]{3,2,1,0:T(8,128)(2,1)S(1)} %copy-done.5), kind=kOutput, calls=%fused_computation.48 | convolution fusion | flops 167772160 | bytes 7880704 | tf_op jit(solution)/shard_map/oc,crw->orw/dot_general | solution.py:30
  140.2 3.2 %fusion.44 = f32[16,1280,64]{1,2,0:T(8,128)} fusion(bf16[94,18,1282]{2,0,1:T(8,128)(2,1)S(1)} %broadcast_select_fusion, bf16[3,3,64,64]{3,2,1,0:T(8,128)(2,1)S(1)} %copy-done.5), kind=kOutput, calls=%fused_computation.50 | convolution fusion | flops 167772160 | bytes 7880704 | tf_op jit(solution)/shard_map/oc,crw->orw/dot_general | solution.py:30
  143.4 28.8 %fusion.7 = bf16[64,16,1280]{2,0,1:T(8,128)(2,1)S(1)} fusion(f32[16,1280,64]{1,2,0:T(8,128)} %fusion.50, f32[16,1280,64]{1,2,0:T(8,128)} %fusion.52, f32[16,1280,64]{1,2,0:T(8,128)} %fusion.54, f32[16,1280,64]{1,2,0:T(8,128)} %fusion.56, f32[16,1280,64]{1,2,0:T(8,128)} %fusion.58, f32[16,1280,64]{1,2,0:T(8,128)} %fusion.60, f32[16,1280,64]{1,2,0:T(8,128)} %fusion.64, ...), kind=kOutput, calls=%fused_computation.11 | convolution fusion | flops 108789760 | bytes 93069824 | tf_op jit(solution)/shard_map/oc,crw->orw/dot_general | solution.py:30
  172.2 2.3 collective-permute-start.4
  174.5 2.3 collective-permute-done.4
  176.8 2.5 collective-permute-done.5
  183.1 6.8 %collective-permute-done.7 = bf16[64,18,1]{2,0,1:T(8,128)(2,1)S(1)} collective-permute-done((bf16[64,18,1]{2,0,1:T(8,128)(2,1)S(1)}, bf16[64,18,1]{2,0,1:T(8,128)(2,1)S(1)}, u32[]{:S(2)}, u32[]{:S(2)}) %collective-permute-start.7) | collective-permute-done | bytes 2336 | tf_op jit(solution)/shard_map/ppermute | solution.py:18
  189.9 3.2 %collective-permute-done.6 = bf16[64,18,1]{2,0,1:T(8,128)(2,1)} collective-permute-done((bf16[64,18,1]{2,0,1:T(8,128)(2,1)S(1)}, bf16[64,18,1]{2,0,1:T(8,128)(2,1)}, u32[]{:S(2)}, u32[]{:S(2)}) %collective-permute-start.6) | collective-permute-done | bytes 2336 | tf_op jit(solution)/shard_map/ppermute | solution.py:16
  193.1 5.8 %concatenate.19 = bf16[64,18,1282]{2,0,1:T(8,128)(2,1)} concatenate(bf16[64,18,1]{2,0,1:T(8,128)(2,1)} %collective-permute-done.6, bf16[64,18,1280]{2,0,1:T(8,128)(2,1)S(1)} %pad_maximum_fusion.1, bf16[64,18,1]{2,0,1:T(8,128)(2,1)S(1)} %collective-permute-done.7), dimensions={2} | concatenate | bytes 5907456 | tf_op jit(solution)/shard_map/concatenate | solution.py:14
  198.9 2.3 broadcast_select_fusion.1
  201.2 3.3 %fusion.12 = f32[16,1280,64]{1,2,0:T(8,128)} fusion(bf16[64,18,1282]{2,0,1:T(8,128)(2,1)S(1)} %broadcast_select_fusion.1, bf16[3,3,64,64]{3,2,1,0:T(8,128)(2,1)S(1)} %copy-done.6), kind=kOutput, calls=%fused_computation.18 | convolution fusion | flops 167772160 | bytes 7880704 | tf_op jit(solution)/shard_map/oc,crw->orw/dot_general | solution.py:30
  204.4 3.2 %fusion.14 = f32[16,1280,64]{1,2,0:T(8,128)} fusion(bf16[64,18,1282]{2,0,1:T(8,128)(2,1)S(1)} %broadcast_select_fusion.1, bf16[3,3,64,64]{3,2,1,0:T(8,128)(2,1)S(1)} %copy-done.6), kind=kOutput, calls=%fused_computation.20 | convolution fusion | flops 167772160 | bytes 7880704 | tf_op jit(solution)/shard_map/oc,crw->orw/dot_general | solution.py:30
  207.6 3.3 %fusion.16 = f32[16,1280,64]{1,2,0:T(8,128)} fusion(bf16[64,18,1282]{2,0,1:T(8,128)(2,1)S(1)} %broadcast_select_fusion.1, bf16[3,3,64,64]{3,2,1,0:T(8,128)(2,1)S(1)} %copy-done.6), kind=kOutput, calls=%fused_computation.22 | convolution fusion | flops 167772160 | bytes 7880704 | tf_op jit(solution)/shard_map/oc,crw->orw/dot_general | solution.py:30
  210.9 3.2 %fusion.18 = f32[16,1280,64]{1,2,0:T(8,128)} fusion(bf16[64,18,1282]{2,0,1:T(8,128)(2,1)S(1)} %broadcast_select_fusion.1, bf16[3,3,64,64]{3,2,1,0:T(8,128)(2,1)S(1)} %copy-done.6), kind=kOutput, calls=%fused_computation.24 | convolution fusion | flops 167772160 | bytes 7880704 | tf_op jit(solution)/shard_map/oc,crw->orw/dot_general | solution.py:30
  214.2 3.2 %fusion.20 = f32[16,1280,64]{1,2,0:T(8,128)} fusion(bf16[64,18,1282]{2,0,1:T(8,128)(2,1)S(1)} %broadcast_select_fusion.1, bf16[3,3,64,64]{3,2,1,0:T(8,128)(2,1)S(1)} %copy-done.6), kind=kOutput, calls=%fused_computation.26 | convolution fusion | flops 167772160 | bytes 7880704 | tf_op jit(solution)/shard_map/oc,crw->orw/dot_general | solution.py:30
  217.3 3.4 %fusion.22 = f32[16,1280,64]{1,2,0:T(8,128)} fusion(bf16[64,18,1282]{2,0,1:T(8,128)(2,1)S(1)} %broadcast_select_fusion.1, bf16[3,3,64,64]{3,2,1,0:T(8,128)(2,1)S(1)} %copy-done.6), kind=kOutput, calls=%fused_computation.28 | convolution fusion | flops 167772160 | bytes 7880704 | tf_op jit(solution)/shard_map/oc,crw->orw/dot_general | solution.py:30
  220.7 3.3 %fusion.24 = f32[16,1280,64]{1,2,0:T(8,128)} fusion(bf16[64,18,1282]{2,0,1:T(8,128)(2,1)S(1)} %broadcast_select_fusion.1, bf16[3,3,64,64]{3,2,1,0:T(8,128)(2,1)S(1)} %copy-done.6), kind=kOutput, calls=%fused_computation.30 | convolution fusion | flops 167772160 | bytes 7880704 | tf_op jit(solution)/shard_map/oc,crw->orw/dot_general | solution.py:30
  223.9 3.1 %fusion.26 = f32[16,1280,64]{1,2,0:T(8,128)} fusion(bf16[64,18,1282]{2,0,1:T(8,128)(2,1)S(1)} %broadcast_select_fusion.1, bf16[3,3,64,64]{3,2,1,0:T(8,128)(2,1)S(1)} %copy-done.6), kind=kOutput, calls=%fused_computation.32 | convolution fusion | flops 167772160 | bytes 7880704 | tf_op jit(solution)/shard_map/oc,crw->orw/dot_general | solution.py:30
  227.0 17.1 %fusion.2 = bf16[64,16,1280]{2,0,1:T(8,128)(2,1)} fusion(f32[16,1280,64]{1,2,0:T(8,128)} %fusion.12, f32[16,1280,64]{1,2,0:T(8,128)} %fusion.14, f32[16,1280,64]{1,2,0:T(8,128)} %fusion.16, f32[16,1280,64]{1,2,0:T(8,128)} %fusion.18, f32[16,1280,64]{1,2,0:T(8,128)} %fusion.20, f32[16,1280,64]{1,2,0:T(8,128)} %fusion.22, f32[16,1280,64]{1,2,0:T(8,128)} %fusion.26, ...), kind=kOutput, calls=%fused_computation.4 | convolution fusion | flops 183500800 | bytes 49824256 | tf_op jit(solution)/shard_map/oc,crw->orw/dot_general | solution.py:30
  244.2 4.7 %copy.45 = bf16[64,16,1280]{2,1,0:T(8,128)(2,1)} copy(bf16[64,16,1280]{2,0,1:T(8,128)(2,1)} %fusion.2) | data formatting | bytes 5242880 | tf_op jit(solution)/shard_map/convert_element_type | solution.py:123
  (53 shorter events, 18.2 us)
Async XLA Ops:
  0.0 17.7 %copy-start = (bf16[1,4,30,128]{3,1,2,0:T(4,128)(2,1)S(1)}, bf16[1,4,30,128]{3,1,2,0:T(4,128)(2,1)}, u32[]{:S(2)}) copy-start(bf16[1,4,30,128]{3,1,2,0:T(4,128)(2,1)} %param.13) | copy-start | bytes 92164
  18.2 18.0 %copy-start.10 = (s32[1,1,4,4]{3,2,1,0:T(4,128)S(1)}, s32[1,1,4,4]{3,2,1,0:T(4,128)}, u32[]{:S(2)}) copy-start(s32[1,1,4,4]{3,2,1,0:T(4,128)} %param.16) | copy-start | bytes 196
  19.4 16.0 %all-to-all-start.1 = ((bf16[16,6,30,128]{3,2,1,0:T(8,128)(2,1)}), bf16[16,6,30,128]{3,2,1,0:T(8,128)(2,1)S(1)}, u32[]{:S(2)}, u32[]{:S(2)}) async-start(bf16[16,6,30,128]{3,2,1,0:T(8,128)(2,1)} %copy.38), calls=%async_computation.1 | async-start | bytes 1572864 | tf_op jit(solution)/shard_map/all_to_all | solution.py:89
  44.9 1.1 copy-start.4
  46.7 7.5 %collective-permute-start = (bf16[94,1,1280]{2,0,1:T(8,128)(2,1)}, bf16[94,1,1280]{2,0,1:T(8,128)(2,1)S(1)}, u32[]{:S(2)}, u32[]{:S(2)}) collective-permute-start(bf16[94,1,1280]{2,0,1:T(8,128)(2,1)} %get-tuple-element.7), channel_id=1, source_target_pairs={{0,16},{16,32},{32,48},{48,64},{64,80},{80,96},{96,112},{112,0},{1... | collective-permute-start | bytes 721928 | tf_op jit(solution)/shard_map/ppermute | solution.py:16
  50.7 5.6 %collective-permute-start.1 = (bf16[94,1,1280]{2,0,1:T(8,128)(2,1)S(1)}, bf16[94,1,1280]{2,0,1:T(8,128)(2,1)S(1)}, u32[]{:S(2)}, u32[]{:S(2)}) collective-permute-start(bf16[94,1,1280]{2,0,1:T(8,128)(2,1)S(1)} %get-tuple-element.8), channel_id=1, source_target_pairs={{16,0},{32,16},{48,32},{64,48},{80,64},{96,80},{112,96},{0,112},{1... | collective-permute-start | bytes 721928 | tf_op jit(solution)/shard_map/ppermute | solution.py:18
  58.0 2.1 copy-start.2
  60.3 11.5 %collective-permute-start.3 = (bf16[94,18,1]{2,0,1:T(8,128)(2,1)S(1)}, bf16[94,18,1]{2,0,1:T(8,128)(2,1)S(1)}, u32[]{:S(2)}, u32[]{:S(2)}) collective-permute-start(bf16[94,18,1]{2,0,1:T(8,128)(2,1)S(1)} %get-tuple-element.5), channel_id=1, source_target_pairs={{1,0},{2,1},{3,2},{4,3},{5,4},{6,5},{7,6},{8,7},{9,8},{10,9},{11,1... | collective-permute-start | bytes 10160 | tf_op jit(solution)/shard_map/ppermute | solution.py:18
  61.2 14.4 %collective-permute-start.2 = (bf16[94,18,1]{2,0,1:T(8,128)(2,1)S(1)}, bf16[94,18,1]{2,0,1:T(8,128)(2,1)S(1)}, u32[]{:S(2)}, u32[]{:S(2)}) collective-permute-start(bf16[94,18,1]{2,0,1:T(8,128)(2,1)S(1)} %get-tuple-element.6), channel_id=1, source_target_pairs={{0,1},{1,2},{2,3},{3,4},{4,5},{5,6},{6,7},{7,8},{8,9},{9,10},{10,1... | collective-permute-start | bytes 10160 | tf_op jit(solution)/shard_map/ppermute | solution.py:16
  85.1 2.9 %copy-start.7 = (bf16[3,3,64,30]{2,3,1,0:T(8,128)(2,1)S(1)}, bf16[3,3,64,30]{2,3,1,0:T(8,128)(2,1)}, u32[]{:S(2)}) copy-start(bf16[3,3,64,30]{2,3,1,0:T(8,128)(2,1)} %param.20) | copy-start | bytes 103684
  110.7 3.2 %copy-start.5 = (bf16[3,3,64,64]{3,2,1,0:T(8,128)(2,1)S(1)}, bf16[3,3,64,64]{3,2,1,0:T(8,128)(2,1)}, u32[]{:S(2)}) copy-start(bf16[3,3,64,64]{3,2,1,0:T(8,128)(2,1)} %param.19) | copy-start | bytes 221188
  140.2 3.2 %copy-start.9 = (f32[64]{0:T(128)S(1)}, f32[64]{0:T(128)}, u32[]{:S(2)}) copy-start(f32[64]{0:T(128)} %param.21) | copy-start | bytes 772
  172.2 4.6 %copy-start.3 = (bf16[64,16,1280]{2,0,1:T(8,128)(2,1)}, bf16[64,16,1280]{2,0,1:T(8,128)(2,1)S(1)}, u32[]{:S(2)}) copy-start(bf16[64,16,1280]{2,0,1:T(8,128)(2,1)S(1)} %fusion.7) | copy-start | bytes 7864324
  172.2 4.6 %collective-permute-start.4 = (bf16[64,1,1280]{2,0,1:T(8,128)(2,1)S(1)}, bf16[64,1,1280]{2,0,1:T(8,128)(2,1)S(1)}, u32[]{:S(2)}, u32[]{:S(2)}) collective-permute-start(bf16[64,1,1280]{2,0,1:T(8,128)(2,1)S(1)} %get-tuple-element.11), channel_id=1, source_target_pairs={{0,16},{16,32},{32,48},{48,64},{64,80},{80,96},{96,112},{112,0},{1... | collective-permute-start | bytes 491528 | tf_op jit(solution)/shard_map/ppermute | solution.py:16
  174.5 4.7 %collective-permute-start.5 = (bf16[64,1,1280]{2,0,1:T(8,128)(2,1)S(1)}, bf16[64,1,1280]{2,0,1:T(8,128)(2,1)S(1)}, u32[]{:S(2)}, u32[]{:S(2)}) collective-permute-start(bf16[64,1,1280]{2,0,1:T(8,128)(2,1)S(1)} %get-tuple-element.12), channel_id=1, source_target_pairs={{16,0},{32,16},{48,32},{64,48},{80,64},{96,80},{112,96},{0,112},{1... | collective-permute-start | bytes 491528 | tf_op jit(solution)/shard_map/ppermute | solution.py:18
  181.5 8.4 %collective-permute-start.7 = (bf16[64,18,1]{2,0,1:T(8,128)(2,1)S(1)}, bf16[64,18,1]{2,0,1:T(8,128)(2,1)S(1)}, u32[]{:S(2)}, u32[]{:S(2)}) collective-permute-start(bf16[64,18,1]{2,0,1:T(8,128)(2,1)S(1)} %get-tuple-element.9), channel_id=1, source_target_pairs={{1,0},{2,1},{3,2},{4,3},{5,4},{6,5},{7,6},{8,7},{9,8},{10,9},{11,1... | collective-permute-start | bytes 6920 | tf_op jit(solution)/shard_map/ppermute | solution.py:18
  181.6 11.5 %collective-permute-start.6 = (bf16[64,18,1]{2,0,1:T(8,128)(2,1)S(1)}, bf16[64,18,1]{2,0,1:T(8,128)(2,1)}, u32[]{:S(2)}, u32[]{:S(2)}) collective-permute-start(bf16[64,18,1]{2,0,1:T(8,128)(2,1)S(1)} %get-tuple-element.10), channel_id=1, source_target_pairs={{0,1},{1,2},{2,3},{3,4},{4,5},{5,6},{6,7},{7,8},{8,9},{9,10},{10,1... | collective-permute-start | bytes 6920 | tf_op jit(solution)/shard_map/ppermute | solution.py:16
  198.9 2.3 copy-start.6
  223.9 3.1 %copy-start.8 = (f32[64]{0:T(128)S(1)}, f32[64]{0:T(128)}, u32[]{:S(2)}) copy-start(f32[64]{0:T(128)} %param.23) | copy-start | bytes 772
  227.0 21.8 %copy-start.1 = (bf16[1,4,30,128]{3,1,2,0:T(4,128)(2,1)S(1)}, bf16[1,4,30,128]{3,1,2,0:T(4,128)(2,1)}, u32[]{:S(2)}) copy-start(bf16[1,4,30,128]{3,1,2,0:T(4,128)(2,1)} %param.13) | copy-start | bytes 92164
where the time goes:
time: 250 us; the launch traced here: 249 us
  matrix products  133 us (53%)
  waiting for transfers between devices  44 us (18%)
  local copies, waits for them, and re-layouts  32.3 us (13%)
  blocking collectives  14.8 us (6%)
  starting transfers between devices  13 us (5%)
  other arithmetic  11.5 us (5%)
    dot_general x27, matrix products, conv_sum(): jnp.einsum('oc,crw->orw', kernel[shift_r, shift_c], window, preferred_ele...  127 us
    ppermute x4, waiting for transfers between devices, padded_2(): lax.ppermute(head, axis, [((i + 1) % count, i) for i in range(count)])  21.4 us
    concatenate x2, local copies, waits for them, and re-layouts, padded_2(): jnp.concatenate([lax.ppermute(tail, axis, [(i, (i + 1) % count) for i in...  15.2 us
    all_to_all x1, blocking collectives, local(): lax.all_to_all(wanted, 'lon', split_axis=0, concat_axis=0, tiled=True)  14.8 us
    ppermute x4, waiting for transfers between devices, padded_2(): lax.ppermute(tail, axis, [(i, (i + 1) % count) for i in range(count)])  12.7 us
    all_to_all x1, waiting for transfers between devices, local(): lax.all_to_all(found, 'lon', split_axis=0, concat_axis=0, tiled=True)  9.85 us
    ppermute x4, starting transfers between devices, padded_2(): lax.ppermute(tail, axis, [(i, (i + 1) % count) for i in range(count)])  8.39 us
    unnamed x23, local copies, waits for them, and re-layouts  5.68 us
  transfers between devices with their start and end apart: 9, of which 9 were waited for; matrix products, arithmetic and copies ran while one was open for 1% of the time, Pallas kernels for 0%

commit v1 on v0

v1 whole, which is shorter than its diff:
```python
import jax
import jax.numpy as jnp
from jax import lax
from jax.experimental import pallas as pl
from jax.experimental.pallas import tpu as pltpu
from jax.sharding import PartitionSpec as P

BF = jnp.bfloat16
F32 = jnp.float32
MIB = 1024 * 1024

C = 64
CP = 32
R = 16
W = 1280
LT = 128
WX = W + LT
PEERS = 16
HELD = 4
SUBS = 4
SLOTS = 4
KINDS = 4
MSG = HELD * CP + C


def vmem(n=1):
    return [pl.BlockSpec(memory_space=pltpu.VMEM)] * n


def smem(n=1):
    return [pl.BlockSpec(memory_space=pltpu.SMEM)] * n


def params(mib):
    return pltpu.CompilerParams(vmem_limit_bytes=mib * MIB)


def struct(shape, dtype=BF):
    return jax.ShapeDtypeStruct(shape, dtype)


def iota(shape, dim):
    return lax.broadcasted_iota(jnp.int32, shape, dim)


def message_kernel(first, last, coarse, owner, slot, weight, counts, out):
    lane = iota((C, R, LT), 2)
    edge = jnp.where(lane < 64, first[...].astype(F32), last[...].astype(F32))
    edge = jnp.swapaxes(edge.astype(BF), 0, 1)
    edge = jnp.concatenate([edge[r] for r in range(R)], axis=1)
    row = iota((R * LT, LT), 0)
    col = iota((R * LT, LT), 1)
    at = row % LT
    kind = jnp.where(at < 64, at, at - 124)
    wanted = ((at < 2) | (at >= 126)) & (col == kind * R + row // LT)
    pick = jnp.where(wanted, 1.0, 0.0).astype(BF)
    packed = jnp.dot(edge, pick, preferred_element_type=F32)
    lanes = iota((C, LT), 1)
    for s in range(SUBS):
        live = counts[0, 0, s]
        for k in range(SLOTS):
            n = s * SLOTS + k
            block = owner[0, 0, s, k] * HELD + slot[0, 0, s, k]
            kind_id = jnp.where(k < live, weight[0, 0, s, k], KINDS)
            packed = jnp.where(lanes == 64 + n, block.astype(F32), packed)
            packed = jnp.where(lanes == 80 + n, kind_id.astype(F32), packed)
    packed = packed.astype(BF)
    zeros = jnp.zeros((CP - coarse.shape[2], LT), F32)
    blocks = [jnp.concatenate([coarse[0, b].astype(F32), zeros], axis=0).astype(BF) for b in range(HELD)]
    whole = jnp.concatenate(blocks + [packed], axis=0)
    for p in range(PEERS):
        out[p] = whole


def message(noisy, coarse, owner, slot, weight, counts):
    return pl.pallas_call(
        message_kernel,
        grid=(1,),
        out_shape=struct((PEERS, MSG, LT)),
        in_specs=[
            pl.BlockSpec((C, R, LT), lambda i: (0, 0, 0)),
            pl.BlockSpec((C, R, LT), lambda i: (0, 0, W // LT - 1)),
            pl.BlockSpec(coarse.shape, lambda i: (0, 0, 0, 0)),
        ]
        + smem(4),
        out_specs=pl.BlockSpec((PEERS, MSG, LT), lambda i: (0, 0, 0)),
        compiler_params=params(12),
    )(noisy, noisy, coarse, owner, slot, weight, counts)


def shifted(x, width):
    return [pltpu.roll(x, 1, 1), x, pltpu.roll(x, width - 1, 1)]


def pair_weights(kernel, pad):
    out_ch = kernel.shape[2]
    def block(dr, dc):
        w = kernel[dr, dc]
        if pad:
            w = jnp.concatenate([w.astype(F32), jnp.zeros((out_ch, pad), F32)], axis=1).astype(BF)
        return w
    rows = jnp.concatenate([block(dr, dc) for dr in range(3) for dc in range(3)], axis=1)
    blank = jnp.zeros((out_ch, rows.shape[1] // 3), BF)
    return jnp.concatenate(
        [jnp.concatenate([rows, blank], axis=1), jnp.concatenate([blank, rows], axis=1)], axis=0
    )


def own_kernel(noisy, conv_in, conv_cond, conv_out, xs, hid, w_in, w_cond, w_out, x3):
    w_in[...] = pair_weights(conv_in, 0)
    w_out[...] = pair_weights(conv_out, 0)
    w_cond[...] = pair_weights(conv_cond, CP - conv_cond.shape[3])
    xs[...] = jnp.swapaxes(noisy[...], 0, 1).reshape(R * C, W)
    blank = jnp.zeros((C, LT), BF)
    for r in range(R):
        x = jnp.concatenate([xs[pl.ds(r * C, C), :], blank], axis=1)
        for d, y in enumerate(shifted(x, WX)):
            x3[pl.ds((r * 3 + d) * C, C), :] = y
    for i in range(R // 2 - 1):
        hid[pl.ds(i * 2 * C, 2 * C), :] = jnp.dot(
            w_in[...], x3[pl.ds(i * 6 * C, 12 * C), :], preferred_element_type=F32
        )


def own_tile(noisy, conv_in, conv_cond, conv_out):
    return pl.pallas_call(
        own_kernel,
        out_shape=(
            struct((R * C, W)),
            struct(((R - 2) * C, WX), F32),
            struct((2 * C, 12 * C)),
            struct((2 * C, 12 * CP)),
            struct((2 * C, 12 * C)),
        ),
        in_specs=vmem(4),
        out_specs=tuple(vmem(5)),
        scratch_shapes=[pltpu.VMEM((R * 3 * C, WX), BF)],
        compiler_params=params(28),
        cost_estimate=pl.CostEstimate(flops=3 * 10**9, bytes_accessed=12 * 10**6, transcendentals=0),
    )(noisy, conv_in, conv_cond, conv_out)


def cond_kernel(got, owner, slot, weight, counts, table, xs, cond, halo, top, bottom, acc, grp, ints, lists, sem):
    me = lax.axis_index("lon")
    left = lax.rem(me + PEERS - 1, PEERS)
    right = lax.rem(me + 1, PEERS)
    edge_l = got[left, pl.ds(HELD * CP, C), :]
    edge_r = got[right, pl.ds(HELD * CP, C), :]
    ints[0] = edge_l[0:8].astype(F32).astype(jnp.int32)
    ints[1] = edge_r[0:8].astype(F32).astype(jnp.int32)
    copy = pltpu.make_async_copy(ints, lists, sem)
    copy.start()
    acc[...] = jnp.zeros_like(acc)

    def add(d, s, block, kind):
        part = got[block // HELD, pl.ds(pl.multiple_of(lax.rem(block, HELD) * CP, CP), CP), :]
        at = (d * SUBS + s) * (KINDS + 1) + kind
        acc[at] = acc[at] + part.astype(F32)

    for s in range(SUBS):
        for k in range(SLOTS):
            kind = jnp.where(k < counts[0, 0, s], weight[0, 0, s, k], KINDS)
            add(0, s, owner[0, 0, s, k] * HELD + slot[0, 0, s, k], kind)

    lane = iota((C, LT), 1)
    both = jnp.where(lane < 32, edge_r.astype(F32), jnp.where(lane < 64, edge_l.astype(F32), 0.0)).astype(BF)
    src = iota((LT, R * LT), 0)
    dst = iota((LT, R * LT), 1)
    at = dst % LT
    kind = jnp.where(at < 64, at, at - 124)
    wanted = ((at < 2) | (at >= 126)) & (src == kind * R + dst // LT)
    place = jnp.where(wanted, 1.0, 0.0).astype(BF)
    tiles = jnp.dot(both, place, preferred_element_type=F32).astype(BF)
    for r in range(R):
        halo[pl.ds(r * C, C), :] = tiles[:, r * LT : (r + 1) * LT]

    copy.wait()
    for d in range(2):
        for s in range(SUBS):
            for k in range(SLOTS):
                n = s * SLOTS + k
                add(d + 1, s, lists[d, 0, 64 + n], lists[d, 0, 80 + n])
    for d in range(3):
        for s in range(SUBS):
            for w in range(KINDS):
                grp[d, pl.ds(s * CP, CP), w * LT : (w + 1) * LT] = acc[(d * SUBS + s) * (KINDS + 1) + w].astype(BF)

    lane = iota((SUBS * CP, LT), 1)
    for r in range(R // SUBS):
        own = jnp.dot(grp[0], table[:, r * W : (r + 1) * W], preferred_element_type=F32).astype(BF)
        lhs = jnp.dot(grp[1], table[:, (r + 1) * W - LT : (r + 1) * W], preferred_element_type=F32)
        rhs = jnp.dot(grp[2], table[:, r * W : r * W + LT], preferred_element_type=F32)
        side = jnp.where(lane < 2, rhs, jnp.where(lane >= 126, lhs, 0.0)).astype(BF)
        for s in range(SUBS):
            at = pl.ds((s * SUBS + r) * CP, CP)
            cond[at, 0:W] = own[s * CP : (s + 1) * CP]
            cond[at, W:WX] = side[s * CP : (s + 1) * CP]
    for out, r0 in ((top, 0), (bottom, R - 2)):
        out[0 : 2 * C, 0:W] = xs[pl.ds(r0 * C, 2 * C), :]
        out[0 : 2 * C, W:WX] = halo[pl.ds(r0 * C, 2 * C), :]
        out[2 * C : 2 * C + 2 * CP, :] = cond[pl.ds(r0 * CP, 2 * CP), :]


def cond_tile(got, owner, slot, weight, counts, table, xs):
    edge = struct((2 * (C + CP), WX))
    return pl.pallas_call(
        cond_kernel,
        out_shape=(struct((R * CP, WX)), struct((R * C, LT)), edge, edge),
        in_specs=vmem(1) + smem(4) + vmem(2),
        out_specs=tuple(vmem(4)),
        scratch_shapes=[
            pltpu.VMEM((3 * SUBS * (KINDS + 1), CP, LT), F32),
            pltpu.VMEM((3, SUBS * CP, KINDS * LT), BF),
            pltpu.VMEM((2, 8, LT), jnp.int32),
            pltpu.SMEM((2, 8, LT), jnp.int32),
            pltpu.SemaphoreType.DMA,
        ],
        compiler_params=params(20),
    )(got, owner, slot, weight, counts, table, xs)


def silu(v):
    return v / (1.0 + jnp.exp(-v))


def inner_kernel(hid, cond, halo, w_in, w_cond, bias, act, c3, h3):
    for r in range(R):
        for d, y in enumerate(shifted(cond[pl.ds(r * CP, CP), :], WX)):
            c3[pl.ds((r * 3 + d) * CP, CP), :] = y
        blank = jnp.zeros((C, LT), BF)
        h = jnp.concatenate([blank, halo[pl.ds(r * C, C), :], blank], axis=1)
        for d, y in enumerate(shifted(h, 3 * LT)):
            h3[pl.ds((r * 3 + d) * C, C), :] = y
    for i in range(R // 2 - 1):
        at = pl.ds(i * 2 * C, 2 * C)
        v = jnp.dot(w_cond[...], c3[pl.ds(i * 6 * CP, 12 * CP), :], preferred_element_type=F32)
        v = v + hid[at, :] + bias[...]
        e = jnp.dot(w_in[...], h3[pl.ds(i * 6 * C, 12 * C), :], preferred_element_type=F32)
        act[at, LT : W - LT] = silu(v[:, LT : W - LT]).astype(BF)
        act[at, W - LT : WX] = silu(v[:, W - LT : WX] + e[:, 0 : 2 * LT]).astype(BF)
        act[at, 0:LT] = silu(v[:, 0:LT] + e[:, 2 * LT : 3 * LT]).astype(BF)


def inner_rows(hid, cond, halo, w_in, w_cond, bias):
    return pl.pallas_call(
        inner_kernel,
        out_shape=struct(((R - 2) * C, WX)),
        in_specs=vmem(6),
        out_specs=vmem()[0],
        scratch_shapes=[
            pltpu.VMEM((R * 3 * CP, WX), BF),
            pltpu.VMEM((R * 3 * C, 3 * LT), BF),
        ],
        compiler_params=params(24),
        cost_estimate=pl.CostEstimate(flops=2 * 10**9, bytes_accessed=10 * 10**6, transcendentals=10**6),
    )(hid, cond, halo, w_in, w_cond, bias)


def outer_kernel(act, top, bottom, above, below, xs, w_in, w_cond, w_out, bias, bias_out, out, n3, c3, a3, z):
    lat = lax.axis_index("lat")
    first = jnp.where(lat == 0, 0.0, 1.0)
    last = jnp.where(lat == 7, 0.0, 1.0)

    def put(row, x):
        for d, y in enumerate(shifted(x, WX)):
            a3[pl.ds((row * 3 + d) * C, C), :] = y[:, 0:W]

    for r in range(R - 2):
        put(r + 2, act[pl.ds(r * C, C), :])
    for part, (lo, hi) in enumerate(((above, top), (bottom, below))):
        for r, ref in enumerate((lo, lo, hi, hi)):
            for d, y in enumerate(shifted(ref[pl.ds(r % 2 * C, C), :], WX)):
                n3[pl.ds((r * 3 + d) * C, C), :] = y
            for d, y in enumerate(shifted(ref[pl.ds(2 * C + r % 2 * CP, CP), :], WX)):
                c3[pl.ds((r * 3 + d) * CP, CP), :] = y
        v = jnp.dot(w_in[...], n3[...], preferred_element_type=F32)
        v = v + jnp.dot(w_cond[...], c3[...], preferred_element_type=F32) + bias[...]
        v = silu(v)
        if part == 0:
            put(0, (v[0:C] * first).astype(BF))
            put(1, v[C:].astype(BF))
        else:
            put(R, v[0:C].astype(BF))
            put(R + 1, (v[C:] * last).astype(BF))
    for i in range(R // 2):
        at = pl.ds(i * 2 * C, 2 * C)
        y = jnp.dot(w_out[...], a3[pl.ds(i * 6 * C, 12 * C), :], preferred_element_type=F32)
        z[at, :] = (y + xs[at, :].astype(F32) + bias_out[...]).astype(BF)
    out[...] = jnp.swapaxes(z[...].reshape(R, C, W), 0, 1)


def outer_rows(act, top, bottom, above, below, xs, w_in, w_cond, w_out, bias, bias_out):
    return pl.pallas_call(
        outer_kernel,
        out_shape=struct((C, R, W)),
        in_specs=vmem(11),
        out_specs=vmem()[0],
        scratch_shapes=[
            pltpu.VMEM((12 * C, WX), BF),
            pltpu.VMEM((12 * CP, WX), BF),
            pltpu.VMEM(((R + 2) * 3 * C, W), BF),
            pltpu.VMEM((R * C, W), BF),
        ],
        compiler_params=params(32),
    )(act, top, bottom, above, below, xs, w_in, w_cond, w_out, bias, bias_out)


def local(noisy, coarse, owner, slot, weight, counts, table, conv_in, conv_cond, bias_in, conv_out, bias_out):
    msg = message(noisy, coarse, owner, slot, weight, counts)
    got = lax.all_to_all(msg, "lon", split_axis=0, concat_axis=0, tiled=True)
    xs, hid, w_in, w_cond, w_out = own_tile(noisy, conv_in, conv_cond, conv_out)
    table = table.reshape(KINDS * LT, table.shape[2])
    cond, halo, top, bottom = cond_tile(got, owner, slot, weight, counts, table, xs)
    count = lax.axis_size("lat")
    above = lax.ppermute(bottom, "lat", [(i, i + 1) for i in range(count - 1)])
    below = lax.ppermute(top, "lat", [(i + 1, i) for i in range(count - 1)])
    bias = jnp.concatenate([bias_in, bias_in])[:, None]
    bias_2 = jnp.concatenate([bias_out, bias_out])[:, None]
    act = inner_rows(hid, cond, halo, w_in, w_cond, bias)
    return outer_rows(act, top, bottom, above, below, xs, w_in, w_cond, w_out, bias, bias_2)


def solution(mesh):
    grid = P("lat", "lon")
    in_specs = (P(None, "lat", "lon"),) + (grid,) * 5 + (P(),) * 6
    return jax.shard_map(local, mesh=mesh, in_specs=in_specs, out_specs=P(None, "lat", "lon"), check_vma=False)
```

time: 250 us -> 62.2 us (0.25)
  matrix products: 133 us -> 0 us
  waiting for transfers between devices: 44 us -> 1.23 us
  Pallas kernels: 0 us -> 19.7 us
  blocking collectives: 14.8 us -> 0 us
  other arithmetic: 11.5 us -> 0.15 us
  local copies, waits for them, and re-layouts: 32.3 us -> 24.3 us
  starting transfers between devices: 13 us -> 16 us
    dot_general x31 -> x0, matrix products: 133 us -> none  [the longest x27 127 us: conv_sum(): jnp.einsum('oc,crw->orw', kernel[shift_r, shift_c], window, preferred_ele...]
    ppermute x8 -> x2, waiting for transfers between devices: 34.2 us -> 0.01 us  [the longest x1 0.01 us: local(): above = lax.ppermute(bottom, 'lat', [(i, i + 1) for i in range(count - 1)])]
    pallas_call x0 -> x5, Pallas kernels: none -> 19.7 us  [the longest x1 7.75 us: outer_rows(): pl.pallas_call(outer_kernel, out_shape=struct((C, R, W)), in_specs=vmem(1...]
    unnamed x23 -> x58, local copies, waits for them, and re-layouts: 5.68 us -> 24.1 us
    concatenate x2 -> x0, local copies, waits for them, and re-layouts: 15.2 us -> none  [padded_2(): jnp.concatenate([lax.ppermute(tail, axis, [(i, (i + 1) % count) for i in...]
    all_to_all x1 -> x0, blocking collectives: 14.8 us -> none  [local(): lax.all_to_all(wanted, 'lon', split_axis=0, concat_axis=0, tiled=True)]
    all_to_all x1, waiting for transfers between devices: 9.85 us -> 1.22 us  [local(): got = lax.all_to_all(msg, 'lon', split_axis=0, concat_axis=0, tiled=True)]
    convert_element_type x2 -> x0, local copies, waits for them, and re-layouts: 5.84 us -> none  [the longest x1 4.67 us: local(): return result.astype(jnp.bfloat16)]
  transfers between devices with their start and end apart: 9 -> 3, of which waited for: 9 -> 1; matrix products, arithmetic and copies ran while one was open for 1% -> 2% of each run, Pallas kernels for 0% -> 10%
where the time goes in v1:
time: 62.2 us; the launch traced here: 61.5 us
  local copies, waits for them, and re-layouts  24.3 us (39%)
  Pallas kernels  19.7 us (32%)
  starting transfers between devices  16 us (26%)
  waiting for transfers between devices  1.23 us (2%)
    unnamed x58, local copies, waits for them, and re-layouts  24.1 us
    all_to_all x1, starting transfers between devices, local(): got = lax.all_to_all(msg, 'lon', split_axis=0, concat_axis=0, tiled=True)  8.6 us
    pallas_call x1, Pallas kernels, outer_rows(): pl.pallas_call(outer_kernel, out_shape=struct((C, R, W)), in_specs=vmem(1...  7.75 us
    ppermute x1, starting transfers between devices, local(): above = lax.ppermute(bottom, 'lat', [(i, i + 1) for i in range(count - 1)])  5.27 us
    pallas_call x1, Pallas kernels, cond_tile(): pl.pallas_call(cond_kernel, out_shape=(struct((R * CP, WX)), struct((R *...  3.94 us
    pallas_call x1, Pallas kernels, inner_rows(): pl.pallas_call(inner_kernel, out_shape=struct(((R - 2) * C, WX)), in_spec...  3.06 us
    pallas_call x1, Pallas kernels, own_tile(): pl.pallas_call(own_kernel, out_shape=(struct((R * C, W)), struct(((R - 2)...  3.05 us
    ppermute x1, starting transfers between devices, local(): below = lax.ppermute(top, 'lat', [(i + 1, i) for i in range(count - 1)])  2.1 us
  transfers between devices with their start and end apart: 3, of which 1 were waited for; matrix products, arithmetic and copies ran while one was open for 2% of the time, Pallas kernels for 10%

profile of v1, /device:TPU:1, one launch (start us, length us, event | category | flops | bytes accessed | tf_op | source)
XLA Modules:
  0.0 61.5 jit_solution(12374745658358644298)
XLA Ops:
  0.0 0.8 %copy.14.coarse = bf16[1,4,30,128]{3,2,1,0:T(8,128)(2,1)S(1)} copy(bf16[1,4,30,128]{3,1,2,0:T(4,128)(2,1)} %param.13) | data formatting | bytes 61440 | tf_op args[1]
  0.8 1.7 %copy-done = bf16[64,16,1280]{2,1,0:T(8,128)(2,1)S(1)} copy-done((bf16[64,16,1280]{2,1,0:T(8,128)(2,1)S(1)}, bf16[64,16,1280]{2,1,0:T(8,128)(2,1)}, u32[]{:S(2)}) %copy-start) | copy-done | bytes 2621464
  2.5 0.7 %copy-done.15 = s32[1,1,4,4]{3,2,1,0:T(4,128)S(1)} copy-done((s32[1,1,4,4]{3,2,1,0:T(4,128)S(1)}, s32[1,1,4,4]{3,2,1,0:T(4,128)}, u32[]{:S(2)}) %copy-start.15) | copy-done | bytes 88
  3.2 0.7 %copy-done.17 = s32[1,1,4,4]{3,2,1,0:T(4,128)S(1)} copy-done((s32[1,1,4,4]{3,2,1,0:T(4,128)S(1)}, s32[1,1,4,4]{3,2,1,0:T(4,128)}, u32[]{:S(2)}) %copy-start.17) | copy-done | bytes 88
  3.9 0.7 %copy-done.19 = s32[1,1,4,4]{3,2,1,0:T(4,128)S(1)} copy-done((s32[1,1,4,4]{3,2,1,0:T(4,128)S(1)}, s32[1,1,4,4]{3,2,1,0:T(4,128)}, u32[]{:S(2)}) %copy-start.19) | copy-done | bytes 88
  4.5 0.7 %copy-done.21 = s32[1,1,4]{2,1,0:T(1,128)S(1)} copy-done((s32[1,1,4]{2,1,0:T(1,128)S(1)}, s32[1,1,4]{2,1,0:T(1,128)}, u32[]{:S(2)}) %copy-start.21) | copy-done | bytes 40
  5.2 1.9 %shard_map.119 = bf16[16,192,128]{2,1,0:T(8,128)(2,1)} custom-call(bf16[64,16,1280]{2,1,0:T(8,128)(2,1)S(1)} %copy-done, bf16[64,16,1280]{2,1,0:T(8,128)(2,1)S(1)} %copy-done, bf16[1,4,30,128]{3,2,1,0:T(8,128)(2,1)S(1)} %copy.14.coarse, s32[1,1,4,4]{3,2,1,0:T(4,128)S(1)} %copy-done.15, s32[1,1,4,4]{3,2,1,0:T(4,128)S(1)} %copy-done.17, ...), custom_call_target="tpu_custom_call" | custom-call | tf_op jit(solution)/shard_map/pallas_call | solution.py:76
  7.1 8.6 %all-to-all-start = ((bf16[16,192,128]{2,1,0:T(8,128)(2,1)}), bf16[16,192,128]{2,1,0:T(8,128)(2,1)S(1)}, u32[]{:S(2)}, u32[]{:S(2)}) async-start(bf16[16,192,128]{2,1,0:T(8,128)(2,1)} %shard_map.119), calls=%async_computation | async-start | bytes 1572864 | tf_op jit(solution)/shard_map/all_to_all | solution.py:310
  15.7 0.0 copy-done.25
  15.7 0.8 %copy.13.conv_cond = bf16[3,3,64,30]{3,2,1,0:T(8,128)(2,1)} copy(bf16[3,3,64,30]{2,3,1,0:T(8,128)(2,1)S(1)} %copy-done.25) | data formatting | bytes 69120 | tf_op args[8]
  16.5 1.7 %copy-done.1 = bf16[64,16,1280]{2,1,0:T(8,128)(2,1)S(1)} copy-done((bf16[64,16,1280]{2,1,0:T(8,128)(2,1)S(1)}, bf16[64,16,1280]{2,1,0:T(8,128)(2,1)}, u32[]{:S(2)}) %copy-start.1) | copy-done | bytes 2621464
  18.3 0.9 %copy-done.14 = bf16[3,3,64,30]{3,2,1,0:T(8,128)(2,1)S(1)} copy-done((bf16[3,3,64,30]{3,2,1,0:T(8,128)(2,1)S(1)}, bf16[3,3,64,30]{3,2,1,0:T(8,128)(2,1)}, u32[]{:S(2)}) %copy-start.14) | copy-done | bytes 34584
  19.2 0.9 %copy-done.23 = bf16[3,3,64,64]{3,2,1,0:T(8,128)(2,1)S(1)} copy-done((bf16[3,3,64,64]{3,2,1,0:T(8,128)(2,1)S(1)}, bf16[3,3,64,64]{3,2,1,0:T(8,128)(2,1)}, u32[]{:S(2)}) %copy-start.23) | copy-done | bytes 73752
  20.1 0.9 %copy-done.24 = bf16[3,3,64,64]{3,2,1,0:T(8,128)(2,1)S(1)} copy-done((bf16[3,3,64,64]{3,2,1,0:T(8,128)(2,1)S(1)}, bf16[3,3,64,64]{3,2,1,0:T(8,128)(2,1)}, u32[]{:S(2)}) %copy-start.24) | copy-done | bytes 73752
  21.0 3.0 %shard_map.118 = (bf16[1024,1280]{1,0:T(8,128)(2,1)S(1)}, f32[896,1408]{1,0:T(8,128)S(1)}, bf16[128,768]{1,0:T(8,128)(2,1)S(1)}, bf16[128,384]{1,0:T(8,128)(2,1)S(1)}, bf16[128,768]{1,0:T(8,128)(2,1)S(1)}) custom-call(bf16[64,16,1280]{2,1,0:T(8,128)(2,1)S(1)} %copy-done.1, bf16[3,3,64,64]{3,2,1,0:T(8,128)(2,1)S(1)} %copy-done.23, ...), custom_call_target="tpu_custom_call" | custom-call | flops 3000000000 | bytes 12000000 | tf_op jit(solution)/shard_map/pallas_call | solution.py:126
  24.1 0.0 copy-start.3
  24.1 2.2 %copy-done.3 = f32[896,1408]{1,0:T(8,128)} copy-done((f32[896,1408]{1,0:T(8,128)}, f32[896,1408]{1,0:T(8,128)S(1)}, u32[]{:S(2)}) %copy-start.3) | copy-done | bytes 5046296
  26.3 0.7 %copy-done.7 = bf16[128,768]{1,0:T(8,128)(2,1)} copy-done((bf16[128,768]{1,0:T(8,128)(2,1)}, bf16[128,768]{1,0:T(8,128)(2,1)S(1)}, u32[]{:S(2)}) %copy-start.7) | copy-done | bytes 196632
  27.0 0.7 %copy-done.12 = bf16[128,768]{1,0:T(8,128)(2,1)} copy-done((bf16[128,768]{1,0:T(8,128)(2,1)}, bf16[128,768]{1,0:T(8,128)(2,1)S(1)}, u32[]{:S(2)}) %copy-start.12) | copy-done | bytes 196632
  27.7 1.2 %all-to-all-done.got = bf16[16,192,128]{2,1,0:T(8,128)(2,1)S(1)} async-done(((bf16[16,192,128]{2,1,0:T(8,128)(2,1)}), bf16[16,192,128]{2,1,0:T(8,128)(2,1)S(1)}, u32[]{:S(2)}, u32[]{:S(2)}) %all-to-all-start) | async-done | bytes 786464 | tf_op jit(solution)/shard_map/all_to_all | solution.py:310
  28.9 0.0 copy-done.16
  28.9 0.0 copy-done.18
  28.9 0.0 copy-done.20
  28.9 0.0 copy-done.22
  28.9 0.0 copy-start.2
  28.9 2.5 %copy-done.2 = bf16[4,128,5120]{2,1,0:T(8,128)(2,1)S(1)} copy-done((bf16[4,128,5120]{2,1,0:T(8,128)(2,1)S(1)}, bf16[4,128,5120]{2,1,0:T(8,128)(2,1)}, u32[]{:S(2)}) %copy-start.2) | copy-done | bytes 5242904
  31.4 3.9 %shard_map.120 = (bf16[512,1408]{1,0:T(8,128)(2,1)S(1)}, bf16[1024,128]{1,0:T(8,128)(2,1)S(1)}, bf16[192,1408]{1,0:T(8,128)(2,1)}, bf16[192,1408]{1,0:T(8,128)(2,1)}) custom-call(bf16[16,192,128]{2,1,0:T(8,128)(2,1)S(1)} %all-to-all-done.got, s32[1,1,4,4]{3,2,1,0:T(4,128)S(1)} %copy-done.16, s32[1,1,4,4]{3,2,1,0:T(4,128)S(1)} %copy-done.18, ...), custom_call_target="tpu_custom_call" | custom-call | tf_op jit(solution)/shard_map/pallas_call | solution.py:206
  35.4 0.0 copy-start.5
  35.4 1.1 %copy-done.5 = bf16[512,1408]{1,0:T(8,128)(2,1)} copy-done((bf16[512,1408]{1,0:T(8,128)(2,1)}, bf16[512,1408]{1,0:T(8,128)(2,1)S(1)}, u32[]{:S(2)}) %copy-start.5) | copy-done | bytes 1441816
  36.5 0.7 %copy-done.10 = bf16[1024,128]{1,0:T(8,128)(2,1)} copy-done((bf16[1024,128]{1,0:T(8,128)(2,1)}, bf16[1024,128]{1,0:T(8,128)(2,1)S(1)}, u32[]{:S(2)}) %copy-start.10) | copy-done | bytes 262168
  37.2 5.3 %collective-permute-start = (bf16[192,1408]{1,0:T(8,128)(2,1)}, bf16[192,1408]{1,0:T(8,128)(2,1)S(1)}, u32[]{:S(2)}, u32[]{:S(2)}) collective-permute-start(bf16[192,1408]{1,0:T(8,128)(2,1)} %get-tuple-element.21.bottom), channel_id=1, source_target_pairs={{0,16},{16,32},{32,48},{48,64},{64,80},{80,96},{96,112},{1,17},{17... | collective-permute-start | bytes 1622024 | tf_op jit(solution)/shard_map/ppermute | solution.py:315
  42.5 2.1 %collective-permute-start.1 = (bf16[192,1408]{1,0:T(8,128)(2,1)}, bf16[192,1408]{1,0:T(8,128)(2,1)}, u32[]{:S(2)}, u32[]{:S(2)}) collective-permute-start(bf16[192,1408]{1,0:T(8,128)(2,1)} %get-tuple-element.20.top), channel_id=1, source_target_pairs={{16,0},{32,16},{48,32},{64,48},{80,64},{96,80},{112,96},{17,1},{33... | collective-permute-start | bytes 1622024 | tf_op jit(solution)/shard_map/ppermute | solution.py:316
  44.6 0.0 copy-done.26
  44.6 0.1 maximum_bitcast_fusion
  44.7 0.1 copy.15.bias
  44.8 0.0 copy-done.27
  44.8 0.1 maximum_bitcast_fusion.1
  44.9 0.1 copy.17.bias_out
  45.0 2.4 %copy-done.4 = f32[896,1408]{1,0:T(8,128)S(1)} copy-done((f32[896,1408]{1,0:T(8,128)S(1)}, f32[896,1408]{1,0:T(8,128)}, u32[]{:S(2)}) %copy-start.4) | copy-done | bytes 5046296
  47.4 1.4 %copy-done.6 = bf16[512,1408]{1,0:T(8,128)(2,1)S(1)} copy-done((bf16[512,1408]{1,0:T(8,128)(2,1)S(1)}, bf16[512,1408]{1,0:T(8,128)(2,1)}, u32[]{:S(2)}) %copy-start.6) | copy-done | bytes 1441816
  48.8 0.9 %copy-done.8 = bf16[128,768]{1,0:T(8,128)(2,1)S(1)} copy-done((bf16[128,768]{1,0:T(8,128)(2,1)S(1)}, bf16[128,768]{1,0:T(8,128)(2,1)}, u32[]{:S(2)}) %copy-start.8) | copy-done | bytes 196632
  49.7 0.9 %copy-done.11 = bf16[1024,128]{1,0:T(8,128)(2,1)S(1)} copy-done((bf16[1024,128]{1,0:T(8,128)(2,1)S(1)}, bf16[1024,128]{1,0:T(8,128)(2,1)}, u32[]{:S(2)}) %copy-start.11) | copy-done | bytes 262168
  50.7 3.1 %shard_map.121.act = bf16[896,1408]{1,0:T(8,128)(2,1)S(1)} custom-call(f32[896,1408]{1,0:T(8,128)S(1)} %copy-done.4, bf16[512,1408]{1,0:T(8,128)(2,1)S(1)} %copy-done.6, bf16[1024,128]{1,0:T(8,128)(2,1)S(1)} %copy-done.11, bf16[128,768]{1,0:T(8,128)(2,1)S(1)} %copy-done.8, bf16[128,384]{1,0:T(8,128)(2,1)S(1)} %get-tuple-element.19.w_cond, ...), custom_call_target="tpu_custom_call" | custom-call | flops 2000000000 | bytes 10000000 | tf_op jit(solution)/shard_map/pallas_call | solution.py:245
  53.7 0.0 collective-permute-done.above
  53.7 0.0 collective-permute-done.1.below
  53.8 0.0 copy-done.9
  53.8 0.0 copy-done.13
  53.8 7.7 %shard_map.122 = bf16[64,16,1280]{2,1,0:T(8,128)(2,1)} custom-call(bf16[896,1408]{1,0:T(8,128)(2,1)S(1)} %shard_map.121.act, bf16[192,1408]{1,0:T(8,128)(2,1)} %get-tuple-element.20.top, bf16[192,1408]{1,0:T(8,128)(2,1)} %get-tuple-element.21.bottom, bf16[192,1408]{1,0:T(8,128)(2,1)S(1)} %collective-permute-done.above, ...), custom_call_target="tpu_custom_call" | custom-call | tf_op jit(solution)/shard_map/pallas_call | solution.py:293
  (25 shorter events, 0.0 us)
Async XLA Ops:
  0.8 1.7 %copy-start = (bf16[64,16,1280]{2,1,0:T(8,128)(2,1)S(1)}, bf16[64,16,1280]{2,1,0:T(8,128)(2,1)}, u32[]{:S(2)}) copy-start(bf16[64,16,1280]{2,1,0:T(8,128)(2,1)} %last.1) | copy-start | bytes 7864324
  2.5 0.7 %copy-start.15 = (s32[1,1,4,4]{3,2,1,0:T(4,128)S(1)}, s32[1,1,4,4]{3,2,1,0:T(4,128)}, u32[]{:S(2)}) copy-start(s32[1,1,4,4]{3,2,1,0:T(4,128)} %owner.3) | copy-start | bytes 196
  3.2 0.7 %copy-start.17 = (s32[1,1,4,4]{3,2,1,0:T(4,128)S(1)}, s32[1,1,4,4]{3,2,1,0:T(4,128)}, u32[]{:S(2)}) copy-start(s32[1,1,4,4]{3,2,1,0:T(4,128)} %slot.3) | copy-start | bytes 196
  3.9 0.7 %copy-start.19 = (s32[1,1,4,4]{3,2,1,0:T(4,128)S(1)}, s32[1,1,4,4]{3,2,1,0:T(4,128)}, u32[]{:S(2)}) copy-start(s32[1,1,4,4]{3,2,1,0:T(4,128)} %weight.3) | copy-start | bytes 196
  4.5 0.7 %copy-start.21 = (s32[1,1,4]{2,1,0:T(1,128)S(1)}, s32[1,1,4]{2,1,0:T(1,128)}, u32[]{:S(2)}) copy-start(s32[1,1,4]{2,1,0:T(1,128)} %counts.3) | copy-start | bytes 52
  5.2 10.5 %copy-start.25 = (bf16[3,3,64,30]{2,3,1,0:T(8,128)(2,1)S(1)}, bf16[3,3,64,30]{2,3,1,0:T(8,128)(2,1)}, u32[]{:S(2)}) copy-start(bf16[3,3,64,30]{2,3,1,0:T(8,128)(2,1)} %param.20) | copy-start | bytes 103684
  7.1 21.8 %all-to-all-start = ((bf16[16,192,128]{2,1,0:T(8,128)(2,1)}), bf16[16,192,128]{2,1,0:T(8,128)(2,1)S(1)}, u32[]{:S(2)}, u32[]{:S(2)}) async-start(bf16[16,192,128]{2,1,0:T(8,128)(2,1)} %shard_map.119), calls=%async_computation | async-start | bytes 1572864 | tf_op jit(solution)/shard_map/all_to_all | solution.py:310
  16.5 1.7 %copy-start.1 = (bf16[64,16,1280]{2,1,0:T(8,128)(2,1)S(1)}, bf16[64,16,1280]{2,1,0:T(8,128)(2,1)}, u32[]{:S(2)}) copy-start(bf16[64,16,1280]{2,1,0:T(8,128)(2,1)} %last.1) | copy-start | bytes 7864324
  18.3 0.9 %copy-start.14 = (bf16[3,3,64,30]{3,2,1,0:T(8,128)(2,1)S(1)}, bf16[3,3,64,30]{3,2,1,0:T(8,128)(2,1)}, u32[]{:S(2)}) copy-start(bf16[3,3,64,30]{3,2,1,0:T(8,128)(2,1)} %copy.13.conv_cond) | copy-start | bytes 103684
  19.2 0.9 %copy-start.23 = (bf16[3,3,64,64]{3,2,1,0:T(8,128)(2,1)S(1)}, bf16[3,3,64,64]{3,2,1,0:T(8,128)(2,1)}, u32[]{:S(2)}) copy-start(bf16[3,3,64,64]{3,2,1,0:T(8,128)(2,1)} %conv_in.1) | copy-start | bytes 221188
  20.1 0.9 %copy-start.24 = (bf16[3,3,64,64]{3,2,1,0:T(8,128)(2,1)S(1)}, bf16[3,3,64,64]{3,2,1,0:T(8,128)(2,1)}, u32[]{:S(2)}) copy-start(bf16[3,3,64,64]{3,2,1,0:T(8,128)(2,1)} %conv_out.1) | copy-start | bytes 221188
  21.0 7.9 %copy-start.16 = (s32[1,1,4,4]{3,2,1,0:T(4,128)S(1)}, s32[1,1,4,4]{3,2,1,0:T(4,128)}, u32[]{:S(2)}) copy-start(s32[1,1,4,4]{3,2,1,0:T(4,128)} %owner.3) | copy-start | bytes 196
  21.0 7.9 %copy-start.18 = (s32[1,1,4,4]{3,2,1,0:T(4,128)S(1)}, s32[1,1,4,4]{3,2,1,0:T(4,128)}, u32[]{:S(2)}) copy-start(s32[1,1,4,4]{3,2,1,0:T(4,128)} %slot.3) | copy-start | bytes 196
  21.0 7.9 %copy-start.20 = (s32[1,1,4,4]{3,2,1,0:T(4,128)S(1)}, s32[1,1,4,4]{3,2,1,0:T(4,128)}, u32[]{:S(2)}) copy-start(s32[1,1,4,4]{3,2,1,0:T(4,128)} %weight.3) | copy-start | bytes 196
  21.0 7.9 %copy-start.22 = (s32[1,1,4]{2,1,0:T(1,128)S(1)}, s32[1,1,4]{2,1,0:T(1,128)}, u32[]{:S(2)}) copy-start(s32[1,1,4]{2,1,0:T(1,128)} %counts.3) | copy-start | bytes 52
  24.1 2.3 %copy-start.3 = (f32[896,1408]{1,0:T(8,128)}, f32[896,1408]{1,0:T(8,128)S(1)}, u32[]{:S(2)}) copy-start(f32[896,1408]{1,0:T(8,128)S(1)} %get-tuple-element.14.hid) | copy-start | bytes 15138820
  26.3 0.7 %copy-start.7 = (bf16[128,768]{1,0:T(8,128)(2,1)}, bf16[128,768]{1,0:T(8,128)(2,1)S(1)}, u32[]{:S(2)}) copy-start(bf16[128,768]{1,0:T(8,128)(2,1)S(1)} %get-tuple-element.18.w_in) | copy-start | bytes 589828
  27.0 0.7 %copy-start.12 = (bf16[128,768]{1,0:T(8,128)(2,1)}, bf16[128,768]{1,0:T(8,128)(2,1)S(1)}, u32[]{:S(2)}) copy-start(bf16[128,768]{1,0:T(8,128)(2,1)S(1)} %get-tuple-element.22.w_out) | copy-start | bytes 589828
  28.9 2.5 %copy-start.2 = (bf16[4,128,5120]{2,1,0:T(8,128)(2,1)S(1)}, bf16[4,128,5120]{2,1,0:T(8,128)(2,1)}, u32[]{:S(2)}) copy-start(bf16[4,128,5120]{2,1,0:T(8,128)(2,1)} %param.18) | copy-start | bytes 15728644
  31.4 13.2 %copy-start.26 = (f32[64]{0:T(128)S(1)}, f32[64]{0:T(128)}, u32[]{:S(2)}) copy-start(f32[64]{0:T(128)} %param.21) | copy-start | bytes 772
  31.4 13.4 %copy-start.27 = (f32[64]{0:T(128)S(1)}, f32[64]{0:T(128)}, u32[]{:S(2)}) copy-start(f32[64]{0:T(128)} %param.23) | copy-start | bytes 772
  35.4 1.1 %copy-start.5 = (bf16[512,1408]{1,0:T(8,128)(2,1)}, bf16[512,1408]{1,0:T(8,128)(2,1)S(1)}, u32[]{:S(2)}) copy-start(bf16[512,1408]{1,0:T(8,128)(2,1)S(1)} %get-tuple-element.16.cond) | copy-start | bytes 4325380
  36.5 0.7 %copy-start.10 = (bf16[1024,128]{1,0:T(8,128)(2,1)}, bf16[1024,128]{1,0:T(8,128)(2,1)S(1)}, u32[]{:S(2)}) copy-start(bf16[1024,128]{1,0:T(8,128)(2,1)S(1)} %get-tuple-element.17.halo) | copy-start | bytes 786436
  37.2 16.5 %collective-permute-start = (bf16[192,1408]{1,0:T(8,128)(2,1)}, bf16[192,1408]{1,0:T(8,128)(2,1)S(1)}, u32[]{:S(2)}, u32[]{:S(2)}) collective-permute-start(bf16[192,1408]{1,0:T(8,128)(2,1)} %get-tuple-element.21.bottom), channel_id=1, source_target_pairs={{0,16},{16,32},{32,48},{48,64},{64,80},{80,96},{96,112},{1,17},{17... | collective-permute-start | bytes 1622024 | tf_op jit(solution)/shard_map/ppermute | solution.py:315
  42.5 11.3 %collective-permute-start.1 = (bf16[192,1408]{1,0:T(8,128)(2,1)}, bf16[192,1408]{1,0:T(8,128)(2,1)}, u32[]{:S(2)}, u32[]{:S(2)}) collective-permute-start(bf16[192,1408]{1,0:T(8,128)(2,1)} %get-tuple-element.20.top), channel_id=1, source_target_pairs={{16,0},{32,16},{48,32},{64,48},{80,64},{96,80},{112,96},{17,1},{33... | collective-permute-start | bytes 1622024 | tf_op jit(solution)/shard_map/ppermute | solution.py:316
  45.0 2.4 %copy-start.4 = (f32[896,1408]{1,0:T(8,128)S(1)}, f32[896,1408]{1,0:T(8,128)}, u32[]{:S(2)}) copy-start(f32[896,1408]{1,0:T(8,128)} %copy-done.3) | copy-start | bytes 15138820
  47.4 1.4 %copy-start.6 = (bf16[512,1408]{1,0:T(8,128)(2,1)S(1)}, bf16[512,1408]{1,0:T(8,128)(2,1)}, u32[]{:S(2)}) copy-start(bf16[512,1408]{1,0:T(8,128)(2,1)} %copy-done.5) | copy-start | bytes 4325380
  48.8 0.9 %copy-start.8 = (bf16[128,768]{1,0:T(8,128)(2,1)S(1)}, bf16[128,768]{1,0:T(8,128)(2,1)}, u32[]{:S(2)}) copy-start(bf16[128,768]{1,0:T(8,128)(2,1)} %copy-done.7) | copy-start | bytes 589828
  49.7 0.9 %copy-start.11 = (bf16[1024,128]{1,0:T(8,128)(2,1)S(1)}, bf16[1024,128]{1,0:T(8,128)(2,1)}, u32[]{:S(2)}) copy-start(bf16[1024,128]{1,0:T(8,128)(2,1)} %copy-done.10) | copy-start | bytes 786436
  50.7 3.1 %copy-start.9 = (bf16[128,768]{1,0:T(8,128)(2,1)S(1)}, bf16[128,768]{1,0:T(8,128)(2,1)}, u32[]{:S(2)}) copy-start(bf16[128,768]{1,0:T(8,128)(2,1)} %copy-done.7) | copy-start | bytes 589828
  50.7 3.1 %copy-start.13 = (bf16[128,768]{1,0:T(8,128)(2,1)S(1)}, bf16[128,768]{1,0:T(8,128)(2,1)}, u32[]{:S(2)}) copy-start(bf16[128,768]{1,0:T(8,128)(2,1)} %copy-done.12) | copy-start | bytes 589828

commit v2 on v1

v2 whole, which is shorter than its diff:
```python
import jax
import jax.numpy as jnp
from jax import lax
from jax.experimental import pallas as pl
from jax.experimental.pallas import tpu as pltpu
from jax.sharding import PartitionSpec as P

BF = jnp.bfloat16
F32 = jnp.float32
MIB = 1024 * 1024

C = 64
CP = 32
R = 16
W = 1280
LT = 128
WX = W + LT
PEERS = 16
HELD = 4
SUBS = 4
SLOTS = 4
KINDS = 4
EDGE = 16
MSG = HELD * CP + EDGE
PAIRS = R // 2 - 1
TAPS = 12 * C
TAPS_C = 12 * CP
PARTS = 4


def vmem(n=1):
    return [pl.BlockSpec(memory_space=pltpu.VMEM)] * n


def smem(n=1):
    return [pl.BlockSpec(memory_space=pltpu.SMEM)] * n


def params(mib):
    return pltpu.CompilerParams(vmem_limit_bytes=mib * MIB)


def struct(shape, dtype=BF):
    return jax.ShapeDtypeStruct(shape, dtype)


def kept(shape, dtype=BF):
    return pltpu.VMEM(shape, dtype)


def hbm(n=1):
    return [pl.BlockSpec(memory_space=pltpu.HBM)] * n


def in_hbm(*arrays):
    return [pltpu.with_memory_space_constraint(a, pltpu.HBM) for a in arrays]


def in_vmem(*arrays):
    return [pltpu.with_memory_space_constraint(a, pltpu.VMEM) for a in arrays]


def iota(shape, dim):
    return lax.broadcasted_iota(jnp.int32, shape, dim)


def message_kernel(first, last, coarse, owner, slot, weight, counts, out):
    me = lax.axis_index("lon")
    lane = iota((C, R, LT), 2)
    edge = jnp.where(lane < 64, first[...].astype(F32), last[...].astype(F32))
    edge = jnp.swapaxes(edge.astype(BF), 0, 1)
    edge = jnp.concatenate([edge[r] for r in range(R)], axis=1)
    row = iota((R * LT, LT), 0)
    col = iota((R * LT, LT), 1)
    at = row % LT
    kind = jnp.where(at < 64, at, at - 124)
    wanted = ((at < 2) | (at >= 126)) & (col == kind * R + row // LT)
    pick = jnp.where(wanted, 1.0, 0.0).astype(BF)
    packed = jnp.dot(edge, pick, preferred_element_type=F32)
    sides = []
    for side in range(2):
        parts = [packed[g * EDGE : (g + 1) * EDGE, side * 32 : side * 32 + 32] for g in range(C // EDGE)]
        sides.append(jnp.concatenate(parts, axis=1))
    lanes = iota((2, HELD, LT), 2)
    lists = jnp.zeros((2, HELD, LT), F32)
    for s in range(SUBS):
        live = counts[0, 0, s]
        for k in range(SLOTS):
            n = s * SLOTS + k
            block = owner[0, 0, s, k] * HELD + slot[0, 0, s, k]
            kind_id = jnp.where(k < live, weight[0, 0, s, k], KINDS)
            lists = jnp.where(lanes == n, block.astype(F32), lists)
            lists = jnp.where(lanes == 16 + n, kind_id.astype(F32), lists)
    chans = coarse[0].astype(F32)
    blocks = jnp.swapaxes(jnp.concatenate([chans, lists], axis=0), 0, 1)
    blocks = blocks.reshape(HELD * CP, LT).astype(BF)
    right = lax.rem(me + 1, PEERS)
    for p in range(PEERS):
        out[p, 0 : HELD * CP] = blocks
        out[p, HELD * CP :] = jnp.where(right == p, sides[1], sides[0]).astype(BF)


def message(noisy, coarse, owner, slot, weight, counts):
    return pl.pallas_call(
        message_kernel,
        grid=(1,),
        out_shape=struct((PEERS, MSG, LT)),
        in_specs=[
            pl.BlockSpec((C, R, LT), lambda i: (0, 0, 0)),
            pl.BlockSpec((C, R, LT), lambda i: (0, 0, W // LT - 1)),
            pl.BlockSpec(coarse.shape, lambda i: (0, 0, 0, 0)),
        ]
        + smem(4),
        out_specs=pl.BlockSpec((PEERS, MSG, LT), lambda i: (0, 0, 0)),
        compiler_params=params(12),
    )(*in_hbm(noisy, noisy, coarse, owner, slot, weight, counts))


def load(src, dst, sem):
    copy = pltpu.make_async_copy(src, dst, sem)
    copy.start()
    return copy


def shifted(x, width):
    return [pltpu.roll(x, 1, 1), x, pltpu.roll(x, width - 1, 1)]


def pair_weights(taps):
    rows = jnp.concatenate(taps, axis=1)
    blank = jnp.zeros((rows.shape[0], rows.shape[1] // 3), BF)
    return jnp.concatenate(
        [jnp.concatenate([rows, blank], axis=1), jnp.concatenate([blank, rows], axis=1)], axis=0
    )


def cond_tap(tap):
    tap = jnp.concatenate([tap.astype(F32), jnp.zeros((CP - tap.shape[0], tap.shape[1]), F32)], axis=0)
    return tap.T.astype(BF)


def bias_column(row):
    same = iota((C, C), 0) == iota((C, C), 1)
    column = jnp.sum(jnp.where(same, row, 0.0), axis=1, keepdims=True)
    return jnp.concatenate([column, column], axis=0)


def own_kernel(noisy, conv_in, conv_cond, conv_out, bias_in, bias_out, xs, hid, wts, bias, x3, buf, sems):
    loads = []
    for g in range(PARTS):
        part = pl.ds(g * (C // PARTS), C // PARTS)
        loads.append(load(noisy.at[part], buf.at[part], sems.at[g]))
    taps = [(i, j) for i in range(3) for j in range(3)]
    wts[:, 0:TAPS] = pair_weights([conv_in[i, j] for i, j in taps])
    wts[:, TAPS : 2 * TAPS] = pair_weights([conv_out[i, j] for i, j in taps])
    wts[:, 2 * TAPS :] = pair_weights([cond_tap(conv_cond[i, j]) for i, j in taps])
    bias[:, 0:LT] = jnp.broadcast_to(bias_column(bias_in[...]), (2 * C, LT))
    bias[:, LT:] = jnp.broadcast_to(bias_column(bias_out[...]), (2 * C, LT))
    for copy in loads:
        copy.wait()
    xs[...] = jnp.swapaxes(buf[...], 0, 1).reshape(R * C, W)
    blank = jnp.zeros((C, LT), BF)
    for r in range(R):
        x = jnp.concatenate([xs[pl.ds(r * C, C), :], blank], axis=1)
        for d, y in enumerate(shifted(x, WX)):
            x3[pl.ds((r * 3 + d) * C, C), :] = y
    for i in range(PAIRS):
        v = jnp.dot(wts[:, 0:TAPS], x3[pl.ds(i * 6 * C, 12 * C), :], preferred_element_type=F32)
        hid[i] = (v + bias[:, 0:1]).astype(BF)


def own_tile(noisy, conv_in, conv_cond, conv_out, bias_in, bias_out):
    return pl.pallas_call(
        own_kernel,
        out_shape=(
            kept((R * C, W)),
            kept((PAIRS, 2 * C, WX)),
            kept((2 * C, 2 * TAPS + TAPS_C)),
            kept((2 * C, 2 * LT), F32),
        ),
        in_specs=hbm(1) + vmem(5),
        out_specs=tuple(vmem(4)),
        scratch_shapes=[
            pltpu.VMEM((R * 3 * C, WX), BF),
            pltpu.VMEM((C, R, W), BF),
            pltpu.SemaphoreType.DMA((PARTS,)),
        ],
        compiler_params=params(18),
        cost_estimate=pl.CostEstimate(flops=3 * 10**9, bytes_accessed=12 * 10**6, transcendentals=0),
    )(*in_hbm(noisy, conv_in, conv_cond, conv_out, bias_in, bias_out))


def cond_kernel(got, table_hbm, xs, cond, halo, top, bottom, acc, grp, ints, lists, table, sem, sems):
    loads = []
    for r in range(R // SUBS):
        loads.append(load(table_hbm.at[:, pl.ds(r * W, W)], table.at[r], sems.at[r]))
    me = lax.axis_index("lon")
    left = lax.rem(me + PEERS - 1, PEERS)
    right = lax.rem(me + 1, PEERS)
    for d, p in enumerate((me, left, right)):
        ints[d] = got[p, CP - 16 : CP, :].astype(F32).astype(jnp.int32)
    copy = load(ints, lists, sem)
    acc[...] = jnp.zeros_like(acc)

    rows = []
    for g in range(C // EDGE):
        cols = slice(g * 32, g * 32 + 32)
        side = [got[p, HELD * CP :, cols].astype(F32) for p in (right, left)]
        rows.append(jnp.concatenate(side + [jnp.zeros((EDGE, 64), F32)], axis=1))
    both = jnp.concatenate(rows, axis=0).astype(BF)
    src = iota((LT, R * LT), 0)
    dst = iota((LT, R * LT), 1)
    at = dst % LT
    kind = jnp.where(at < 64, at, at - 124)
    wanted = ((at < 2) | (at >= 126)) & (src == kind * R + dst // LT)
    place = jnp.where(wanted, 1.0, 0.0).astype(BF)
    tiles = jnp.dot(both, place, preferred_element_type=F32).astype(BF)
    for r in range(R):
        halo[pl.ds(r * C, C), :] = tiles[:, r * LT : (r + 1) * LT]

    copy.wait()
    for d in range(3):
        for s in range(SUBS):
            for k in range(SLOTS):
                n = s * SLOTS + k
                block = lists[d, 14, n]
                part = got[block // HELD, pl.ds(pl.multiple_of(lax.rem(block, HELD) * CP, CP), CP), :]
                at = (d * SUBS + s) * (KINDS + 1) + lists[d, 14, 16 + n]
                acc[at] = acc[at] + part.astype(F32)
    for d in range(3):
        for s in range(SUBS):
            for w in range(KINDS):
                grp[d, pl.ds(s * CP, CP), w * LT : (w + 1) * LT] = acc[(d * SUBS + s) * (KINDS + 1) + w].astype(BF)

    lane = iota((SUBS * CP, LT), 1)
    for r in range(R // SUBS):
        loads[r].wait()
        own = jnp.dot(grp[0], table[r], preferred_element_type=F32).astype(BF)
        lhs = jnp.dot(grp[1], table[r, :, W - LT : W], preferred_element_type=F32)
        rhs = jnp.dot(grp[2], table[r, :, 0:LT], preferred_element_type=F32)
        side = jnp.where(lane < 2, rhs, jnp.where(lane >= 126, lhs, 0.0)).astype(BF)
        for s in range(SUBS):
            at = pl.ds((s * SUBS + r) * CP, CP)
            cond[at, 0:W] = own[s * CP : (s + 1) * CP]
            cond[at, W:WX] = side[s * CP : (s + 1) * CP]
    for out, r0 in ((top, 0), (bottom, R - 2)):
        out[0 : 2 * C, 0:W] = xs[pl.ds(r0 * C, 2 * C), :]
        out[0 : 2 * C, W:WX] = halo[pl.ds(r0 * C, 2 * C), :]
        out[2 * C : 2 * C + 2 * CP, :] = cond[pl.ds(r0 * CP, 2 * CP), :]


def cond_tile(got, table, xs):
    edge = struct((2 * (C + CP), WX))
    return pl.pallas_call(
        cond_kernel,
        out_shape=(kept((R * CP, WX)), kept((R * C, LT)), edge, edge),
        in_specs=vmem(1) + hbm(1) + vmem(1),
        out_specs=tuple(vmem(4)),
        scratch_shapes=[
            pltpu.VMEM((3 * SUBS * (KINDS + 1), CP, LT), F32),
            pltpu.VMEM((3, SUBS * CP, KINDS * LT), BF),
            pltpu.VMEM((3, 16, LT), jnp.int32),
            pltpu.SMEM((3, 16, LT), jnp.int32),
            pltpu.VMEM((R // SUBS, KINDS * LT, W), BF),
            pltpu.SemaphoreType.DMA,
            pltpu.SemaphoreType.DMA((R // SUBS,)),
        ],
        compiler_params=params(14),
    )(*in_vmem(got), *in_hbm(table), *in_vmem(xs))


def silu(v):
    return v / (1.0 + jnp.exp(-v))


def inner_kernel(hid, cond, halo, xs, wts, bias, zi, edge, c3, h3, a3):
    for r in range(R):
        for d, y in enumerate(shifted(cond[pl.ds(r * CP, CP), :], WX)):
            c3[pl.ds((r * 3 + d) * CP, CP), :] = y
        blank = jnp.zeros((C, LT), BF)
        h = jnp.concatenate([blank, halo[pl.ds(r * C, C), :], blank], axis=1)
        for d, y in enumerate(shifted(h, 3 * LT)):
            h3[pl.ds((r * 3 + d) * C, C), :] = y
    for i in range(PAIRS):
        v = jnp.dot(wts[:, 2 * TAPS :], c3[pl.ds(i * 6 * CP, 12 * CP), :], preferred_element_type=F32)
        e = jnp.dot(wts[:, 0:TAPS], h3[pl.ds(i * 6 * C, 12 * C), :], preferred_element_type=F32)
        v = v + hid[i].astype(F32)
        v = jnp.concatenate(
            [v[:, 0:LT] + e[:, 2 * LT :], v[:, LT : W - LT], v[:, W - LT :] + e[:, 0 : 2 * LT]], axis=1
        )
        a = silu(v).astype(BF)
        for j in range(2):
            r = i * 2 + j
            x = a[j * C : (j + 1) * C]
            if r < 2 or r >= R - 4:
                edge[pl.ds((r if r < 2 else r - R + 6) * C, C), :] = x
            for d, y in enumerate(shifted(x, WX)):
                a3[pl.ds((r * 3 + d) * C, C), :] = y[:, 0:W]
    for i in range(PAIRS - 1):
        y = jnp.dot(wts[:, TAPS : 2 * TAPS], a3[pl.ds(i * 6 * C, 12 * C), :], preferred_element_type=F32)
        y = y + xs[pl.ds((i + 1) * 2 * C, 2 * C), :].astype(F32) + bias[:, LT : LT + 1]
        zi[pl.ds(i * 2 * C, 2 * C), :] = y.astype(BF)


def inner_rows(hid, cond, halo, xs, wts, bias):
    return pl.pallas_call(
        inner_kernel,
        out_shape=(kept(((R - 4) * C, W)), kept((4 * C, WX))),
        in_specs=vmem(6),
        out_specs=tuple(vmem(2)),
        scratch_shapes=[
            pltpu.VMEM((R * 3 * CP, WX), BF),
            pltpu.VMEM((R * 3 * C, 3 * LT), BF),
            pltpu.VMEM(((R - 2) * 3 * C, W), BF),
        ],
        compiler_params=params(20),
        cost_estimate=pl.CostEstimate(flops=4 * 10**9, bytes_accessed=12 * 10**6, transcendentals=10**6),
    )(*in_vmem(hid, cond, halo, xs, wts, bias))


def outer_kernel(
    zi, edge, top, bottom, above, below, xs, wts, bias, out, n3, c3, a3, z, buf, sems
):
    lat = lax.axis_index("lat")
    first = jnp.where(lat == 0, 0.0, 1.0)
    last = jnp.where(lat == lax.axis_size("lat") - 1, 0.0, 1.0)

    def put(row, x):
        for d, y in enumerate(shifted(x, WX)):
            a3[pl.ds((row * 3 + d) * C, C), :] = y[:, 0:W]

    for r in range(4):
        put(2 + r, edge[pl.ds(r * C, C), :])
    for part, (lo, hi) in enumerate(((above, top), (bottom, below))):
        for r, ref in enumerate((lo, lo, hi, hi)):
            n = part * 4 + r
            for d, y in enumerate(shifted(ref[pl.ds(r % 2 * C, C), :], WX)):
                n3[pl.ds((n * 3 + d) * C, C), :] = y
            for d, y in enumerate(shifted(ref[pl.ds(2 * C + r % 2 * CP, CP), :], WX)):
                c3[pl.ds((n * 3 + d) * CP, CP), :] = y
    for part in range(2):
        v = jnp.dot(wts[:, 0:TAPS], n3[pl.ds(part * 12 * C, 12 * C), :], preferred_element_type=F32)
        v = v + jnp.dot(wts[:, 2 * TAPS :], c3[pl.ds(part * 12 * CP, 12 * CP), :], preferred_element_type=F32)
        v = silu(v + bias[:, 0:1])
        if part == 0:
            put(0, (v[0:C] * first).astype(BF))
            put(1, v[C:].astype(BF))
        else:
            put(6, v[0:C].astype(BF))
            put(7, (v[C:] * last).astype(BF))
    for part, r0 in ((0, 0), (1, R - 2)):
        at = pl.ds(r0 * C, 2 * C)
        y = jnp.dot(
            wts[:, TAPS : 2 * TAPS], a3[pl.ds(part * 12 * C, 12 * C), :], preferred_element_type=F32
        )
        z[pl.ds(part * 2 * C, 2 * C), :] = (y + xs[at, :].astype(F32) + bias[:, LT : LT + 1]).astype(BF)
    copies = []
    each = C // PARTS
    for g in range(PARTS):
        rows = [z[pl.ds(r * C + g * each, each), :] for r in range(2)]
        rows += [zi[pl.ds(r * C + g * each, each), :] for r in range(R - 4)]
        rows += [z[pl.ds(r * C + g * each, each), :] for r in range(2, 4)]
        part = pl.ds(g * each, each)
        buf[part] = jnp.swapaxes(jnp.stack(rows, axis=0), 0, 1)
        copies.append(load(buf.at[part], out.at[part], sems.at[g]))
    for copy in copies:
        copy.wait()


def outer_rows(zi, edge, top, bottom, above, below, xs, wts, bias):
    return pl.pallas_call(
        outer_kernel,
        out_shape=pltpu.HBM((C, R, W), BF),
        in_specs=vmem(9),
        out_specs=hbm(1)[0],
        scratch_shapes=[
            pltpu.VMEM((24 * C, WX), BF),
            pltpu.VMEM((24 * CP, WX), BF),
            pltpu.VMEM((24 * C, W), BF),
            pltpu.VMEM((4 * C, W), BF),
            pltpu.VMEM((C, R, W), BF),
            pltpu.SemaphoreType.DMA((PARTS,)),
        ],
        compiler_params=params(22),
    )(*in_vmem(zi, edge), top, bottom, above, below, *in_vmem(xs, wts, bias))


def local(noisy, coarse, owner, slot, weight, counts, table, conv_in, conv_cond, bias_in, conv_out, bias_out):
    coarse = jnp.transpose(coarse, (0, 2, 1, 3))
    conv_cond = jnp.transpose(conv_cond, (0, 1, 3, 2))
    table = table.reshape(KINDS * LT, table.shape[2])
    msg = message(noisy, coarse, owner, slot, weight, counts)
    got = lax.all_to_all(msg, "lon", split_axis=0, concat_axis=0, tiled=True)
    xs, hid, wts, bias = own_tile(noisy, conv_in, conv_cond, conv_out, bias_in[None], bias_out[None])
    cond, halo, top, bottom = cond_tile(got, table, xs)
    count = lax.axis_size("lat")
    above = lax.ppermute(bottom, "lat", [(i, i + 1) for i in range(count - 1)])
    below = lax.ppermute(top, "lat", [(i + 1, i) for i in range(count - 1)])
    zi, edge = inner_rows(hid, cond, halo, xs, wts, bias)
    return outer_rows(zi, edge, top, bottom, above, below, xs, wts, bias)


def solution(mesh):
    grid = P("lat", "lon")
    in_specs = (P(None, "lat", "lon"),) + (grid,) * 5 + (P(),) * 6
    return jax.shard_map(local, mesh=mesh, in_specs=in_specs, out_specs=P(None, "lat", "lon"), check_vma=False)
```

time: 62.2 us -> 43.7 us (0.70)
  local copies, waits for them, and re-layouts: 24.3 us -> 2.24 us
  waiting for transfers between devices: 1.23 us -> 4.24 us
  Pallas kernels: 19.7 us -> 20.8 us
    unnamed x58 -> x8, local copies, waits for them, and re-layouts: 24.1 us -> 2.24 us
    ppermute x1, starting transfers between devices: 5.27 us -> 3.2 us  [local(): above = lax.ppermute(bottom, 'lat', [(i, i + 1) for i in range(count - 1)])]
    ppermute x1, starting transfers between devices: 2.1 us -> 4.02 us  [local(): below = lax.ppermute(top, 'lat', [(i + 1, i) for i in range(count - 1)])]
    all_to_all x1, waiting for transfers between devices: 1.22 us -> 2.93 us  [local(): got = lax.all_to_all(msg, 'lon', split_axis=0, concat_axis=0, tiled=True)]
    ppermute x1, waiting for transfers between devices: 0.01 us -> 1.18 us  [local(): above = lax.ppermute(bottom, 'lat', [(i, i + 1) for i in range(count - 1)])]
    pallas_call x4, Pallas kernels: 17.8 us -> 18.6 us  [the longest x1 5.89 us: own_tile(): pl.pallas_call(own_kernel, out_shape=(kept((R * C, W)), kept((PAIRS, 2 *...]
  transfers between devices with their start and end apart: 3 -> 3, of which waited for: 1 -> 3; matrix products, arithmetic and copies ran while one was open for 2% -> 0% of each run, Pallas kernels for 10% -> 25%
where the time goes in v2:
time: 43.7 us; the launch traced here: 43.3 us
  Pallas kernels  20.8 us (48%)
  starting transfers between devices  15.8 us (36%)
  waiting for transfers between devices  4.24 us (10%)
  local copies, waits for them, and re-layouts  2.24 us (5%)
    all_to_all x1, starting transfers between devices, local(): got = lax.all_to_all(msg, 'lon', split_axis=0, concat_axis=0, tiled=True)  8.6 us
    pallas_call x1, Pallas kernels, own_tile(): pl.pallas_call(own_kernel, out_shape=(kept((R * C, W)), kept((PAIRS, 2 *...  5.89 us
    pallas_call x1, Pallas kernels, inner_rows(): pl.pallas_call(inner_kernel, out_shape=(kept(((R - 4) * C, W)), kept((4 *...  4.76 us
    pallas_call x1, Pallas kernels, outer_rows(): pl.pallas_call(outer_kernel, out_shape=pltpu.HBM((C, R, W), BF), in_specs...  4.57 us
    ppermute x1, starting transfers between devices, local(): below = lax.ppermute(top, 'lat', [(i + 1, i) for i in range(count - 1)])  4.02 us
    pallas_call x1, Pallas kernels, cond_tile(): pl.pallas_call(cond_kernel, out_shape=(kept((R * CP, WX)), kept((R * C, L...  3.36 us
    ppermute x1, starting transfers between devices, local(): above = lax.ppermute(bottom, 'lat', [(i, i + 1) for i in range(count - 1)])  3.2 us
    all_to_all x1, waiting for transfers between devices, local(): got = lax.all_to_all(msg, 'lon', split_axis=0, concat_axis=0, tiled=True)  2.93 us
  transfers between devices with their start and end apart: 3, of which 3 were waited for; matrix products, arithmetic and copies ran while one was open for 0% of the time, Pallas kernels for 25%

profile of v2, /device:TPU:1, one launch (start us, length us, event | category | flops | bytes accessed | tf_op | source)
XLA Modules:
  0.0 43.3 jit_solution(3667575492595232268)
XLA Ops:
  0.0 2.2 %shard_map.119 = bf16[16,144,128]{2,1,0:T(8,128)(2,1)} custom-call(bf16[64,16,1280]{2,1,0:T(8,128)(2,1)} %last.1, bf16[64,16,1280]{2,1,0:T(8,128)(2,1)} %last.1, bf16[1,30,4,128]{3,2,1,0:T(4,128)(2,1)} %bitcast.6, s32[1,1,4,4]{3,2,1,0:T(4,128)} %owner.1, s32[1,1,4,4]{3,2,1,0:T(4,128)} %slot.1, s32[1,1,4,4]{3,2,1,0:T(4,128)} %weight.1, s32[1,1,4]{2,1,0:T(1,128)} %counts.1), custom_call_target="tpu_custom_call" | custom-call | tf_op jit(solution)/shard_map/pallas_call | solution.py:104
  2.2 8.6 %all-to-all-start = ((bf16[16,144,128]{2,1,0:T(8,128)(2,1)}), bf16[16,144,128]{2,1,0:T(8,128)(2,1)S(1)}, u32[]{:S(2)}, u32[]{:S(2)}) async-start(bf16[16,144,128]{2,1,0:T(8,128)(2,1)} %shard_map.119), calls=%async_computation | async-start | bytes 1179648 | tf_op jit(solution)/shard_map/all_to_all | solution.py:393
  10.8 5.9 %shard_map.118 = (bf16[1024,1280]{1,0:T(8,128)(2,1)S(1)}, bf16[7,128,1408]{2,1,0:T(8,128)(2,1)S(1)}, bf16[128,1920]{1,0:T(8,128)(2,1)S(1)}, f32[128,256]{1,0:T(8,128)S(1)}) custom-call(bf16[64,16,1280]{2,1,0:T(8,128)(2,1)} %last.1, bf16[3,3,64,64]{3,2,1,0:T(8,128)(2,1)} %conv_in.1, bf16[3,3,30,64]{3,2,1,0:T(8,128)(2,1)} %bitcast.7, ...), custom_call_target="tpu_custom_call" | custom-call | flops 3000000000 | bytes 12000000 | tf_op jit(solution)/shard_map/pallas_call | solution.py:173
  16.7 0.0 copy-start
  16.8 0.8 %copy-done = bf16[128,1920]{1,0:T(8,128)(2,1)} copy-done((bf16[128,1920]{1,0:T(8,128)(2,1)}, bf16[128,1920]{1,0:T(8,128)(2,1)S(1)}, u32[]{:S(2)}) %copy-start) | copy-done | bytes 491544
  17.5 0.0 copy-start.2
  17.5 1.5 %copy-done.2 = bf16[7,128,1408]{2,1,0:T(8,128)(2,1)} copy-done((bf16[7,128,1408]{2,1,0:T(8,128)(2,1)}, bf16[7,128,1408]{2,1,0:T(8,128)(2,1)S(1)}, u32[]{:S(2)}) %copy-start.2) | copy-done | bytes 2523160
  19.0 2.9 %all-to-all-done.got = bf16[16,144,128]{2,1,0:T(8,128)(2,1)S(1)} async-done(((bf16[16,144,128]{2,1,0:T(8,128)(2,1)}), bf16[16,144,128]{2,1,0:T(8,128)(2,1)S(1)}, u32[]{:S(2)}, u32[]{:S(2)}) %all-to-all-start) | async-done | bytes 589856 | tf_op jit(solution)/shard_map/all_to_all | solution.py:393
  21.9 0.0 copy-start.1
  21.9 0.0 copy-start.3
  21.9 3.4 %shard_map.120 = (bf16[512,1408]{1,0:T(8,128)(2,1)S(1)}, bf16[1024,128]{1,0:T(8,128)(2,1)S(1)}, bf16[192,1408]{1,0:T(8,128)(2,1)S(1)}, bf16[192,1408]{1,0:T(8,128)(2,1)S(1)}) custom-call(bf16[16,144,128]{2,1,0:T(8,128)(2,1)S(1)} %all-to-all-done.got, bf16[512,5120]{1,0:T(8,128)(2,1)} %bitcast.5, bf16[1024,1280]{1,0:T(8,128)(2,1)S(1)} %get-tuple-element.16.xs), custom_call_target="tpu_custom_call" | custom-call | tf_op jit(solution)/shard_map/pallas_call | solution.py:254
  25.3 4.0 %collective-permute-start.1 = (bf16[192,1408]{1,0:T(8,128)(2,1)S(1)}, bf16[192,1408]{1,0:T(8,128)(2,1)S(1)}, u32[]{:S(2)}, u32[]{:S(2)}) collective-permute-start(bf16[192,1408]{1,0:T(8,128)(2,1)S(1)} %get-tuple-element.23.top), channel_id=1, source_target_pairs={{16,0},{32,16},{48,32},{64,48},{80,64},{96,80},{112,96},{17,1},{33... | collective-permute-start | bytes 1622024 | tf_op jit(solution)/shard_map/ppermute | solution.py:398
  29.3 3.2 %collective-permute-start = (bf16[192,1408]{1,0:T(8,128)(2,1)S(1)}, bf16[192,1408]{1,0:T(8,128)(2,1)S(1)}, u32[]{:S(2)}, u32[]{:S(2)}) collective-permute-start(bf16[192,1408]{1,0:T(8,128)(2,1)S(1)} %get-tuple-element.24.bottom), channel_id=1, source_target_pairs={{0,16},{16,32},{32,48},{48,64},{64,80},{80,96},{96,112},{1,17},{17... | collective-permute-start | bytes 1622024 | tf_op jit(solution)/shard_map/ppermute | solution.py:397
  32.5 0.0 copy-done.1
  32.5 0.0 copy-done.3
  32.5 4.8 %shard_map.121 = (bf16[768,1280]{1,0:T(8,128)(2,1)S(1)}, bf16[256,1408]{1,0:T(8,128)(2,1)S(1)}) custom-call(bf16[7,128,1408]{2,1,0:T(8,128)(2,1)S(1)} %copy-done.3, bf16[512,1408]{1,0:T(8,128)(2,1)S(1)} %get-tuple-element.17.cond, bf16[1024,128]{1,0:T(8,128)(2,1)S(1)} %get-tuple-element.18.halo, bf16[1024,1280]{1,0:T(8,128)(2,1)S(1)} %get-tuple-element.16.xs, ...), custom_call_target="tpu_custom_call" | custom-call | flops 4000000000 | bytes 12000000 | tf_op jit(solution)/shard_map/pallas_call | solution.py:306
  37.3 0.1 collective-permute-done.1.below
  37.4 1.2 %collective-permute-done.above = bf16[192,1408]{1,0:T(8,128)(2,1)S(1)} collective-permute-done((bf16[192,1408]{1,0:T(8,128)(2,1)S(1)}, bf16[192,1408]{1,0:T(8,128)(2,1)S(1)}, u32[]{:S(2)}, u32[]{:S(2)}) %collective-permute-start) | collective-permute-done | bytes 540704 | tf_op jit(solution)/shard_map/ppermute | solution.py:397
  38.6 4.6 %shard_map.122 = bf16[64,16,1280]{2,1,0:T(8,128)(2,1)} custom-call(bf16[768,1280]{1,0:T(8,128)(2,1)S(1)} %get-tuple-element.21.zi, bf16[256,1408]{1,0:T(8,128)(2,1)S(1)} %get-tuple-element.22.edge, bf16[192,1408]{1,0:T(8,128)(2,1)S(1)} %get-tuple-element.23.top, bf16[192,1408]{1,0:T(8,128)(2,1)S(1)} %get-tuple-element.24.bottom, ...), custom_call_target="tpu_custom_call" | custom-call | tf_op jit(solution)/shard_map/pallas_call | solution.py:371
Async XLA Ops:
  2.2 19.7 %all-to-all-start = ((bf16[16,144,128]{2,1,0:T(8,128)(2,1)}), bf16[16,144,128]{2,1,0:T(8,128)(2,1)S(1)}, u32[]{:S(2)}, u32[]{:S(2)}) async-start(bf16[16,144,128]{2,1,0:T(8,128)(2,1)} %shard_map.119), calls=%async_computation | async-start | bytes 1179648 | tf_op jit(solution)/shard_map/all_to_all | solution.py:393
  16.7 0.8 %copy-start = (bf16[128,1920]{1,0:T(8,128)(2,1)}, bf16[128,1920]{1,0:T(8,128)(2,1)S(1)}, u32[]{:S(2)}) copy-start(bf16[128,1920]{1,0:T(8,128)(2,1)S(1)} %get-tuple-element.19.wts) | copy-start | bytes 1474564
  17.5 1.5 %copy-start.2 = (bf16[7,128,1408]{2,1,0:T(8,128)(2,1)}, bf16[7,128,1408]{2,1,0:T(8,128)(2,1)S(1)}, u32[]{:S(2)}) copy-start(bf16[7,128,1408]{2,1,0:T(8,128)(2,1)S(1)} %get-tuple-element.15.hid) | copy-start | bytes 7569412
  21.9 10.6 %copy-start.1 = (bf16[128,1920]{1,0:T(8,128)(2,1)S(1)}, bf16[128,1920]{1,0:T(8,128)(2,1)}, u32[]{:S(2)}) copy-start(bf16[128,1920]{1,0:T(8,128)(2,1)} %copy-done) | copy-start | bytes 1474564
  21.9 10.6 %copy-start.3 = (bf16[7,128,1408]{2,1,0:T(8,128)(2,1)S(1)}, bf16[7,128,1408]{2,1,0:T(8,128)(2,1)}, u32[]{:S(2)}) copy-start(bf16[7,128,1408]{2,1,0:T(8,128)(2,1)} %copy-done.2) | copy-start | bytes 7569412
  25.3 12.2 %collective-permute-start.1 = (bf16[192,1408]{1,0:T(8,128)(2,1)S(1)}, bf16[192,1408]{1,0:T(8,128)(2,1)S(1)}, u32[]{:S(2)}, u32[]{:S(2)}) collective-permute-start(bf16[192,1408]{1,0:T(8,128)(2,1)S(1)} %get-tuple-element.23.top), channel_id=1, source_target_pairs={{16,0},{32,16},{48,32},{64,48},{80,64},{96,80},{112,96},{17,1},{33... | collective-permute-start | bytes 1622024 | tf_op jit(solution)/shard_map/ppermute | solution.py:398
  29.3 9.3 %collective-permute-start = (bf16[192,1408]{1,0:T(8,128)(2,1)S(1)}, bf16[192,1408]{1,0:T(8,128)(2,1)S(1)}, u32[]{:S(2)}, u32[]{:S(2)}) collective-permute-start(bf16[192,1408]{1,0:T(8,128)(2,1)S(1)} %get-tuple-element.24.bottom), channel_id=1, source_target_pairs={{0,16},{16,32},{32,48},{48,64},{64,80},{80,96},{96,112},{1,17},{17... | collective-permute-start | bytes 1622024 | tf_op jit(solution)/shard_map/ppermute | solution.py:397

commit v3 on v2

v3 whole, which is shorter than its diff:
```python
import jax
import jax.numpy as jnp
from jax import lax
from jax.experimental import pallas as pl
from jax.experimental.pallas import tpu as pltpu
from jax.sharding import PartitionSpec as P

BF = jnp.bfloat16
F32 = jnp.float32
MIB = 1024 * 1024

C = 64
CP = 32
R = 16
W = 1280
LT = 128
WX = W + LT
PEERS = 16
HELD = 4
SUBS = 4
SLOTS = 4
KINDS = 4
EDGE = 16
MSG = HELD * CP + EDGE
PAIRS = R // 2 - 1
TAP = 3 * (C + CP)
TAPS = 4 * TAP
TAPS_OUT = 12 * C
PARTS = 4


def vmem(n=1):
    return [pl.BlockSpec(memory_space=pltpu.VMEM)] * n


def smem(n=1):
    return [pl.BlockSpec(memory_space=pltpu.SMEM)] * n


def params(mib):
    return pltpu.CompilerParams(vmem_limit_bytes=mib * MIB)


def struct(shape, dtype=BF):
    return jax.ShapeDtypeStruct(shape, dtype)


def kept(shape, dtype=BF):
    return pltpu.VMEM(shape, dtype)


def hbm(n=1):
    return [pl.BlockSpec(memory_space=pltpu.HBM)] * n


def in_hbm(*arrays):
    return [pltpu.with_memory_space_constraint(a, pltpu.HBM) for a in arrays]


def in_vmem(*arrays):
    return [pltpu.with_memory_space_constraint(a, pltpu.VMEM) for a in arrays]


def iota(shape, dim):
    return lax.broadcasted_iota(jnp.int32, shape, dim)


def message_kernel(noisy, coarse_hbm, ids, out, tiles, coarse, owner, slot, weight, counts, sems):
    me = lax.axis_index("lon")
    loads = [
        load(noisy.at[:, :, 0:LT], tiles.at[0], sems.at[0]),
        load(noisy.at[:, :, W - LT : W], tiles.at[1], sems.at[1]),
        load(coarse_hbm, coarse, sems.at[2]),
    ]
    loads += [load(a, b, sems.at[3 + i]) for i, (a, b) in enumerate(zip(ids, (owner, slot, weight, counts)))]
    for copy in loads:
        copy.wait()
    lane = iota((C, R, LT), 2)
    edge = jnp.where(lane < 64, tiles[0].astype(F32), tiles[1].astype(F32))
    edge = jnp.swapaxes(edge.astype(BF), 0, 1)
    edge = jnp.concatenate([edge[r] for r in range(R)], axis=1)
    row = iota((R * LT, LT), 0)
    col = iota((R * LT, LT), 1)
    at = row % LT
    kind = jnp.where(at < 64, at, at - 124)
    wanted = ((at < 2) | (at >= 126)) & (col == kind * R + row // LT)
    pick = jnp.where(wanted, 1.0, 0.0).astype(BF)
    packed = jnp.dot(edge, pick, preferred_element_type=F32)
    sides = []
    for side in range(2):
        parts = [packed[g * EDGE : (g + 1) * EDGE, side * 32 : side * 32 + 32] for g in range(C // EDGE)]
        sides.append(jnp.concatenate(parts, axis=1))
    lanes = iota((2, HELD, LT), 2)
    lists = jnp.zeros((2, HELD, LT), F32)
    for s in range(SUBS):
        live = counts[0, 0, s]
        for k in range(SLOTS):
            n = s * SLOTS + k
            block = owner[0, 0, s, k] * HELD + slot[0, 0, s, k]
            kind_id = jnp.where(k < live, weight[0, 0, s, k], KINDS)
            lists = jnp.where(lanes == n, block.astype(F32), lists)
            lists = jnp.where(lanes == 16 + n, kind_id.astype(F32), lists)
    chans = coarse[0].astype(F32)
    blocks = jnp.swapaxes(jnp.concatenate([chans, lists], axis=0), 0, 1)
    blocks = blocks.reshape(HELD * CP, LT).astype(BF)
    right = lax.rem(me + 1, PEERS)
    for p in range(PEERS):
        out[p, 0 : HELD * CP] = blocks
        out[p, HELD * CP :] = jnp.where(right == p, sides[1], sides[0]).astype(BF)


def message(noisy, coarse, *ids):
    def kernel(noisy_ref, coarse_ref, owner, slot, weight, counts, *rest):
        message_kernel(noisy_ref, coarse_ref, (owner, slot, weight, counts), *rest)

    return pl.pallas_call(
        kernel,
        out_shape=kept((PEERS, MSG, LT)),
        in_specs=hbm(6),
        out_specs=vmem()[0],
        scratch_shapes=[pltpu.VMEM((2, C, R, LT), BF), pltpu.VMEM(coarse.shape, BF)]
        + [pltpu.SMEM(a.shape, jnp.int32) for a in ids]
        + [pltpu.SemaphoreType.DMA((7,))],
        compiler_params=params(12),
    )(*in_hbm(noisy, coarse, *ids))


def load(src, dst, sem):
    copy = pltpu.make_async_copy(src, dst, sem)
    copy.start()
    return copy


def shifted(x, width):
    return [pltpu.roll(x, 1, 1), x, pltpu.roll(x, width - 1, 1)]


def pair_weights(taps):
    rows = jnp.concatenate(taps, axis=1)
    blank = jnp.zeros((rows.shape[0], rows.shape[1] // 3), BF)
    return jnp.concatenate(
        [jnp.concatenate([rows, blank], axis=1), jnp.concatenate([blank, rows], axis=1)], axis=0
    )


def cond_tap(tap):
    tap = jnp.concatenate([tap.astype(F32), jnp.zeros((CP - tap.shape[0], tap.shape[1]), F32)], axis=0)
    return tap.T.astype(BF)


def bias_column(row):
    same = iota((C, C), 0) == iota((C, C), 1)
    column = jnp.sum(jnp.where(same, row, 0.0), axis=1, keepdims=True)
    return jnp.concatenate([column, column], axis=0)


def near_rows():
    odd = lax.rem(lax.axis_index("lat"), 2)
    return (1 - odd) * (R - 2), odd * (R - 2)


def turn_kernel(
    noisy, conv_in, conv_cond, conv_out, bias_in, bias_out, xs, first, second, wts_hbm, bias_hbm, buf, wts, bias, sems
):
    loads = []
    for g in range(PARTS):
        part = pl.ds(g * (C // PARTS), C // PARTS)
        loads.append(load(noisy.at[part], buf.at[part], sems.at[g]))
    taps = []
    for i in range(3):
        taps += [conv_in[i, j] for j in range(3)] + [cond_tap(conv_cond[i, j]) for j in range(3)]
    wts[:, 0:TAPS] = pair_weights(taps)
    wts[:, TAPS:] = pair_weights([conv_out[i, j] for i in range(3) for j in range(3)])
    bias[:, 0:LT] = jnp.broadcast_to(bias_column(bias_in[...]), (2 * C, LT))
    bias[:, LT:] = jnp.broadcast_to(bias_column(bias_out[...]), (2 * C, LT))
    stores = [load(wts, wts_hbm, sems.at[PARTS]), load(bias, bias_hbm, sems.at[PARTS + 1])]
    for copy in loads:
        copy.wait()
    xs[...] = jnp.swapaxes(buf[...], 0, 1).reshape(R * C, W)
    for i, (out, r0) in enumerate(zip((first, second), near_rows())):
        rows = pl.ds(pl.multiple_of(r0 * C, C), 2 * C)
        stores.append(load(xs.at[rows], out, sems.at[PARTS + 2 + i]))
    for copy in stores:
        copy.wait()


def turned(noisy, conv_in, conv_cond, conv_out, bias_in, bias_out):
    return pl.pallas_call(
        turn_kernel,
        out_shape=(
            kept((R * C, W)),
            pltpu.HBM((2 * C, W), BF),
            pltpu.HBM((2 * C, W), BF),
            pltpu.HBM((2 * C, TAPS + TAPS_OUT), BF),
            pltpu.HBM((2 * C, 2 * LT), F32),
        ),
        in_specs=hbm(1) + vmem(5),
        out_specs=tuple(vmem(1) + hbm(4)),
        scratch_shapes=[
            pltpu.VMEM((C, R, W), BF),
            pltpu.VMEM((2 * C, TAPS + TAPS_OUT), BF),
            pltpu.VMEM((2 * C, 2 * LT), F32),
            pltpu.SemaphoreType.DMA((PARTS + 4,)),
        ],
        compiler_params=params(10),
        cost_estimate=pl.CostEstimate(flops=3 * 10**9, bytes_accessed=12 * 10**6, transcendentals=0),
    )(*in_hbm(noisy, conv_in, conv_cond, conv_out, bias_in, bias_out))


def cond_kernel(got, table_hbm, wts_hbm, bias_hbm, cond, halo, first, second, wts, bias, acc, grp, ints, lists, table, sem, sems):
    loads = []
    for r in range(R // SUBS):
        loads.append(load(table_hbm.at[:, pl.ds(r * W, W)], table.at[r], sems.at[r]))
    others = [load(wts_hbm, wts, sems.at[R // SUBS]), load(bias_hbm, bias, sems.at[R // SUBS + 1])]
    me = lax.axis_index("lon")
    left = lax.rem(me + PEERS - 1, PEERS)
    right = lax.rem(me + 1, PEERS)
    for d, p in enumerate((me, left, right)):
        ints[d] = got[p, CP - 16 : CP, :].astype(F32).astype(jnp.int32)
    copy = load(ints, lists, sem)
    acc[...] = jnp.zeros_like(acc)

    rows = []
    for g in range(C // EDGE):
        cols = slice(g * 32, g * 32 + 32)
        side = [got[p, HELD * CP :, cols].astype(F32) for p in (right, left)]
        rows.append(jnp.concatenate(side + [jnp.zeros((EDGE, 64), F32)], axis=1))
    both = jnp.concatenate(rows, axis=0).astype(BF)
    src = iota((LT, R * LT), 0)
    dst = iota((LT, R * LT), 1)
    at = dst % LT
    kind = jnp.where(at < 64, at, at - 124)
    wanted = ((at < 2) | (at >= 126)) & (src == kind * R + dst // LT)
    place = jnp.where(wanted, 1.0, 0.0).astype(BF)
    tiles = jnp.dot(both, place, preferred_element_type=F32).astype(BF)
    for r in range(R):
        halo[pl.ds(r * C, C), :] = tiles[:, r * LT : (r + 1) * LT]

    copy.wait()
    for d in range(3):
        for s in range(SUBS):
            for k in range(SLOTS):
                n = s * SLOTS + k
                block = lists[d, 14, n]
                part = got[block // HELD, pl.ds(pl.multiple_of(lax.rem(block, HELD) * CP, CP), CP), :]
                at = (d * SUBS + s) * (KINDS + 1) + lists[d, 14, 16 + n]
                acc[at] = acc[at] + part.astype(F32)
    for d in range(3):
        for s in range(SUBS):
            for w in range(KINDS):
                grp[d, pl.ds(s * CP, CP), w * LT : (w + 1) * LT] = acc[(d * SUBS + s) * (KINDS + 1) + w].astype(BF)

    lane = iota((SUBS * CP, LT), 1)
    for r in range(R // SUBS):
        loads[r].wait()
        part = table.at[r]
        own = jnp.dot(grp[0], part[...], preferred_element_type=F32).astype(BF)
        lhs = jnp.dot(grp[1], part[:, W - LT : W], preferred_element_type=F32)
        rhs = jnp.dot(grp[2], part[:, 0:LT], preferred_element_type=F32)
        side = jnp.where(lane < 2, rhs, jnp.where(lane >= 126, lhs, 0.0)).astype(BF)
        for s in range(SUBS):
            at = pl.ds((s * SUBS + r) * CP, CP)
            cond[at, 0:W] = own[s * CP : (s + 1) * CP]
            cond[at, W:WX] = side[s * CP : (s + 1) * CP]
    for out, r0 in zip((first, second), near_rows()):
        out[:, 0:WX] = cond[pl.ds(pl.multiple_of(r0 * CP, CP), 2 * CP), :]
        for j in range(2):
            out[:, WX + j * LT : WX + (j + 1) * LT] = halo[pl.ds(pl.multiple_of((r0 + j) * C, C), C), :]
    for copy in others:
        copy.wait()


def cond_tile(got, table, wts, bias):
    edge = struct((2 * CP, WX + 2 * LT))
    return pl.pallas_call(
        cond_kernel,
        out_shape=(
            kept((R * CP, WX)),
            kept((R * C, LT)),
            edge,
            edge,
            kept(wts.shape),
            kept(bias.shape, F32),
        ),
        in_specs=vmem(1) + hbm(3),
        out_specs=tuple(vmem(6)),
        scratch_shapes=[
            pltpu.VMEM((3 * SUBS * (KINDS + 1), CP, LT), F32),
            pltpu.VMEM((3, SUBS * CP, KINDS * LT), BF),
            pltpu.VMEM((3, 16, LT), jnp.int32),
            pltpu.SMEM((3, 16, LT), jnp.int32),
            pltpu.VMEM((R // SUBS, KINDS * LT, W), BF),
            pltpu.SemaphoreType.DMA,
            pltpu.SemaphoreType.DMA((R // SUBS + 2,)),
        ],
        compiler_params=params(14),
    )(*in_vmem(got), *in_hbm(table, wts, bias))


def silu(v):
    return v / (1.0 + jnp.exp(-v))


def put_taps(dst, row, noisy, cond):
    at = row * TAP
    for d, y in enumerate(shifted(noisy, WX)):
        dst[pl.ds(at + d * C, C), :] = y
    for d, y in enumerate(shifted(cond, WX)):
        dst[pl.ds(at + 3 * C + d * CP, CP), :] = y


def put_act(dst, row, x):
    for d, y in enumerate(shifted(x, WX)):
        dst[pl.ds((row * 3 + d) * C, C), :] = y[:, 0:W]


def own_row(xs, halo, r):
    return jnp.concatenate([xs[pl.ds(r * C, C), :], halo[pl.ds(r * C, C), :]], axis=1)


def first_conv(wts, bias, rows):
    return silu(jnp.dot(wts[:, 0:TAPS], rows, preferred_element_type=F32) + bias[:, 0:1])


def second_conv(wts, bias, rows, x):
    y = jnp.dot(wts[:, TAPS:], rows, preferred_element_type=F32)
    return (y + x.astype(F32) + bias[:, LT : LT + 1]).astype(BF)


def inner_kernel(cond, halo, xs, wts, bias, zi, edge, x3, a3):
    for r in range(R):
        put_taps(x3, r, own_row(xs, halo, r), cond[pl.ds(r * CP, CP), :])
    for i in range(PAIRS):
        a = first_conv(wts, bias, x3[pl.ds(2 * i * TAP, TAPS), :]).astype(BF)
        for j in range(2):
            r = i * 2 + j
            x = a[j * C : (j + 1) * C]
            if r < 2 or r >= R - 4:
                edge[pl.ds((r if r < 2 else r - R + 6) * C, C), :] = x
            put_act(a3, r, x)
    for i in range(PAIRS - 1):
        x = xs[pl.ds((i + 1) * 2 * C, 2 * C), :]
        zi[pl.ds(i * 2 * C, 2 * C), :] = second_conv(wts, bias, a3[pl.ds(i * 6 * C, TAPS_OUT), :], x)


def inner_rows(cond, halo, xs, wts, bias):
    return pl.pallas_call(
        inner_kernel,
        out_shape=(kept(((R - 4) * C, W)), kept((4 * C, WX))),
        in_specs=vmem(5),
        out_specs=tuple(vmem(2)),
        scratch_shapes=[
            pltpu.VMEM((R * TAP, WX), BF),
            pltpu.VMEM(((R - 2) * 3 * C, W), BF),
        ],
        compiler_params=params(26),
        cost_estimate=pl.CostEstimate(flops=6 * 10**9, bytes_accessed=12 * 10**6, transcendentals=10**6),
    )(*in_vmem(cond, halo, xs, wts, bias))


def outer_kernel(
    zi, edge, cond, halo, noisy_1, noisy_hbm, got_1, got_2, xs, wts, bias, out, x3, a3, buf, noisy_2, sems
):
    near = load(noisy_hbm, noisy_2, sems.at[2 * PARTS])
    lat = lax.axis_index("lat")
    first = jnp.where(lat == 0, 0.0, 1.0)
    last = jnp.where(lat == lax.axis_size("lat") - 1, 0.0, 1.0)
    half = R // 2
    each = C // PARTS
    copies = []
    odd = lax.rem(lat, 2) == 1
    for part in range(2):
        put_act(a3, part * 4 + 2 - part * 2, edge[pl.ds(part * 2 * C, C), :])
        put_act(a3, part * 4 + 3 - part * 2, edge[pl.ds((part * 2 + 1) * C, C), :])
        for j in range(2):
            r = part * (R - 2) + j
            put_taps(x3, part * 4 + 2 - part * 2 + j, own_row(xs, halo, r), cond[pl.ds(r * CP, CP), :])
    near.wait()
    for part in range(2):
        for j in range(2):
            mine = odd if part == 0 else ~odd
            n = jnp.where(mine, noisy_1[pl.ds(j * C, C), :], noisy_2[pl.ds(j * C, C), :])
            far = jnp.where(mine, got_1[...], got_2[...])
            n = jnp.concatenate([n, far[:, WX + j * LT : WX + (j + 1) * LT]], axis=1)
            put_taps(x3, part * 6 + j, n, far[j * CP : (j + 1) * CP, 0:WX])
        v = first_conv(wts, bias, x3[pl.ds(part * TAPS, TAPS), :])
        if part == 0:
            put_act(a3, 0, (v[0:C] * first).astype(BF))
            put_act(a3, 1, v[C:].astype(BF))
        else:
            put_act(a3, 6, v[0:C].astype(BF))
            put_act(a3, 7, (v[C:] * last).astype(BF))
        z = second_conv(wts, bias, a3[pl.ds(part * TAPS_OUT, TAPS_OUT), :], xs[pl.ds(part * (R - 2) * C, 2 * C), :])
        rows = [z[0:C], z[C:]]
        inner = [zi[pl.ds((part * (half - 2) + r) * C, C), :] for r in range(half - 2)]
        rows = inner + rows if part else rows + inner
        here = pl.ds(part * half, half)
        for g in range(PARTS):
            chans = pl.ds(g * each, each)
            group = jnp.stack([row[g * each : (g + 1) * each] for row in rows], axis=0)
            buf[chans, here, :] = jnp.swapaxes(group, 0, 1)
            sem = sems.at[part * PARTS + g]
            copies.append(load(buf.at[chans, here, :], out.at[chans, here, :], sem))
    for copy in copies:
        copy.wait()


def outer_rows(zi, edge, cond, halo, noisy_1, noisy_2, got_1, got_2, xs, wts, bias):
    return pl.pallas_call(
        outer_kernel,
        out_shape=pltpu.HBM((C, R, W), BF),
        in_specs=vmem(5) + hbm(1) + vmem(5),
        out_specs=hbm(1)[0],
        scratch_shapes=[
            pltpu.VMEM((2 * TAPS, WX), BF),
            pltpu.VMEM((2 * TAPS_OUT, W), BF),
            pltpu.VMEM((C, R, W), BF),
            pltpu.VMEM((2 * C, W), BF),
            pltpu.SemaphoreType.DMA((2 * PARTS + 1,)),
        ],
        compiler_params=params(24),
    )(*in_vmem(zi, edge, cond, halo), noisy_1, *in_hbm(noisy_2), got_1, got_2, *in_vmem(xs, wts, bias))


def exchanged(first, second):
    count = lax.axis_size("lat")
    got_1 = lax.ppermute(first, "lat", [(i, i ^ 1) for i in range(count)])
    got_2 = lax.ppermute(second, "lat", [(i, ((i + 1) ^ 1) - 1) for i in range(1, count - 1)])
    return got_1, got_2


def local(noisy, coarse, owner, slot, weight, counts, table, conv_in, conv_cond, bias_in, conv_out, bias_out):
    coarse = jnp.transpose(coarse, (0, 2, 1, 3))
    conv_cond = jnp.transpose(conv_cond, (0, 1, 3, 2))
    table = table.reshape(KINDS * LT, table.shape[2])
    msg = message(noisy, coarse, owner, slot, weight, counts)
    got = lax.all_to_all(msg, "lon", split_axis=0, concat_axis=0, tiled=True)
    xs, first, second, wts, bias = turned(noisy, conv_in, conv_cond, conv_out, bias_in[None], bias_out[None])
    noisy_1, noisy_2 = exchanged(first, second)
    cond, halo, first, second, wts, bias = cond_tile(got, table, wts, bias)
    got_1, got_2 = exchanged(first, second)
    zi, edge = inner_rows(cond, halo, xs, wts, bias)
    return outer_rows(zi, edge, cond, halo, noisy_1, noisy_2, got_1, got_2, xs, wts, bias)


def solution(mesh):
    grid = P("lat", "lon")
    in_specs = (P(None, "lat", "lon"),) + (grid,) * 5 + (P(),) * 6
    return jax.shard_map(local, mesh=mesh, in_specs=in_specs, out_specs=P(None, "lat", "lon"), check_vma=False)
```

time: 43.7 us -> 42.2 us (0.966)
  starting transfers between devices: 15.8 us -> 18.1 us
  local copies, waits for them, and re-layouts: 2.24 us -> 0 us
  waiting for transfers between devices: 4.24 us -> 2.4 us
    unnamed x8 -> x0, local copies, waits for them, and re-layouts: 2.24 us -> none
    ppermute x2 -> x4, starting transfers between devices: 7.22 us -> 9.45 us  [the longest x2 6.21 us: exchanged(): lax.ppermute(second, 'lat', [(i, (i + 1 ^ 1) - 1) for i in range(1, count...]
    ppermute x2 -> x4, waiting for transfers between devices: 1.31 us -> 0.01 us  [the longest x2 0.01 us: exchanged(): got_1 = lax.ppermute(first, 'lat', [(i, i ^ 1) for i in range(count)])]
    pallas_call x1, Pallas kernels: 4.76 us -> 6.03 us  [inner_rows(): pl.pallas_call(inner_kernel, out_shape=(kept(((R - 4) * C, W)), kept((4 *...]
    pallas_call x2, Pallas kernels: 8.13 us -> 6.93 us  [the longest x1 4.61 us: turned(): pl.pallas_call(turn_kernel, out_shape=(kept((R * C, W)), pltpu.HBM((2 * C...]
    all_to_all x1, waiting for transfers between devices: 2.93 us -> 2.39 us  [local(): got = lax.all_to_all(msg, 'lon', split_axis=0, concat_axis=0, tiled=True)]
  transfers between devices with their start and end apart: 3 -> 5, of which waited for: 3 -> 1; matrix products, arithmetic and copies ran while one was open for 0% -> 0% of each run, Pallas kernels for 25% -> 33%
where the time goes in v3:
time: 42.2 us; the launch traced here: 41.9 us
  Pallas kernels  21.2 us (50%)
  starting transfers between devices  18.1 us (43%)
  waiting for transfers between devices  2.4 us (6%)
    all_to_all x1, starting transfers between devices, local(): got = lax.all_to_all(msg, 'lon', split_axis=0, concat_axis=0, tiled=True)  8.61 us
    ppermute x2, starting transfers between devices, exchanged(): lax.ppermute(second, 'lat', [(i, (i + 1 ^ 1) - 1) for i in range(1, count...  6.21 us
    pallas_call x1, Pallas kernels, inner_rows(): pl.pallas_call(inner_kernel, out_shape=(kept(((R - 4) * C, W)), kept((4 *...  6.03 us
    pallas_call x1, Pallas kernels, outer_rows(): pl.pallas_call(outer_kernel, out_shape=pltpu.HBM((C, R, W), BF), in_specs...  4.9 us
    pallas_call x1, Pallas kernels, turned(): pl.pallas_call(turn_kernel, out_shape=(kept((R * C, W)), pltpu.HBM((2 * C...  4.61 us
    pallas_call x1, Pallas kernels, cond_tile(): pl.pallas_call(cond_kernel, out_shape=(kept((R * CP, WX)), kept((R * C, L...  3.3 us
    ppermute x2, starting transfers between devices, exchanged(): got_1 = lax.ppermute(first, 'lat', [(i, i ^ 1) for i in range(count)])  3.24 us
    all_to_all x1, waiting for transfers between devices, local(): got = lax.all_to_all(msg, 'lon', split_axis=0, concat_axis=0, tiled=True)  2.39 us
  transfers between devices with their start and end apart: 5, of which 1 were waited for; matrix products, arithmetic and copies ran while one was open for 0% of the time, Pallas kernels for 33%

profile of v3, /device:TPU:1, one launch (start us, length us, event | category | flops | bytes accessed | tf_op | source)
XLA Modules:
  0.0 41.9 jit_solution(4555272529878822477)
XLA Ops:
  0.0 2.3 %shard_map.118 = bf16[16,144,128]{2,1,0:T(8,128)(2,1)} custom-call(bf16[64,16,1280]{2,1,0:T(8,128)(2,1)} %noisy.1, bf16[1,30,4,128]{3,2,1,0:T(4,128)(2,1)} %bitcast.6, s32[1,1,4,4]{3,2,1,0:T(4,128)} %owner.1, s32[1,1,4,4]{3,2,1,0:T(4,128)} %slot.1, s32[1,1,4,4]{3,2,1,0:T(4,128)} %weight.1, s32[1,1,4]{2,1,0:T(1,128)} %counts.1), custom_call_target="tpu_custom_call" | custom-call | tf_op jit(solution)/shard_map/pallas_call | solution.py:116
  2.3 8.6 %all-to-all-start = ((bf16[16,144,128]{2,1,0:T(8,128)(2,1)}), bf16[16,144,128]{2,1,0:T(8,128)(2,1)S(1)}, u32[]{:S(2)}, u32[]{:S(2)}) async-start(bf16[16,144,128]{2,1,0:T(8,128)(2,1)} %shard_map.118), calls=%async_computation | async-start | bytes 1179648 | tf_op jit(solution)/shard_map/all_to_all | solution.py:437
  10.9 4.6 %shard_map.119 = (bf16[1024,1280]{1,0:T(8,128)(2,1)S(1)}, bf16[128,1280]{1,0:T(8,128)(2,1)}, bf16[128,1280]{1,0:T(8,128)(2,1)}, bf16[128,1920]{1,0:T(8,128)(2,1)}, f32[128,256]{1,0:T(8,128)}) custom-call(bf16[64,16,1280]{2,1,0:T(8,128)(2,1)} %noisy.1, bf16[3,3,64,64]{3,2,1,0:T(8,128)(2,1)} %conv_in.1, bf16[3,3,30,64]{3,2,1,0:T(8,128)(2,1)} %bitcast.7, ...), custom_call_target="tpu_custom_call" | custom-call | flops 3000000000 | bytes 12000000 | tf_op jit(solution)/shard_map/pallas_call | solution.py:188
  15.6 1.0 %collective-permute-start = (bf16[128,1280]{1,0:T(8,128)(2,1)}, bf16[128,1280]{1,0:T(8,128)(2,1)S(1)}, u32[]{:S(2)}, u32[]{:S(2)}) collective-permute-start(bf16[128,1280]{1,0:T(8,128)(2,1)} %get-tuple-element.27), channel_id=1, source_target_pairs={{0,16},{16,0},{32,48},{48,32},{64,80},{80,64},{96,112},{112,96},{1... | collective-permute-start | bytes 983048 | tf_op jit(solution)/shard_map/ppermute | solution.py:427
  16.6 3.0 %collective-permute-start.1 = (bf16[128,1280]{1,0:T(8,128)(2,1)}, bf16[128,1280]{1,0:T(8,128)(2,1)}, u32[]{:S(2)}, u32[]{:S(2)}) collective-permute-start(bf16[128,1280]{1,0:T(8,128)(2,1)} %get-tuple-element.28), channel_id=1, source_target_pairs={{16,32},{32,16},{48,64},{64,48},{80,96},{96,80},{17,33},{33,17},{4... | collective-permute-start | bytes 983048 | tf_op jit(solution)/shard_map/ppermute | solution.py:428
  19.6 2.4 %all-to-all-done.got = bf16[16,144,128]{2,1,0:T(8,128)(2,1)S(1)} async-done(((bf16[16,144,128]{2,1,0:T(8,128)(2,1)}), bf16[16,144,128]{2,1,0:T(8,128)(2,1)S(1)}, u32[]{:S(2)}, u32[]{:S(2)}) %all-to-all-start) | async-done | bytes 589856 | tf_op jit(solution)/shard_map/all_to_all | solution.py:437
  22.0 3.3 %shard_map.120 = (bf16[512,1408]{1,0:T(8,128)(2,1)S(1)}, bf16[1024,128]{1,0:T(8,128)(2,1)S(1)}, bf16[64,1664]{1,0:T(8,128)(2,1)S(1)}, bf16[64,1664]{1,0:T(8,128)...) custom-call(bf16[16,144,128]{2,1,0:T(8,128)(2,1)S(1)} %all-to-all-done.got, bf16[512,5120]{1,0:T(8,128)(2,1)} %bitcast.5, ...), custom_call_target="tpu_custom_call" | custom-call | tf_op jit(solution)/shard_map/pallas_call | solution.py:275
  25.3 2.2 %collective-permute-start.2 = (bf16[64,1664]{1,0:T(8,128)(2,1)S(1)}, bf16[64,1664]{1,0:T(8,128)(2,1)S(1)}, u32[]{:S(2)}, u32[]{:S(2)}) collective-permute-start(bf16[64,1664]{1,0:T(8,128)(2,1)S(1)} %get-tuple-element.29), channel_id=1, source_target_pairs={{0,16},{16,0},{32,48},{48,32},{64,80},{80,64},{96,112},{112,96},{1... | collective-permute-start | bytes 638984 | tf_op jit(solution)/shard_map/ppermute | solution.py:427
  27.5 3.2 %collective-permute-start.3 = (bf16[64,1664]{1,0:T(8,128)(2,1)S(1)}, bf16[64,1664]{1,0:T(8,128)(2,1)S(1)}, u32[]{:S(2)}, u32[]{:S(2)}) collective-permute-start(bf16[64,1664]{1,0:T(8,128)(2,1)S(1)} %get-tuple-element.30), channel_id=1, source_target_pairs={{16,32},{32,16},{48,64},{64,48},{80,96},{96,80},{17,33},{33,17},{4... | collective-permute-start | bytes 638984 | tf_op jit(solution)/shard_map/ppermute | solution.py:428
  30.7 6.0 %shard_map.121 = (bf16[768,1280]{1,0:T(8,128)(2,1)S(1)}, bf16[256,1408]{1,0:T(8,128)(2,1)S(1)}) custom-call(bf16[512,1408]{1,0:T(8,128)(2,1)S(1)} %get-tuple-element.20.cond, bf16[1024,128]{1,0:T(8,128)(2,1)S(1)} %get-tuple-element.21.halo, bf16[1024,1280]{1,0:T(8,128)(2,1)S(1)} %get-tuple-element.22.xs, bf16[128,1920]{1,0:T(8,128)(2,1)S(1)} %get-tuple-element.23.wts, ...), custom_call_target="tpu_custom_call" | custom-call | flops 6000000000 | bytes 12000000 | tf_op jit(solution)/shard_map/pallas_call | solution.py:347
  36.8 0.0 collective-permute-done.noisy_1
  36.8 0.0 collective-permute-done.1.noisy_hbm
  36.8 0.0 collective-permute-done.2.got_1
  36.8 0.0 collective-permute-done.3.got_2
  36.8 4.9 %shard_map.122 = bf16[64,16,1280]{2,1,0:T(8,128)(2,1)} custom-call(bf16[768,1280]{1,0:T(8,128)(2,1)S(1)} %get-tuple-element.25.zi, bf16[256,1408]{1,0:T(8,128)(2,1)S(1)} %get-tuple-element.26.edge, bf16[512,1408]{1,0:T(8,128)(2,1)S(1)} %get-tuple-element.20.cond, bf16[1024,128]{1,0:T(8,128)(2,1)S(1)} %get-tuple-element.21.halo, ...), custom_call_target="tpu_custom_call" | custom-call | tf_op jit(solution)/shard_map/pallas_call | solution.py:409
Async XLA Ops:
  2.3 19.7 %all-to-all-start = ((bf16[16,144,128]{2,1,0:T(8,128)(2,1)}), bf16[16,144,128]{2,1,0:T(8,128)(2,1)S(1)}, u32[]{:S(2)}, u32[]{:S(2)}) async-start(bf16[16,144,128]{2,1,0:T(8,128)(2,1)} %shard_map.118), calls=%async_computation | async-start | bytes 1179648 | tf_op jit(solution)/shard_map/all_to_all | solution.py:437
  15.6 21.2 %collective-permute-start = (bf16[128,1280]{1,0:T(8,128)(2,1)}, bf16[128,1280]{1,0:T(8,128)(2,1)S(1)}, u32[]{:S(2)}, u32[]{:S(2)}) collective-permute-start(bf16[128,1280]{1,0:T(8,128)(2,1)} %get-tuple-element.27), channel_id=1, source_target_pairs={{0,16},{16,0},{32,48},{48,32},{64,80},{80,64},{96,112},{112,96},{1... | collective-permute-start | bytes 983048 | tf_op jit(solution)/shard_map/ppermute | solution.py:427
  16.6 20.2 %collective-permute-start.1 = (bf16[128,1280]{1,0:T(8,128)(2,1)}, bf16[128,1280]{1,0:T(8,128)(2,1)}, u32[]{:S(2)}, u32[]{:S(2)}) collective-permute-start(bf16[128,1280]{1,0:T(8,128)(2,1)} %get-tuple-element.28), channel_id=1, source_target_pairs={{16,32},{32,16},{48,64},{64,48},{80,96},{96,80},{17,33},{33,17},{4... | collective-permute-start | bytes 983048 | tf_op jit(solution)/shard_map/ppermute | solution.py:428
  25.3 11.5 %collective-permute-start.2 = (bf16[64,1664]{1,0:T(8,128)(2,1)S(1)}, bf16[64,1664]{1,0:T(8,128)(2,1)S(1)}, u32[]{:S(2)}, u32[]{:S(2)}) collective-permute-start(bf16[64,1664]{1,0:T(8,128)(2,1)S(1)} %get-tuple-element.29), channel_id=1, source_target_pairs={{0,16},{16,0},{32,48},{48,32},{64,80},{80,64},{96,112},{112,96},{1... | collective-permute-start | bytes 638984 | tf_op jit(solution)/shard_map/ppermute | solution.py:427
  27.5 9.3 %collective-permute-start.3 = (bf16[64,1664]{1,0:T(8,128)(2,1)S(1)}, bf16[64,1664]{1,0:T(8,128)(2,1)S(1)}, u32[]{:S(2)}, u32[]{:S(2)}) collective-permute-start(bf16[64,1664]{1,0:T(8,128)(2,1)S(1)} %get-tuple-element.30), channel_id=1, source_target_pairs={{16,32},{32,16},{48,64},{64,48},{80,96},{96,80},{17,33},{33,17},{4... | collective-permute-start | bytes 638984 | tf_op jit(solution)/shard_map/ppermute | solution.py:428

commit v4 on v3

--- a/solution.py
+++ b/solution.py
@@ -160,12 +160,16 @@
 
 
 def turn_kernel(
-    noisy, conv_in, conv_cond, conv_out, bias_in, bias_out, xs, first, second, wts_hbm, bias_hbm, buf, wts, bias, sems
+    noisy, params_hbm, xs, first, second, wts_hbm, bias_hbm, buf, wts, bias, small, sems, small_sems
 ):
+    small_loads = [load(a, b, small_sems.at[i]) for i, (a, b) in enumerate(zip(params_hbm, small))]
+    conv_in, conv_cond, conv_out, bias_in, bias_out = small
     loads = []
     for g in range(PARTS):
         part = pl.ds(g * (C // PARTS), C // PARTS)
         loads.append(load(noisy.at[part], buf.at[part], sems.at[g]))
+    for copy in small_loads:
+        copy.wait()
     taps = []
     for i in range(3):
         taps += [conv_in[i, j] for j in range(3)] + [cond_tap(conv_cond[i, j]) for j in range(3)]
@@ -184,9 +188,17 @@
         copy.wait()
 
 
-def turned(noisy, conv_in, conv_cond, conv_out, bias_in, bias_out):
+def turned(noisy, *small):
+    count = len(small)
+
+    def kernel(noisy_ref, *refs):
+        scratch = refs[count + 5 :]
+        turn_kernel(
+            noisy_ref, refs[:count], *refs[count : count + 5], *scratch[:3], scratch[3 : 3 + count], *scratch[3 + count :]
+        )
+
     return pl.pallas_call(
-        turn_kernel,
+        kernel,
         out_shape=(
             kept((R * C, W)),
             pltpu.HBM((2 * C, W), BF),
@@ -194,17 +206,18 @@
             pltpu.HBM((2 * C, TAPS + TAPS_OUT), BF),
             pltpu.HBM((2 * C, 2 * LT), F32),
         ),
-        in_specs=hbm(1) + vmem(5),
+        in_specs=hbm(1 + count),
         out_specs=tuple(vmem(1) + hbm(4)),
         scratch_shapes=[
             pltpu.VMEM((C, R, W), BF),
             pltpu.VMEM((2 * C, TAPS + TAPS_OUT), BF),
             pltpu.VMEM((2 * C, 2 * LT), F32),
-            pltpu.SemaphoreType.DMA((PARTS + 4,)),
-        ],
+        ]
+        + [pltpu.VMEM(a.shape, a.dtype) for a in small]
+        + [pltpu.SemaphoreType.DMA((PARTS + 4,)), pltpu.SemaphoreType.DMA((count,))],
         compiler_params=params(10),
         cost_estimate=pl.CostEstimate(flops=3 * 10**9, bytes_accessed=12 * 10**6, transcendentals=0),
-    )(*in_hbm(noisy, conv_in, conv_cond, conv_out, bias_in, bias_out))
+    )(*in_hbm(noisy, *small))
 
 
 def cond_kernel(got, table_hbm, wts_hbm, bias_hbm, cond, halo, first, second, wts, bias, acc, grp, ints, lists, table, sem, sems):
@@ -361,48 +374,48 @@
 def outer_kernel(
     zi, edge, cond, halo, noisy_1, noisy_hbm, got_1, got_2, xs, wts, bias, out, x3, a3, buf, noisy_2, sems
 ):
-    near = load(noisy_hbm, noisy_2, sems.at[2 * PARTS])
     lat = lax.axis_index("lat")
-    first = jnp.where(lat == 0, 0.0, 1.0)
-    last = jnp.where(lat == lax.axis_size("lat") - 1, 0.0, 1.0)
     half = R // 2
     each = C // PARTS
-    copies = []
-    odd = lax.rem(lat, 2) == 1
-    for part in range(2):
-        put_act(a3, part * 4 + 2 - part * 2, edge[pl.ds(part * 2 * C, C), :])
-        put_act(a3, part * 4 + 3 - part * 2, edge[pl.ds((part * 2 + 1) * C, C), :])
-        for j in range(2):
-            r = part * (R - 2) + j
-            put_taps(x3, part * 4 + 2 - part * 2 + j, own_row(xs, halo, r), cond[pl.ds(r * CP, CP), :])
-    near.wait()
-    for part in range(2):
-        for j in range(2):
-            mine = odd if part == 0 else ~odd
-            n = jnp.where(mine, noisy_1[pl.ds(j * C, C), :], noisy_2[pl.ds(j * C, C), :])
-            far = jnp.where(mine, got_1[...], got_2[...])
-            n = jnp.concatenate([n, far[:, WX + j * LT : WX + (j + 1) * LT]], axis=1)
-            put_taps(x3, part * 6 + j, n, far[j * CP : (j + 1) * CP, 0:WX])
-        v = first_conv(wts, bias, x3[pl.ds(part * TAPS, TAPS), :])
-        if part == 0:
-            put_act(a3, 0, (v[0:C] * first).astype(BF))
-            put_act(a3, 1, v[C:].astype(BF))
-        else:
-            put_act(a3, 6, v[0:C].astype(BF))
-            put_act(a3, 7, (v[C:] * last).astype(BF))
-        z = second_conv(wts, bias, a3[pl.ds(part * TAPS_OUT, TAPS_OUT), :], xs[pl.ds(part * (R - 2) * C, 2 * C), :])
-        rows = [z[0:C], z[C:]]
-        inner = [zi[pl.ds((part * (half - 2) + r) * C, C), :] for r in range(half - 2)]
-        rows = inner + rows if part else rows + inner
-        here = pl.ds(part * half, half)
-        for g in range(PARTS):
-            chans = pl.ds(g * each, each)
-            group = jnp.stack([row[g * each : (g + 1) * each] for row in rows], axis=0)
-            buf[chans, here, :] = jnp.swapaxes(group, 0, 1)
-            sem = sems.at[part * PARTS + g]
-            copies.append(load(buf.at[chans, here, :], out.at[chans, here, :], sem))
-    for copy in copies:
-        copy.wait()
+    upper = jnp.where(lat == 0, 0.0, 1.0)
+    lower = jnp.where(lat == lax.axis_size("lat") - 1, 0.0, 1.0)
+
+    def both_sides(odd):
+        near = load(noisy_hbm, noisy_2, sems.at[2 * PARTS])
+        copies = []
+        sides = ((1 - odd, got_1), (odd, got_2))
+        for k, (low, _) in enumerate(sides):
+            for j in range(2):
+                put_act(a3.at[k], (1 - low) * 2 + j, edge[pl.ds((low * 2 + j) * C, C), :])
+                r = low * (R - 2) + j
+                put_taps(x3.at[k], (1 - low) * 2 + j, own_row(xs, halo, r), cond[pl.ds(r * CP, CP), :])
+        for k, (low, got) in enumerate(sides):
+            if k == 1:
+                near.wait()
+            noisy = noisy_2 if k else noisy_1
+            for j in range(2):
+                tile = got[:, WX + j * LT : WX + (j + 1) * LT]
+                x = jnp.concatenate([noisy[pl.ds(j * C, C), :], tile], axis=1)
+                put_taps(x3.at[k], low * 2 + j, x, got[j * CP : (j + 1) * CP, 0:WX])
+            v = first_conv(wts, bias, x3[k])
+            v0, v1 = (v[0:C], v[C:] * lower) if low else (v[0:C] * upper, v[C:])
+            put_act(a3.at[k], low * 2, v0.astype(BF))
+            put_act(a3.at[k], low * 2 + 1, v1.astype(BF))
+            z = second_conv(wts, bias, a3[k], xs[pl.ds(low * (R - 2) * C, 2 * C), :])
+            rows = [z[0:C], z[C:]]
+            inner = [zi[pl.ds((low * (half - 2) + r) * C, C), :] for r in range(half - 2)]
+            rows = inner + rows if low else rows + inner
+            here = pl.ds(low * half, half)
+            for g in range(PARTS):
+                chans = pl.ds(g * each, each)
+                group = jnp.stack([row[g * each : (g + 1) * each] for row in rows], axis=0)
+                buf[k, chans] = jnp.swapaxes(group, 0, 1)
+                copies.append(load(buf.at[k, chans], out.at[chans, here, :], sems.at[k * PARTS + g]))
+        for copy in copies:
+            copy.wait()
+
+    for odd in range(2):
+        pl.when(lax.rem(lat, 2) == odd)(lambda odd=odd: both_sides(odd))
 
 
 def outer_rows(zi, edge, cond, halo, noisy_1, noisy_2, got_1, got_2, xs, wts, bias):
@@ -412,9 +425,9 @@
         in_specs=vmem(5) + hbm(1) + vmem(5),
         out_specs=hbm(1)[0],
         scratch_shapes=[
-            pltpu.VMEM((2 * TAPS, WX), BF),
-            pltpu.VMEM((2 * TAPS_OUT, W), BF),
-            pltpu.VMEM((C, R, W), BF),
+            pltpu.VMEM((2, TAPS, WX), BF),
+            pltpu.VMEM((2, TAPS_OUT, W), BF),
+            pltpu.VMEM((2, C, R // 2, W), BF),
             pltpu.VMEM((2 * C, W), BF),
             pltpu.SemaphoreType.DMA((2 * PARTS + 1,)),
         ],

time: 42.2 us -> 41.7 us (0.988)
  Pallas kernels: 21.2 us -> 19.9 us
  waiting for transfers between devices: 2.4 us -> 3.38 us
    pallas_call x1, Pallas kernels: 4.61 us -> 3.63 us  [turned(): pl.pallas_call(kernel, out_shape=(kept((R * C, W)), pltpu.HBM((2 * C, W),...]
    all_to_all x1, waiting for transfers between devices: 2.39 us -> 3.37 us  [local(): got = lax.all_to_all(msg, 'lon', split_axis=0, concat_axis=0, tiled=True)]
  transfers between devices with their start and end apart: 5 -> 5, of which waited for: 1 -> 1; matrix products, arithmetic and copies ran while one was open for 0% -> 0% of each run, Pallas kernels for 33% -> 31%
where the time goes in v4:
time: 41.7 us; the launch traced here: 41.5 us
  Pallas kernels  19.9 us (48%)
  starting transfers between devices  17.9 us (43%)
  waiting for transfers between devices  3.38 us (8%)
    all_to_all x1, starting transfers between devices, local(): got = lax.all_to_all(msg, 'lon', split_axis=0, concat_axis=0, tiled=True)  8.61 us
    ppermute x2, starting transfers between devices, exchanged(): lax.ppermute(second, 'lat', [(i, (i + 1 ^ 1) - 1) for i in range(1, count...  6.04 us
    pallas_call x1, Pallas kernels, inner_rows(): pl.pallas_call(inner_kernel, out_shape=(kept(((R - 4) * C, W)), kept((4 *...  6.02 us
    pallas_call x1, Pallas kernels, outer_rows(): pl.pallas_call(outer_kernel, out_shape=pltpu.HBM((C, R, W), BF), in_specs...  4.67 us
    pallas_call x1, Pallas kernels, turned(): pl.pallas_call(kernel, out_shape=(kept((R * C, W)), pltpu.HBM((2 * C, W),...  3.63 us
    all_to_all x1, waiting for transfers between devices, local(): got = lax.all_to_all(msg, 'lon', split_axis=0, concat_axis=0, tiled=True)  3.37 us
    pallas_call x1, Pallas kernels, cond_tile(): pl.pallas_call(cond_kernel, out_shape=(kept((R * CP, WX)), kept((R * C, L...  3.31 us
    ppermute x2, starting transfers between devices, exchanged(): got_1 = lax.ppermute(first, 'lat', [(i, i ^ 1) for i in range(count)])  3.24 us
  transfers between devices with their start and end apart: 5, of which 1 were waited for; matrix products, arithmetic and copies ran while one was open for 0% of the time, Pallas kernels for 31%

profile of v4, /device:TPU:1, one launch (start us, length us, event | category | flops | bytes accessed | tf_op | source)
XLA Modules:
  0.0 41.5 jit_solution(10527759107651775324)
XLA Ops:
  0.0 2.3 %shard_map.118 = bf16[16,144,128]{2,1,0:T(8,128)(2,1)} custom-call(bf16[64,16,1280]{2,1,0:T(8,128)(2,1)} %noisy_ref.3, bf16[1,30,4,128]{3,2,1,0:T(4,128)(2,1)} %bitcast.6, s32[1,1,4,4]{3,2,1,0:T(4,128)} %owner.1, s32[1,1,4,4]{3,2,1,0:T(4,128)} %slot.1, s32[1,1,4,4]{3,2,1,0:T(4,128)} %weight.1, s32[1,1,4]{2,1,0:T(1,128)} %counts.1), custom_call_target="tpu_custom_call" | custom-call | tf_op jit(solution)/shard_map/pallas_call | solution.py:116
  2.3 8.6 %all-to-all-start = ((bf16[16,144,128]{2,1,0:T(8,128)(2,1)}), bf16[16,144,128]{2,1,0:T(8,128)(2,1)S(1)}, u32[]{:S(2)}, u32[]{:S(2)}) async-start(bf16[16,144,128]{2,1,0:T(8,128)(2,1)} %shard_map.118), calls=%async_computation | async-start | bytes 1179648 | tf_op jit(solution)/shard_map/all_to_all | solution.py:450
  10.9 3.6 %shard_map.119 = (bf16[1024,1280]{1,0:T(8,128)(2,1)S(1)}, bf16[128,1280]{1,0:T(8,128)(2,1)}, bf16[128,1280]{1,0:T(8,128)(2,1)}, bf16[128,1920]{1,0:T(8,128)(2,1)}, f32[128,256]{1,0:T(8,128)}) custom-call(bf16[64,16,1280]{2,1,0:T(8,128)(2,1)} %noisy_ref.3, bf16[3,3,64,64]{3,2,1,0:T(8,128)(2,1)} %refs_0_.1, bf16[3,3,30,64]{3,2,1,0:T(8,128)(2,1)} %bitcast.7, ...), custom_call_target="tpu_custom_call" | custom-call | flops 3000000000 | bytes 12000000 | tf_op jit(solution)/shard_map/pallas_call | solution.py:200
  14.6 1.0 %collective-permute-start = (bf16[128,1280]{1,0:T(8,128)(2,1)}, bf16[128,1280]{1,0:T(8,128)(2,1)S(1)}, u32[]{:S(2)}, u32[]{:S(2)}) collective-permute-start(bf16[128,1280]{1,0:T(8,128)(2,1)} %get-tuple-element.27), channel_id=1, source_target_pairs={{0,16},{16,0},{32,48},{48,32},{64,80},{80,64},{96,112},{112,96},{1... | collective-permute-start | bytes 983048 | tf_op jit(solution)/shard_map/ppermute | solution.py:440
  15.6 3.0 %collective-permute-start.1 = (bf16[128,1280]{1,0:T(8,128)(2,1)}, bf16[128,1280]{1,0:T(8,128)(2,1)}, u32[]{:S(2)}, u32[]{:S(2)}) collective-permute-start(bf16[128,1280]{1,0:T(8,128)(2,1)} %get-tuple-element.28), channel_id=1, source_target_pairs={{16,32},{32,16},{48,64},{64,48},{80,96},{96,80},{17,33},{33,17},{4... | collective-permute-start | bytes 983048 | tf_op jit(solution)/shard_map/ppermute | solution.py:441
  18.6 3.4 %all-to-all-done.got = bf16[16,144,128]{2,1,0:T(8,128)(2,1)S(1)} async-done(((bf16[16,144,128]{2,1,0:T(8,128)(2,1)}), bf16[16,144,128]{2,1,0:T(8,128)(2,1)S(1)}, u32[]{:S(2)}, u32[]{:S(2)}) %all-to-all-start) | async-done | bytes 589856 | tf_op jit(solution)/shard_map/all_to_all | solution.py:450
  22.0 3.3 %shard_map.120 = (bf16[512,1408]{1,0:T(8,128)(2,1)S(1)}, bf16[1024,128]{1,0:T(8,128)(2,1)S(1)}, bf16[64,1664]{1,0:T(8,128)(2,1)S(1)}, bf16[64,1664]{1,0:T(8,128)...) custom-call(bf16[16,144,128]{2,1,0:T(8,128)(2,1)S(1)} %all-to-all-done.got, bf16[512,5120]{1,0:T(8,128)(2,1)} %bitcast.5, ...), custom_call_target="tpu_custom_call" | custom-call | tf_op jit(solution)/shard_map/pallas_call | solution.py:288
  25.3 2.2 %collective-permute-start.2 = (bf16[64,1664]{1,0:T(8,128)(2,1)S(1)}, bf16[64,1664]{1,0:T(8,128)(2,1)S(1)}, u32[]{:S(2)}, u32[]{:S(2)}) collective-permute-start(bf16[64,1664]{1,0:T(8,128)(2,1)S(1)} %get-tuple-element.29), channel_id=1, source_target_pairs={{0,16},{16,0},{32,48},{48,32},{64,80},{80,64},{96,112},{112,96},{1... | collective-permute-start | bytes 638984 | tf_op jit(solution)/shard_map/ppermute | solution.py:440
  27.5 3.0 %collective-permute-start.3 = (bf16[64,1664]{1,0:T(8,128)(2,1)S(1)}, bf16[64,1664]{1,0:T(8,128)(2,1)S(1)}, u32[]{:S(2)}, u32[]{:S(2)}) collective-permute-start(bf16[64,1664]{1,0:T(8,128)(2,1)S(1)} %get-tuple-element.30), channel_id=1, source_target_pairs={{16,32},{32,16},{48,64},{64,48},{80,96},{96,80},{17,33},{33,17},{4... | collective-permute-start | bytes 638984 | tf_op jit(solution)/shard_map/ppermute | solution.py:441
  30.6 6.0 %shard_map.121 = (bf16[768,1280]{1,0:T(8,128)(2,1)S(1)}, bf16[256,1408]{1,0:T(8,128)(2,1)S(1)}) custom-call(bf16[512,1408]{1,0:T(8,128)(2,1)S(1)} %get-tuple-element.20.cond, bf16[1024,128]{1,0:T(8,128)(2,1)S(1)} %get-tuple-element.21.halo, bf16[1024,1280]{1,0:T(8,128)(2,1)S(1)} %get-tuple-element.22.xs, bf16[128,1920]{1,0:T(8,128)(2,1)S(1)} %get-tuple-element.23.wts, ...), custom_call_target="tpu_custom_call" | custom-call | flops 6000000000 | bytes 12000000 | tf_op jit(solution)/shard_map/pallas_call | solution.py:360
  36.6 0.0 collective-permute-done.noisy_1
  36.6 0.0 collective-permute-done.1.noisy_hbm
  36.6 0.0 collective-permute-done.2.got_1
  36.6 0.0 collective-permute-done.3.got_2
  36.6 4.7 %shard_map.122 = bf16[64,16,1280]{2,1,0:T(8,128)(2,1)} custom-call(bf16[768,1280]{1,0:T(8,128)(2,1)S(1)} %get-tuple-element.25.zi, bf16[256,1408]{1,0:T(8,128)(2,1)S(1)} %get-tuple-element.26.edge, bf16[512,1408]{1,0:T(8,128)(2,1)S(1)} %get-tuple-element.20.cond, bf16[1024,128]{1,0:T(8,128)(2,1)S(1)} %get-tuple-element.21.halo, ...), custom_call_target="tpu_custom_call" | custom-call | tf_op jit(solution)/shard_map/pallas_call | solution.py:422
Async XLA Ops:
  2.3 19.7 %all-to-all-start = ((bf16[16,144,128]{2,1,0:T(8,128)(2,1)}), bf16[16,144,128]{2,1,0:T(8,128)(2,1)S(1)}, u32[]{:S(2)}, u32[]{:S(2)}) async-start(bf16[16,144,128]{2,1,0:T(8,128)(2,1)} %shard_map.118), calls=%async_computation | async-start | bytes 1179648 | tf_op jit(solution)/shard_map/all_to_all | solution.py:450
  14.6 22.0 %collective-permute-start = (bf16[128,1280]{1,0:T(8,128)(2,1)}, bf16[128,1280]{1,0:T(8,128)(2,1)S(1)}, u32[]{:S(2)}, u32[]{:S(2)}) collective-permute-start(bf16[128,1280]{1,0:T(8,128)(2,1)} %get-tuple-element.27), channel_id=1, source_target_pairs={{0,16},{16,0},{32,48},{48,32},{64,80},{80,64},{96,112},{112,96},{1... | collective-permute-start | bytes 983048 | tf_op jit(solution)/shard_map/ppermute | solution.py:440
  15.6 21.0 %collective-permute-start.1 = (bf16[128,1280]{1,0:T(8,128)(2,1)}, bf16[128,1280]{1,0:T(8,128)(2,1)}, u32[]{:S(2)}, u32[]{:S(2)}) collective-permute-start(bf16[128,1280]{1,0:T(8,128)(2,1)} %get-tuple-element.28), channel_id=1, source_target_pairs={{16,32},{32,16},{48,64},{64,48},{80,96},{96,80},{17,33},{33,17},{4... | collective-permute-start | bytes 983048 | tf_op jit(solution)/shard_map/ppermute | solution.py:441
  25.3 11.3 %collective-permute-start.2 = (bf16[64,1664]{1,0:T(8,128)(2,1)S(1)}, bf16[64,1664]{1,0:T(8,128)(2,1)S(1)}, u32[]{:S(2)}, u32[]{:S(2)}) collective-permute-start(bf16[64,1664]{1,0:T(8,128)(2,1)S(1)} %get-tuple-element.29), channel_id=1, source_target_pairs={{0,16},{16,0},{32,48},{48,32},{64,80},{80,64},{96,112},{112,96},{1... | collective-permute-start | bytes 638984 | tf_op jit(solution)/shard_map/ppermute | solution.py:440
  27.5 9.1 %collective-permute-start.3 = (bf16[64,1664]{1,0:T(8,128)(2,1)S(1)}, bf16[64,1664]{1,0:T(8,128)(2,1)S(1)}, u32[]{:S(2)}, u32[]{:S(2)}) collective-permute-start(bf16[64,1664]{1,0:T(8,128)(2,1)S(1)} %get-tuple-element.30), channel_id=1, source_target_pairs={{16,32},{32,16},{48,64},{64,48},{80,96},{96,80},{17,33},{33,17},{4... | collective-permute-start | bytes 638984 | tf_op jit(solution)/shard_map/ppermute | solution.py:441

commit v5 on v4

--- a/solution.py
+++ b/solution.py
@@ -265,7 +265,9 @@
 
     lane = iota((SUBS * CP, LT), 1)
     for r in range(R // SUBS):
-        loads[r].wait()
+        if r % 2 == 0:
+            loads[r].wait()
+            loads[r + 1].wait()
         part = table.at[r]
         own = jnp.dot(grp[0], part[...], preferred_element_type=F32).astype(BF)
         lhs = jnp.dot(grp[1], part[:, W - LT : W], preferred_element_type=F32)
@@ -340,7 +342,8 @@
     return (y + x.astype(F32) + bias[:, LT : LT + 1]).astype(BF)
 
 
-def inner_kernel(cond, halo, xs, wts, bias, zi, edge, x3, a3):
+def inner_kernel(cond, halo, xs, wts, bias, noisy_hbm, zi, edge, noisy_2, x3, a3, sem):
+    near = load(noisy_hbm, noisy_2, sem)
     for r in range(R):
         put_taps(x3, r, own_row(xs, halo, r), cond[pl.ds(r * CP, CP), :])
     for i in range(PAIRS):
@@ -354,25 +357,27 @@
     for i in range(PAIRS - 1):
         x = xs[pl.ds((i + 1) * 2 * C, 2 * C), :]
         zi[pl.ds(i * 2 * C, 2 * C), :] = second_conv(wts, bias, a3[pl.ds(i * 6 * C, TAPS_OUT), :], x)
-
-
-def inner_rows(cond, halo, xs, wts, bias):
+    near.wait()
+
+
+def inner_rows(cond, halo, xs, wts, bias, noisy_2):
     return pl.pallas_call(
         inner_kernel,
-        out_shape=(kept(((R - 4) * C, W)), kept((4 * C, WX))),
-        in_specs=vmem(5),
-        out_specs=tuple(vmem(2)),
+        out_shape=(kept(((R - 4) * C, W)), kept((4 * C, WX)), kept((2 * C, W))),
+        in_specs=vmem(5) + hbm(1),
+        out_specs=tuple(vmem(3)),
         scratch_shapes=[
             pltpu.VMEM((R * TAP, WX), BF),
             pltpu.VMEM(((R - 2) * 3 * C, W), BF),
+            pltpu.SemaphoreType.DMA,
         ],
         compiler_params=params(26),
         cost_estimate=pl.CostEstimate(flops=6 * 10**9, bytes_accessed=12 * 10**6, transcendentals=10**6),
-    )(*in_vmem(cond, halo, xs, wts, bias))
+    )(*in_vmem(cond, halo, xs, wts, bias), *in_hbm(noisy_2))
 
 
 def outer_kernel(
-    zi, edge, cond, halo, noisy_1, noisy_hbm, got_1, got_2, xs, wts, bias, out, x3, a3, buf, noisy_2, sems
+    zi, edge, cond, halo, noisy_1, noisy_2, got_1, got_2, xs, wts, bias, out, x3, a3, buf, sems
 ):
     lat = lax.axis_index("lat")
     half = R // 2
@@ -381,7 +386,6 @@
     lower = jnp.where(lat == lax.axis_size("lat") - 1, 0.0, 1.0)
 
     def both_sides(odd):
-        near = load(noisy_hbm, noisy_2, sems.at[2 * PARTS])
         copies = []
         sides = ((1 - odd, got_1), (odd, got_2))
         for k, (low, _) in enumerate(sides):
@@ -390,8 +394,6 @@
                 r = low * (R - 2) + j
                 put_taps(x3.at[k], (1 - low) * 2 + j, own_row(xs, halo, r), cond[pl.ds(r * CP, CP), :])
         for k, (low, got) in enumerate(sides):
-            if k == 1:
-                near.wait()
             noisy = noisy_2 if k else noisy_1
             for j in range(2):
                 tile = got[:, WX + j * LT : WX + (j + 1) * LT]
@@ -422,17 +424,16 @@
     return pl.pallas_call(
         outer_kernel,
         out_shape=pltpu.HBM((C, R, W), BF),
-        in_specs=vmem(5) + hbm(1) + vmem(5),
+        in_specs=vmem(11),
         out_specs=hbm(1)[0],
         scratch_shapes=[
             pltpu.VMEM((2, TAPS, WX), BF),
             pltpu.VMEM((2, TAPS_OUT, W), BF),
             pltpu.VMEM((2, C, R // 2, W), BF),
-            pltpu.VMEM((2 * C, W), BF),
-            pltpu.SemaphoreType.DMA((2 * PARTS + 1,)),
+            pltpu.SemaphoreType.DMA((2 * PARTS,)),
         ],
         compiler_params=params(24),
-    )(*in_vmem(zi, edge, cond, halo), noisy_1, *in_hbm(noisy_2), got_1, got_2, *in_vmem(xs, wts, bias))
+    )(*in_vmem(zi, edge, cond, halo), noisy_1, *in_vmem(noisy_2), got_1, got_2, *in_vmem(xs, wts, bias))
 
 
 def exchanged(first, second):
@@ -452,7 +453,7 @@
     noisy_1, noisy_2 = exchanged(first, second)
     cond, halo, first, second, wts, bias = cond_tile(got, table, wts, bias)
     got_1, got_2 = exchanged(first, second)
-    zi, edge = inner_rows(cond, halo, xs, wts, bias)
+    zi, edge, noisy_2 = inner_rows(cond, halo, xs, wts, bias, noisy_2)
     return outer_rows(zi, edge, cond, halo, noisy_1, noisy_2, got_1, got_2, xs, wts, bias)
 
 

time: 41.7 us -> 41.7 us (level)
    ppermute x2, starting transfers between devices: 3.24 us -> 2.29 us  [exchanged(): got_1 = lax.ppermute(first, 'lat', [(i, i ^ 1) for i in range(count)])]
    ppermute x2, starting transfers between devices: 6.04 us -> 6.98 us  [exchanged(): lax.ppermute(second, 'lat', [(i, (i + 1 ^ 1) - 1) for i in range(1, count...]
where the time goes in v5:
time: 41.7 us; the launch traced here: 41.4 us
  Pallas kernels  19.9 us (48%)
  starting transfers between devices  17.9 us (43%)
  waiting for transfers between devices  3.38 us (8%)
    all_to_all x1, starting transfers between devices, local(): got = lax.all_to_all(msg, 'lon', split_axis=0, concat_axis=0, tiled=True)  8.61 us
    ppermute x2, starting transfers between devices, exchanged(): lax.ppermute(second, 'lat', [(i, (i + 1 ^ 1) - 1) for i in range(1, count...  6.98 us
    pallas_call x1, Pallas kernels, inner_rows(): pl.pallas_call(inner_kernel, out_shape=(kept(((R - 4) * C, W)), kept((4 *...  6.04 us
    pallas_call x1, Pallas kernels, outer_rows(): pl.pallas_call(outer_kernel, out_shape=pltpu.HBM((C, R, W), BF), in_specs...  4.58 us
    pallas_call x1, Pallas kernels, turned(): pl.pallas_call(kernel, out_shape=(kept((R * C, W)), pltpu.HBM((2 * C, W),...  3.63 us
    all_to_all x1, waiting for transfers between devices, local(): got = lax.all_to_all(msg, 'lon', split_axis=0, concat_axis=0, tiled=True)  3.37 us
    pallas_call x1, Pallas kernels, cond_tile(): pl.pallas_call(cond_kernel, out_shape=(kept((R * CP, WX)), kept((R * C, L...  3.31 us
    pallas_call x1, Pallas kernels, message(): pl.pallas_call(kernel, out_shape=kept((PEERS, MSG, LT)), in_specs=hbm(6),...  2.31 us
  transfers between devices with their start and end apart: 5, of which 1 were waited for; matrix products, arithmetic and copies ran while one was open for 0% of the time, Pallas kernels for 31%

profile of v5, /device:TPU:1, one launch (start us, length us, event | category | flops | bytes accessed | tf_op | source)
XLA Modules:
  0.0 41.4 jit_solution(13224579466388055611)
XLA Ops:
  0.0 2.3 %shard_map.118 = bf16[16,144,128]{2,1,0:T(8,128)(2,1)} custom-call(bf16[64,16,1280]{2,1,0:T(8,128)(2,1)} %noisy_ref.3, bf16[1,30,4,128]{3,2,1,0:T(4,128)(2,1)} %bitcast.6, s32[1,1,4,4]{3,2,1,0:T(4,128)} %owner.1, s32[1,1,4,4]{3,2,1,0:T(4,128)} %slot.1, s32[1,1,4,4]{3,2,1,0:T(4,128)} %weight.1, s32[1,1,4]{2,1,0:T(1,128)} %counts.1), custom_call_target="tpu_custom_call" | custom-call | tf_op jit(solution)/shard_map/pallas_call | solution.py:116
  2.3 8.6 %all-to-all-start = ((bf16[16,144,128]{2,1,0:T(8,128)(2,1)}), bf16[16,144,128]{2,1,0:T(8,128)(2,1)S(1)}, u32[]{:S(2)}, u32[]{:S(2)}) async-start(bf16[16,144,128]{2,1,0:T(8,128)(2,1)} %shard_map.118), calls=%async_computation | async-start | bytes 1179648 | tf_op jit(solution)/shard_map/all_to_all | solution.py:451
  10.9 3.6 %shard_map.119 = (bf16[1024,1280]{1,0:T(8,128)(2,1)S(1)}, bf16[128,1280]{1,0:T(8,128)(2,1)}, bf16[128,1280]{1,0:T(8,128)(2,1)}, bf16[128,1920]{1,0:T(8,128)(2,1)}, f32[128,256]{1,0:T(8,128)}) custom-call(bf16[64,16,1280]{2,1,0:T(8,128)(2,1)} %noisy_ref.3, bf16[3,3,64,64]{3,2,1,0:T(8,128)(2,1)} %refs_0_.1, bf16[3,3,30,64]{3,2,1,0:T(8,128)(2,1)} %bitcast.7, ...), custom_call_target="tpu_custom_call" | custom-call | flops 3000000000 | bytes 12000000 | tf_op jit(solution)/shard_map/pallas_call | solution.py:200
  14.6 4.0 %collective-permute-start = (bf16[128,1280]{1,0:T(8,128)(2,1)}, bf16[128,1280]{1,0:T(8,128)(2,1)}, u32[]{:S(2)}, u32[]{:S(2)}) collective-permute-start(bf16[128,1280]{1,0:T(8,128)(2,1)} %get-tuple-element.26), channel_id=1, source_target_pairs={{16,32},{32,16},{48,64},{64,48},{80,96},{96,80},{17,33},{33,17},{4... | collective-permute-start | bytes 983048 | tf_op jit(solution)/shard_map/ppermute | solution.py:442
  18.5 0.1 collective-permute-start.1
  18.6 3.4 %all-to-all-done.got = bf16[16,144,128]{2,1,0:T(8,128)(2,1)S(1)} async-done(((bf16[16,144,128]{2,1,0:T(8,128)(2,1)}), bf16[16,144,128]{2,1,0:T(8,128)(2,1)S(1)}, u32[]{:S(2)}, u32[]{:S(2)}) %all-to-all-start) | async-done | bytes 589856 | tf_op jit(solution)/shard_map/all_to_all | solution.py:451
  22.0 3.3 %shard_map.120 = (bf16[512,1408]{1,0:T(8,128)(2,1)S(1)}, bf16[1024,128]{1,0:T(8,128)(2,1)S(1)}, bf16[64,1664]{1,0:T(8,128)(2,1)S(1)}, bf16[64,1664]{1,0:T(8,128)...) custom-call(bf16[16,144,128]{2,1,0:T(8,128)(2,1)S(1)} %all-to-all-done.got, bf16[512,5120]{1,0:T(8,128)(2,1)} %bitcast.5, ...), custom_call_target="tpu_custom_call" | custom-call | tf_op jit(solution)/shard_map/pallas_call | solution.py:290
  25.3 2.2 %collective-permute-start.2 = (bf16[64,1664]{1,0:T(8,128)(2,1)S(1)}, bf16[64,1664]{1,0:T(8,128)(2,1)S(1)}, u32[]{:S(2)}, u32[]{:S(2)}) collective-permute-start(bf16[64,1664]{1,0:T(8,128)(2,1)S(1)} %get-tuple-element.31), channel_id=1, source_target_pairs={{0,16},{16,0},{32,48},{48,32},{64,80},{80,64},{96,112},{112,96},{1... | collective-permute-start | bytes 638984 | tf_op jit(solution)/shard_map/ppermute | solution.py:441
  27.5 3.0 %collective-permute-start.3 = (bf16[64,1664]{1,0:T(8,128)(2,1)S(1)}, bf16[64,1664]{1,0:T(8,128)(2,1)S(1)}, u32[]{:S(2)}, u32[]{:S(2)}) collective-permute-start(bf16[64,1664]{1,0:T(8,128)(2,1)S(1)} %get-tuple-element.32), channel_id=1, source_target_pairs={{16,32},{32,16},{48,64},{64,48},{80,96},{96,80},{17,33},{33,17},{4... | collective-permute-start | bytes 638984 | tf_op jit(solution)/shard_map/ppermute | solution.py:442
  30.6 0.0 collective-permute-done.noisy_hbm
  30.6 6.0 %shard_map.121 = (bf16[768,1280]{1,0:T(8,128)(2,1)S(1)}, bf16[256,1408]{1,0:T(8,128)(2,1)S(1)}, bf16[128,1280]{1,0:T(8,128)(2,1)S(1)}) custom-call(bf16[512,1408]{1,0:T(8,128)(2,1)S(1)} %get-tuple-element.21.cond, bf16[1024,128]{1,0:T(8,128)(2,1)S(1)} %get-tuple-element.22.halo, bf16[1024,1280]{1,0:T(8,128)(2,1)S(1)} %get-tuple-element.23.xs, ...), custom_call_target="tpu_custom_call" | custom-call | flops 6000000000 | bytes 12000000 | tf_op jit(solution)/shard_map/pallas_call | solution.py:364
  36.6 0.0 collective-permute-done.1.noisy_1
  36.6 0.0 collective-permute-done.2.got_1
  36.6 0.0 collective-permute-done.3.got_2
  36.7 4.6 %shard_map.122 = bf16[64,16,1280]{2,1,0:T(8,128)(2,1)} custom-call(bf16[768,1280]{1,0:T(8,128)(2,1)S(1)} %get-tuple-element.27.zi, bf16[256,1408]{1,0:T(8,128)(2,1)S(1)} %get-tuple-element.28.edge, bf16[512,1408]{1,0:T(8,128)(2,1)S(1)} %get-tuple-element.21.cond, bf16[1024,128]{1,0:T(8,128)(2,1)S(1)} %get-tuple-element.22.halo, ...), custom_call_target="tpu_custom_call" | custom-call | tf_op jit(solution)/shard_map/pallas_call | solution.py:424
Async XLA Ops:
  2.3 19.7 %all-to-all-start = ((bf16[16,144,128]{2,1,0:T(8,128)(2,1)}), bf16[16,144,128]{2,1,0:T(8,128)(2,1)S(1)}, u32[]{:S(2)}, u32[]{:S(2)}) async-start(bf16[16,144,128]{2,1,0:T(8,128)(2,1)} %shard_map.118), calls=%async_computation | async-start | bytes 1179648 | tf_op jit(solution)/shard_map/all_to_all | solution.py:451
  14.6 16.0 %collective-permute-start = (bf16[128,1280]{1,0:T(8,128)(2,1)}, bf16[128,1280]{1,0:T(8,128)(2,1)}, u32[]{:S(2)}, u32[]{:S(2)}) collective-permute-start(bf16[128,1280]{1,0:T(8,128)(2,1)} %get-tuple-element.26), channel_id=1, source_target_pairs={{16,32},{32,16},{48,64},{64,48},{80,96},{96,80},{17,33},{33,17},{4... | collective-permute-start | bytes 983048 | tf_op jit(solution)/shard_map/ppermute | solution.py:442
  18.5 18.1 %collective-permute-start.1 = (bf16[128,1280]{1,0:T(8,128)(2,1)}, bf16[128,1280]{1,0:T(8,128)(2,1)S(1)}, u32[]{:S(2)}, u32[]{:S(2)}) collective-permute-start(bf16[128,1280]{1,0:T(8,128)(2,1)} %get-tuple-element.29), channel_id=1, source_target_pairs={{0,16},{16,0},{32,48},{48,32},{64,80},{80,64},{96,112},{112,96},{1... | collective-permute-start | bytes 983048 | tf_op jit(solution)/shard_map/ppermute | solution.py:441
  25.3 11.3 %collective-permute-start.2 = (bf16[64,1664]{1,0:T(8,128)(2,1)S(1)}, bf16[64,1664]{1,0:T(8,128)(2,1)S(1)}, u32[]{:S(2)}, u32[]{:S(2)}) collective-permute-start(bf16[64,1664]{1,0:T(8,128)(2,1)S(1)} %get-tuple-element.31), channel_id=1, source_target_pairs={{0,16},{16,0},{32,48},{48,32},{64,80},{80,64},{96,112},{112,96},{1... | collective-permute-start | bytes 638984 | tf_op jit(solution)/shard_map/ppermute | solution.py:441
  27.5 9.1 %collective-permute-start.3 = (bf16[64,1664]{1,0:T(8,128)(2,1)S(1)}, bf16[64,1664]{1,0:T(8,128)(2,1)S(1)}, u32[]{:S(2)}, u32[]{:S(2)}) collective-permute-start(bf16[64,1664]{1,0:T(8,128)(2,1)S(1)} %get-tuple-element.32), channel_id=1, source_target_pairs={{16,32},{32,16},{48,64},{64,48},{80,96},{96,80},{17,33},{33,17},{4... | collective-permute-start | bytes 638984 | tf_op jit(solution)/shard_map/ppermute | solution.py:442

commit v6 on v5

--- a/solution.py
+++ b/solution.py
@@ -268,10 +268,14 @@
         if r % 2 == 0:
             loads[r].wait()
             loads[r + 1].wait()
+            lt = jnp.concatenate([table[q, :, W - LT : W] for q in (r, r + 1)], axis=1)
+            rt = jnp.concatenate([table[q, :, 0:LT] for q in (r, r + 1)], axis=1)
+            lhs_2 = jnp.dot(grp[1], lt, preferred_element_type=F32)
+            rhs_2 = jnp.dot(grp[2], rt, preferred_element_type=F32)
         part = table.at[r]
+        tile = slice(r % 2 * LT, (r % 2 + 1) * LT)
         own = jnp.dot(grp[0], part[...], preferred_element_type=F32).astype(BF)
-        lhs = jnp.dot(grp[1], part[:, W - LT : W], preferred_element_type=F32)
-        rhs = jnp.dot(grp[2], part[:, 0:LT], preferred_element_type=F32)
+        lhs, rhs = lhs_2[:, tile], rhs_2[:, tile]
         side = jnp.where(lane < 2, rhs, jnp.where(lane >= 126, lhs, 0.0)).astype(BF)
         for s in range(SUBS):
             at = pl.ds((s * SUBS + r) * CP, CP)
@@ -380,13 +384,13 @@
     zi, edge, cond, halo, noisy_1, noisy_2, got_1, got_2, xs, wts, bias, out, x3, a3, buf, sems
 ):
     lat = lax.axis_index("lat")
-    half = R // 2
     each = C // PARTS
     upper = jnp.where(lat == 0, 0.0, 1.0)
     lower = jnp.where(lat == lax.axis_size("lat") - 1, 0.0, 1.0)
 
     def both_sides(odd):
         copies = []
+        ends = {}
         sides = ((1 - odd, got_1), (odd, got_2))
         for k, (low, _) in enumerate(sides):
             for j in range(2):
@@ -404,15 +408,13 @@
             put_act(a3.at[k], low * 2, v0.astype(BF))
             put_act(a3.at[k], low * 2 + 1, v1.astype(BF))
             z = second_conv(wts, bias, a3[k], xs[pl.ds(low * (R - 2) * C, 2 * C), :])
-            rows = [z[0:C], z[C:]]
-            inner = [zi[pl.ds((low * (half - 2) + r) * C, C), :] for r in range(half - 2)]
-            rows = inner + rows if low else rows + inner
-            here = pl.ds(low * half, half)
-            for g in range(PARTS):
-                chans = pl.ds(g * each, each)
-                group = jnp.stack([row[g * each : (g + 1) * each] for row in rows], axis=0)
-                buf[k, chans] = jnp.swapaxes(group, 0, 1)
-                copies.append(load(buf.at[k, chans], out.at[chans, here, :], sems.at[k * PARTS + g]))
+            ends[low] = [z[0:C], z[C:]]
+        rows = ends[0] + [zi[pl.ds(r * C, C), :] for r in range(R - 4)] + ends[1]
+        for g in range(PARTS):
+            chans = pl.ds(g * each, each)
+            group = jnp.stack([row[g * each : (g + 1) * each] for row in rows], axis=0)
+            buf[chans] = jnp.swapaxes(group, 0, 1)
+            copies.append(load(buf.at[chans], out.at[chans], sems.at[g]))
         for copy in copies:
             copy.wait()
 
@@ -429,8 +431,8 @@
         scratch_shapes=[
             pltpu.VMEM((2, TAPS, WX), BF),
             pltpu.VMEM((2, TAPS_OUT, W), BF),
-            pltpu.VMEM((2, C, R // 2, W), BF),
-            pltpu.SemaphoreType.DMA((2 * PARTS,)),
+            pltpu.VMEM((C, R, W), BF),
+            pltpu.SemaphoreType.DMA((PARTS,)),
         ],
         compiler_params=params(24),
     )(*in_vmem(zi, edge, cond, halo), noisy_1, *in_vmem(noisy_2), got_1, got_2, *in_vmem(xs, wts, bias))

time: 41.7 us -> 41.9 us (level)
  no operation moved by 1% of the time
where the time goes in v6:
time: 41.9 us; the launch traced here: 41.6 us
  Pallas kernels  20.1 us (48%)
  starting transfers between devices  17.9 us (43%)
  waiting for transfers between devices  3.38 us (8%)
    all_to_all x1, starting transfers between devices, local(): got = lax.all_to_all(msg, 'lon', split_axis=0, concat_axis=0, tiled=True)  8.61 us
    ppermute x2, starting transfers between devices, exchanged(): lax.ppermute(second, 'lat', [(i, (i + 1 ^ 1) - 1) for i in range(1, count...  6.98 us
    pallas_call x1, Pallas kernels, inner_rows(): pl.pallas_call(inner_kernel, out_shape=(kept(((R - 4) * C, W)), kept((4 *...  6.04 us
    pallas_call x1, Pallas kernels, outer_rows(): pl.pallas_call(outer_kernel, out_shape=pltpu.HBM((C, R, W), BF), in_specs...  4.88 us
    pallas_call x1, Pallas kernels, turned(): pl.pallas_call(kernel, out_shape=(kept((R * C, W)), pltpu.HBM((2 * C, W),...  3.63 us
    all_to_all x1, waiting for transfers between devices, local(): got = lax.all_to_all(msg, 'lon', split_axis=0, concat_axis=0, tiled=True)  3.37 us
    pallas_call x1, Pallas kernels, cond_tile(): pl.pallas_call(cond_kernel, out_shape=(kept((R * CP, WX)), kept((R * C, L...  3.24 us
    pallas_call x1, Pallas kernels, message(): pl.pallas_call(kernel, out_shape=kept((PEERS, MSG, LT)), in_specs=hbm(6),...  2.31 us
  transfers between devices with their start and end apart: 5, of which 1 were waited for; matrix products, arithmetic and copies ran while one was open for 0% of the time, Pallas kernels for 31%

profile of v6, /device:TPU:1, one launch (start us, length us, event | category | flops | bytes accessed | tf_op | source)
XLA Modules:
  0.0 41.6 jit_solution(15384450343967395215)
XLA Ops:
  0.0 2.3 %shard_map.118 = bf16[16,144,128]{2,1,0:T(8,128)(2,1)} custom-call(bf16[64,16,1280]{2,1,0:T(8,128)(2,1)} %noisy_ref.3, bf16[1,30,4,128]{3,2,1,0:T(4,128)(2,1)} %bitcast.6, s32[1,1,4,4]{3,2,1,0:T(4,128)} %owner.1, s32[1,1,4,4]{3,2,1,0:T(4,128)} %slot.1, s32[1,1,4,4]{3,2,1,0:T(4,128)} %weight.1, s32[1,1,4]{2,1,0:T(1,128)} %counts.1), custom_call_target="tpu_custom_call" | custom-call | tf_op jit(solution)/shard_map/pallas_call | solution.py:116
  2.3 8.6 %all-to-all-start = ((bf16[16,144,128]{2,1,0:T(8,128)(2,1)}), bf16[16,144,128]{2,1,0:T(8,128)(2,1)S(1)}, u32[]{:S(2)}, u32[]{:S(2)}) async-start(bf16[16,144,128]{2,1,0:T(8,128)(2,1)} %shard_map.118), calls=%async_computation | async-start | bytes 1179648 | tf_op jit(solution)/shard_map/all_to_all | solution.py:453
  10.9 3.6 %shard_map.119 = (bf16[1024,1280]{1,0:T(8,128)(2,1)S(1)}, bf16[128,1280]{1,0:T(8,128)(2,1)}, bf16[128,1280]{1,0:T(8,128)(2,1)}, bf16[128,1920]{1,0:T(8,128)(2,1)}, f32[128,256]{1,0:T(8,128)}) custom-call(bf16[64,16,1280]{2,1,0:T(8,128)(2,1)} %noisy_ref.3, bf16[3,3,64,64]{3,2,1,0:T(8,128)(2,1)} %refs_0_.1, bf16[3,3,30,64]{3,2,1,0:T(8,128)(2,1)} %bitcast.7, ...), custom_call_target="tpu_custom_call" | custom-call | flops 3000000000 | bytes 12000000 | tf_op jit(solution)/shard_map/pallas_call | solution.py:200
  14.6 4.0 %collective-permute-start = (bf16[128,1280]{1,0:T(8,128)(2,1)}, bf16[128,1280]{1,0:T(8,128)(2,1)}, u32[]{:S(2)}, u32[]{:S(2)}) collective-permute-start(bf16[128,1280]{1,0:T(8,128)(2,1)} %get-tuple-element.26), channel_id=1, source_target_pairs={{16,32},{32,16},{48,64},{64,48},{80,96},{96,80},{17,33},{33,17},{4... | collective-permute-start | bytes 983048 | tf_op jit(solution)/shard_map/ppermute | solution.py:444
  18.5 0.1 collective-permute-start.1
  18.6 3.4 %all-to-all-done.got = bf16[16,144,128]{2,1,0:T(8,128)(2,1)S(1)} async-done(((bf16[16,144,128]{2,1,0:T(8,128)(2,1)}), bf16[16,144,128]{2,1,0:T(8,128)(2,1)S(1)}, u32[]{:S(2)}, u32[]{:S(2)}) %all-to-all-start) | async-done | bytes 589856 | tf_op jit(solution)/shard_map/all_to_all | solution.py:453
  22.0 3.2 %shard_map.120 = (bf16[512,1408]{1,0:T(8,128)(2,1)S(1)}, bf16[1024,128]{1,0:T(8,128)(2,1)S(1)}, bf16[64,1664]{1,0:T(8,128)(2,1)S(1)}, bf16[64,1664]{1,0:T(8,128)...) custom-call(bf16[16,144,128]{2,1,0:T(8,128)(2,1)S(1)} %all-to-all-done.got, bf16[512,5120]{1,0:T(8,128)(2,1)} %bitcast.5, ...), custom_call_target="tpu_custom_call" | custom-call | tf_op jit(solution)/shard_map/pallas_call | solution.py:294
  25.3 2.2 %collective-permute-start.2 = (bf16[64,1664]{1,0:T(8,128)(2,1)S(1)}, bf16[64,1664]{1,0:T(8,128)(2,1)S(1)}, u32[]{:S(2)}, u32[]{:S(2)}) collective-permute-start(bf16[64,1664]{1,0:T(8,128)(2,1)S(1)} %get-tuple-element.31), channel_id=1, source_target_pairs={{0,16},{16,0},{32,48},{48,32},{64,80},{80,64},{96,112},{112,96},{1... | collective-permute-start | bytes 638984 | tf_op jit(solution)/shard_map/ppermute | solution.py:443
  27.5 3.0 %collective-permute-start.3 = (bf16[64,1664]{1,0:T(8,128)(2,1)S(1)}, bf16[64,1664]{1,0:T(8,128)(2,1)S(1)}, u32[]{:S(2)}, u32[]{:S(2)}) collective-permute-start(bf16[64,1664]{1,0:T(8,128)(2,1)S(1)} %get-tuple-element.32), channel_id=1, source_target_pairs={{16,32},{32,16},{48,64},{64,48},{80,96},{96,80},{17,33},{33,17},{4... | collective-permute-start | bytes 638984 | tf_op jit(solution)/shard_map/ppermute | solution.py:444
  30.5 0.0 collective-permute-done.noisy_hbm
  30.5 6.0 %shard_map.121 = (bf16[768,1280]{1,0:T(8,128)(2,1)S(1)}, bf16[256,1408]{1,0:T(8,128)(2,1)S(1)}, bf16[128,1280]{1,0:T(8,128)(2,1)S(1)}) custom-call(bf16[512,1408]{1,0:T(8,128)(2,1)S(1)} %get-tuple-element.21.cond, bf16[1024,128]{1,0:T(8,128)(2,1)S(1)} %get-tuple-element.22.halo, bf16[1024,1280]{1,0:T(8,128)(2,1)S(1)} %get-tuple-element.23.xs, ...), custom_call_target="tpu_custom_call" | custom-call | flops 6000000000 | bytes 12000000 | tf_op jit(solution)/shard_map/pallas_call | solution.py:368
  36.6 0.0 collective-permute-done.1.noisy_1
  36.6 0.0 collective-permute-done.2.got_1
  36.6 0.0 collective-permute-done.3.got_2
  36.6 4.9 %shard_map.122 = bf16[64,16,1280]{2,1,0:T(8,128)(2,1)} custom-call(bf16[768,1280]{1,0:T(8,128)(2,1)S(1)} %get-tuple-element.27.zi, bf16[256,1408]{1,0:T(8,128)(2,1)S(1)} %get-tuple-element.28.edge, bf16[512,1408]{1,0:T(8,128)(2,1)S(1)} %get-tuple-element.21.cond, bf16[1024,128]{1,0:T(8,128)(2,1)S(1)} %get-tuple-element.22.halo, ...), custom_call_target="tpu_custom_call" | custom-call | tf_op jit(solution)/shard_map/pallas_call | solution.py:426
Async XLA Ops:
  2.3 19.7 %all-to-all-start = ((bf16[16,144,128]{2,1,0:T(8,128)(2,1)}), bf16[16,144,128]{2,1,0:T(8,128)(2,1)S(1)}, u32[]{:S(2)}, u32[]{:S(2)}) async-start(bf16[16,144,128]{2,1,0:T(8,128)(2,1)} %shard_map.118), calls=%async_computation | async-start | bytes 1179648 | tf_op jit(solution)/shard_map/all_to_all | solution.py:453
  14.6 15.9 %collective-permute-start = (bf16[128,1280]{1,0:T(8,128)(2,1)}, bf16[128,1280]{1,0:T(8,128)(2,1)}, u32[]{:S(2)}, u32[]{:S(2)}) collective-permute-start(bf16[128,1280]{1,0:T(8,128)(2,1)} %get-tuple-element.26), channel_id=1, source_target_pairs={{16,32},{32,16},{48,64},{64,48},{80,96},{96,80},{17,33},{33,17},{4... | collective-permute-start | bytes 983048 | tf_op jit(solution)/shard_map/ppermute | solution.py:444
  18.5 18.0 %collective-permute-start.1 = (bf16[128,1280]{1,0:T(8,128)(2,1)}, bf16[128,1280]{1,0:T(8,128)(2,1)S(1)}, u32[]{:S(2)}, u32[]{:S(2)}) collective-permute-start(bf16[128,1280]{1,0:T(8,128)(2,1)} %get-tuple-element.29), channel_id=1, source_target_pairs={{0,16},{16,0},{32,48},{48,32},{64,80},{80,64},{96,112},{112,96},{1... | collective-permute-start | bytes 983048 | tf_op jit(solution)/shard_map/ppermute | solution.py:443
  25.3 11.3 %collective-permute-start.2 = (bf16[64,1664]{1,0:T(8,128)(2,1)S(1)}, bf16[64,1664]{1,0:T(8,128)(2,1)S(1)}, u32[]{:S(2)}, u32[]{:S(2)}) collective-permute-start(bf16[64,1664]{1,0:T(8,128)(2,1)S(1)} %get-tuple-element.31), channel_id=1, source_target_pairs={{0,16},{16,0},{32,48},{48,32},{64,80},{80,64},{96,112},{112,96},{1... | collective-permute-start | bytes 638984 | tf_op jit(solution)/shard_map/ppermute | solution.py:443
  27.5 9.1 %collective-permute-start.3 = (bf16[64,1664]{1,0:T(8,128)(2,1)S(1)}, bf16[64,1664]{1,0:T(8,128)(2,1)S(1)}, u32[]{:S(2)}, u32[]{:S(2)}) collective-permute-start(bf16[64,1664]{1,0:T(8,128)(2,1)S(1)} %get-tuple-element.32), channel_id=1, source_target_pairs={{16,32},{32,16},{48,64},{64,48},{80,96},{96,80},{17,33},{33,17},{4... | collective-permute-start | bytes 638984 | tf_op jit(solution)/shard_map/ppermute | solution.py:444

commit v7 on v5

--- a/solution.py
+++ b/solution.py
@@ -221,16 +221,16 @@
 
 
 def cond_kernel(got, table_hbm, wts_hbm, bias_hbm, cond, halo, first, second, wts, bias, acc, grp, ints, lists, table, sem, sems):
-    loads = []
-    for r in range(R // SUBS):
-        loads.append(load(table_hbm.at[:, pl.ds(r * W, W)], table.at[r], sems.at[r]))
-    others = [load(wts_hbm, wts, sems.at[R // SUBS]), load(bias_hbm, bias, sems.at[R // SUBS + 1])]
     me = lax.axis_index("lon")
     left = lax.rem(me + PEERS - 1, PEERS)
     right = lax.rem(me + 1, PEERS)
     for d, p in enumerate((me, left, right)):
         ints[d] = got[p, CP - 16 : CP, :].astype(F32).astype(jnp.int32)
     copy = load(ints, lists, sem)
+    loads = []
+    for r in range(R // SUBS):
+        loads.append(load(table_hbm.at[:, pl.ds(r * W, W)], table.at[r], sems.at[r]))
+    others = [load(wts_hbm, wts, sems.at[R // SUBS]), load(bias_hbm, bias, sems.at[R // SUBS + 1])]
     acc[...] = jnp.zeros_like(acc)
 
     rows = []
@@ -268,10 +268,14 @@
         if r % 2 == 0:
             loads[r].wait()
             loads[r + 1].wait()
+            lt = jnp.concatenate([table[q, :, W - LT : W] for q in (r, r + 1)], axis=1)
+            rt = jnp.concatenate([table[q, :, 0:LT] for q in (r, r + 1)], axis=1)
+            lhs_2 = jnp.dot(grp[1], lt, preferred_element_type=F32)
+            rhs_2 = jnp.dot(grp[2], rt, preferred_element_type=F32)
         part = table.at[r]
+        tile = slice(r % 2 * LT, (r % 2 + 1) * LT)
         own = jnp.dot(grp[0], part[...], preferred_element_type=F32).astype(BF)
-        lhs = jnp.dot(grp[1], part[:, W - LT : W], preferred_element_type=F32)
-        rhs = jnp.dot(grp[2], part[:, 0:LT], preferred_element_type=F32)
+        lhs, rhs = lhs_2[:, tile], rhs_2[:, tile]
         side = jnp.where(lane < 2, rhs, jnp.where(lane >= 126, lhs, 0.0)).astype(BF)
         for s in range(SUBS):
             at = pl.ds((s * SUBS + r) * CP, CP)

time: 41.7 us -> 41.6 us (level)
  no operation moved by 1% of the time
where the time goes in v7:
time: 41.6 us; the launch traced here: 41.3 us
  Pallas kernels  19.8 us (48%)
  starting transfers between devices  17.9 us (43%)
  waiting for transfers between devices  3.38 us (8%)
    all_to_all x1, starting transfers between devices, local(): got = lax.all_to_all(msg, 'lon', split_axis=0, concat_axis=0, tiled=True)  8.61 us
    ppermute x2, starting transfers between devices, exchanged(): lax.ppermute(second, 'lat', [(i, (i + 1 ^ 1) - 1) for i in range(1, count...  6.98 us
    pallas_call x1, Pallas kernels, inner_rows(): pl.pallas_call(inner_kernel, out_shape=(kept(((R - 4) * C, W)), kept((4 *...  6.04 us
    pallas_call x1, Pallas kernels, outer_rows(): pl.pallas_call(outer_kernel, out_shape=pltpu.HBM((C, R, W), BF), in_specs...  4.58 us
    pallas_call x1, Pallas kernels, turned(): pl.pallas_call(kernel, out_shape=(kept((R * C, W)), pltpu.HBM((2 * C, W),...  3.63 us
    all_to_all x1, waiting for transfers between devices, local(): got = lax.all_to_all(msg, 'lon', split_axis=0, concat_axis=0, tiled=True)  3.37 us
    pallas_call x1, Pallas kernels, cond_tile(): pl.pallas_call(cond_kernel, out_shape=(kept((R * CP, WX)), kept((R * C, L...  3.24 us
    pallas_call x1, Pallas kernels, message(): pl.pallas_call(kernel, out_shape=kept((PEERS, MSG, LT)), in_specs=hbm(6),...  2.31 us
  transfers between devices with their start and end apart: 5, of which 1 were waited for; matrix products, arithmetic and copies ran while one was open for 0% of the time, Pallas kernels for 31%

profile of v7, /device:TPU:1, one launch (start us, length us, event | category | flops | bytes accessed | tf_op | source)
XLA Modules:
  0.0 41.3 jit_solution(13445290071706085564)
XLA Ops:
  0.0 2.3 %shard_map.118 = bf16[16,144,128]{2,1,0:T(8,128)(2,1)} custom-call(bf16[64,16,1280]{2,1,0:T(8,128)(2,1)} %noisy_ref.3, bf16[1,30,4,128]{3,2,1,0:T(4,128)(2,1)} %bitcast.6, s32[1,1,4,4]{3,2,1,0:T(4,128)} %owner.1, s32[1,1,4,4]{3,2,1,0:T(4,128)} %slot.1, s32[1,1,4,4]{3,2,1,0:T(4,128)} %weight.1, s32[1,1,4]{2,1,0:T(1,128)} %counts.1), custom_call_target="tpu_custom_call" | custom-call | tf_op jit(solution)/shard_map/pallas_call | solution.py:116
  2.3 8.6 %all-to-all-start = ((bf16[16,144,128]{2,1,0:T(8,128)(2,1)}), bf16[16,144,128]{2,1,0:T(8,128)(2,1)S(1)}, u32[]{:S(2)}, u32[]{:S(2)}) async-start(bf16[16,144,128]{2,1,0:T(8,128)(2,1)} %shard_map.118), calls=%async_computation | async-start | bytes 1179648 | tf_op jit(solution)/shard_map/all_to_all | solution.py:455
  10.9 3.6 %shard_map.119 = (bf16[1024,1280]{1,0:T(8,128)(2,1)S(1)}, bf16[128,1280]{1,0:T(8,128)(2,1)}, bf16[128,1280]{1,0:T(8,128)(2,1)}, bf16[128,1920]{1,0:T(8,128)(2,1)}, f32[128,256]{1,0:T(8,128)}) custom-call(bf16[64,16,1280]{2,1,0:T(8,128)(2,1)} %noisy_ref.3, bf16[3,3,64,64]{3,2,1,0:T(8,128)(2,1)} %refs_0_.1, bf16[3,3,30,64]{3,2,1,0:T(8,128)(2,1)} %bitcast.7, ...), custom_call_target="tpu_custom_call" | custom-call | flops 3000000000 | bytes 12000000 | tf_op jit(solution)/shard_map/pallas_call | solution.py:200
  14.6 4.0 %collective-permute-start = (bf16[128,1280]{1,0:T(8,128)(2,1)}, bf16[128,1280]{1,0:T(8,128)(2,1)}, u32[]{:S(2)}, u32[]{:S(2)}) collective-permute-start(bf16[128,1280]{1,0:T(8,128)(2,1)} %get-tuple-element.26), channel_id=1, source_target_pairs={{16,32},{32,16},{48,64},{64,48},{80,96},{96,80},{17,33},{33,17},{4... | collective-permute-start | bytes 983048 | tf_op jit(solution)/shard_map/ppermute | solution.py:446
  18.5 0.1 collective-permute-start.1
  18.6 3.4 %all-to-all-done.got = bf16[16,144,128]{2,1,0:T(8,128)(2,1)S(1)} async-done(((bf16[16,144,128]{2,1,0:T(8,128)(2,1)}), bf16[16,144,128]{2,1,0:T(8,128)(2,1)S(1)}, u32[]{:S(2)}, u32[]{:S(2)}) %all-to-all-start) | async-done | bytes 589856 | tf_op jit(solution)/shard_map/all_to_all | solution.py:455
  22.0 3.2 %shard_map.120 = (bf16[512,1408]{1,0:T(8,128)(2,1)S(1)}, bf16[1024,128]{1,0:T(8,128)(2,1)S(1)}, bf16[64,1664]{1,0:T(8,128)(2,1)S(1)}, bf16[64,1664]{1,0:T(8,128)...) custom-call(bf16[16,144,128]{2,1,0:T(8,128)(2,1)S(1)} %all-to-all-done.got, bf16[512,5120]{1,0:T(8,128)(2,1)} %bitcast.5, ...), custom_call_target="tpu_custom_call" | custom-call | tf_op jit(solution)/shard_map/pallas_call | solution.py:294
  25.3 2.2 %collective-permute-start.2 = (bf16[64,1664]{1,0:T(8,128)(2,1)S(1)}, bf16[64,1664]{1,0:T(8,128)(2,1)S(1)}, u32[]{:S(2)}, u32[]{:S(2)}) collective-permute-start(bf16[64,1664]{1,0:T(8,128)(2,1)S(1)} %get-tuple-element.31), channel_id=1, source_target_pairs={{0,16},{16,0},{32,48},{48,32},{64,80},{80,64},{96,112},{112,96},{1... | collective-permute-start | bytes 638984 | tf_op jit(solution)/shard_map/ppermute | solution.py:445
  27.5 3.0 %collective-permute-start.3 = (bf16[64,1664]{1,0:T(8,128)(2,1)S(1)}, bf16[64,1664]{1,0:T(8,128)(2,1)S(1)}, u32[]{:S(2)}, u32[]{:S(2)}) collective-permute-start(bf16[64,1664]{1,0:T(8,128)(2,1)S(1)} %get-tuple-element.32), channel_id=1, source_target_pairs={{16,32},{32,16},{48,64},{64,48},{80,96},{96,80},{17,33},{33,17},{4... | collective-permute-start | bytes 638984 | tf_op jit(solution)/shard_map/ppermute | solution.py:446
  30.5 0.0 collective-permute-done.noisy_hbm
  30.5 6.0 %shard_map.121 = (bf16[768,1280]{1,0:T(8,128)(2,1)S(1)}, bf16[256,1408]{1,0:T(8,128)(2,1)S(1)}, bf16[128,1280]{1,0:T(8,128)(2,1)S(1)}) custom-call(bf16[512,1408]{1,0:T(8,128)(2,1)S(1)} %get-tuple-element.21.cond, bf16[1024,128]{1,0:T(8,128)(2,1)S(1)} %get-tuple-element.22.halo, bf16[1024,1280]{1,0:T(8,128)(2,1)S(1)} %get-tuple-element.23.xs, ...), custom_call_target="tpu_custom_call" | custom-call | flops 6000000000 | bytes 12000000 | tf_op jit(solution)/shard_map/pallas_call | solution.py:368
  36.6 0.0 collective-permute-done.1.noisy_1
  36.6 0.0 collective-permute-done.2.got_1
  36.6 0.0 collective-permute-done.3.got_2
  36.6 4.6 %shard_map.122 = bf16[64,16,1280]{2,1,0:T(8,128)(2,1)} custom-call(bf16[768,1280]{1,0:T(8,128)(2,1)S(1)} %get-tuple-element.27.zi, bf16[256,1408]{1,0:T(8,128)(2,1)S(1)} %get-tuple-element.28.edge, bf16[512,1408]{1,0:T(8,128)(2,1)S(1)} %get-tuple-element.21.cond, bf16[1024,128]{1,0:T(8,128)(2,1)S(1)} %get-tuple-element.22.halo, ...), custom_call_target="tpu_custom_call" | custom-call | tf_op jit(solution)/shard_map/pallas_call | solution.py:428
Async XLA Ops:
  2.3 19.7 %all-to-all-start = ((bf16[16,144,128]{2,1,0:T(8,128)(2,1)}), bf16[16,144,128]{2,1,0:T(8,128)(2,1)S(1)}, u32[]{:S(2)}, u32[]{:S(2)}) async-start(bf16[16,144,128]{2,1,0:T(8,128)(2,1)} %shard_map.118), calls=%async_computation | async-start | bytes 1179648 | tf_op jit(solution)/shard_map/all_to_all | solution.py:455
  14.6 15.9 %collective-permute-start = (bf16[128,1280]{1,0:T(8,128)(2,1)}, bf16[128,1280]{1,0:T(8,128)(2,1)}, u32[]{:S(2)}, u32[]{:S(2)}) collective-permute-start(bf16[128,1280]{1,0:T(8,128)(2,1)} %get-tuple-element.26), channel_id=1, source_target_pairs={{16,32},{32,16},{48,64},{64,48},{80,96},{96,80},{17,33},{33,17},{4... | collective-permute-start | bytes 983048 | tf_op jit(solution)/shard_map/ppermute | solution.py:446
  18.5 18.0 %collective-permute-start.1 = (bf16[128,1280]{1,0:T(8,128)(2,1)}, bf16[128,1280]{1,0:T(8,128)(2,1)S(1)}, u32[]{:S(2)}, u32[]{:S(2)}) collective-permute-start(bf16[128,1280]{1,0:T(8,128)(2,1)} %get-tuple-element.29), channel_id=1, source_target_pairs={{0,16},{16,0},{32,48},{48,32},{64,80},{80,64},{96,112},{112,96},{1... | collective-permute-start | bytes 983048 | tf_op jit(solution)/shard_map/ppermute | solution.py:445
  25.3 11.3 %collective-permute-start.2 = (bf16[64,1664]{1,0:T(8,128)(2,1)S(1)}, bf16[64,1664]{1,0:T(8,128)(2,1)S(1)}, u32[]{:S(2)}, u32[]{:S(2)}) collective-permute-start(bf16[64,1664]{1,0:T(8,128)(2,1)S(1)} %get-tuple-element.31), channel_id=1, source_target_pairs={{0,16},{16,0},{32,48},{48,32},{64,80},{80,64},{96,112},{112,96},{1... | collective-permute-start | bytes 638984 | tf_op jit(solution)/shard_map/ppermute | solution.py:445
  27.5 9.1 %collective-permute-start.3 = (bf16[64,1664]{1,0:T(8,128)(2,1)S(1)}, bf16[64,1664]{1,0:T(8,128)(2,1)S(1)}, u32[]{:S(2)}, u32[]{:S(2)}) collective-permute-start(bf16[64,1664]{1,0:T(8,128)(2,1)S(1)} %get-tuple-element.32), channel_id=1, source_target_pairs={{16,32},{32,16},{48,64},{64,48},{80,96},{96,80},{17,33},{33,17},{4... | collective-permute-start | bytes 638984 | tf_op jit(solution)/shard_map/ppermute | solution.py:446

commit v8 on v7

--- a/solution.py
+++ b/solution.py
@@ -265,22 +265,20 @@
 
     lane = iota((SUBS * CP, LT), 1)
     for r in range(R // SUBS):
-        if r % 2 == 0:
-            loads[r].wait()
-            loads[r + 1].wait()
-            lt = jnp.concatenate([table[q, :, W - LT : W] for q in (r, r + 1)], axis=1)
-            rt = jnp.concatenate([table[q, :, 0:LT] for q in (r, r + 1)], axis=1)
-            lhs_2 = jnp.dot(grp[1], lt, preferred_element_type=F32)
-            rhs_2 = jnp.dot(grp[2], rt, preferred_element_type=F32)
-        part = table.at[r]
-        tile = slice(r % 2 * LT, (r % 2 + 1) * LT)
-        own = jnp.dot(grp[0], part[...], preferred_element_type=F32).astype(BF)
-        lhs, rhs = lhs_2[:, tile], rhs_2[:, tile]
-        side = jnp.where(lane < 2, rhs, jnp.where(lane >= 126, lhs, 0.0)).astype(BF)
+        loads[r].wait()
+        own = jnp.dot(grp[0], table[r], preferred_element_type=F32).astype(BF)
         for s in range(SUBS):
-            at = pl.ds((s * SUBS + r) * CP, CP)
-            cond[at, 0:W] = own[s * CP : (s + 1) * CP]
-            cond[at, W:WX] = side[s * CP : (s + 1) * CP]
+            cond[pl.ds((s * SUBS + r) * CP, CP), 0:W] = own[s * CP : (s + 1) * CP]
+        if r % 2 == 1:
+            lt = jnp.concatenate([table[q, :, W - LT : W] for q in (r - 1, r)], axis=1)
+            rt = jnp.concatenate([table[q, :, 0:LT] for q in (r - 1, r)], axis=1)
+            lhs = jnp.dot(grp[1], lt, preferred_element_type=F32)
+            rhs = jnp.dot(grp[2], rt, preferred_element_type=F32)
+            for j in range(2):
+                tile = slice(j * LT, (j + 1) * LT)
+                side = jnp.where(lane < 2, rhs[:, tile], jnp.where(lane >= 126, lhs[:, tile], 0.0)).astype(BF)
+                for s in range(SUBS):
+                    cond[pl.ds((s * SUBS + r - 1 + j) * CP, CP), W:WX] = side[s * CP : (s + 1) * CP]
     for out, r0 in zip((first, second), near_rows()):
         out[:, 0:WX] = cond[pl.ds(pl.multiple_of(r0 * CP, CP), 2 * CP), :]
         for j in range(2):

time: 41.6 us -> 41.6 us (level)
  no operation moved by 1% of the time
where the time goes in v8:
time: 41.6 us; the launch traced here: 41.4 us
  Pallas kernels  19.9 us (48%)
  starting transfers between devices  17.9 us (43%)
  waiting for transfers between devices  3.38 us (8%)
    all_to_all x1, starting transfers between devices, local(): got = lax.all_to_all(msg, 'lon', split_axis=0, concat_axis=0, tiled=True)  8.61 us
    ppermute x2, starting transfers between devices, exchanged(): lax.ppermute(second, 'lat', [(i, (i + 1 ^ 1) - 1) for i in range(1, count...  6.98 us
    pallas_call x1, Pallas kernels, inner_rows(): pl.pallas_call(inner_kernel, out_shape=(kept(((R - 4) * C, W)), kept((4 *...  6.04 us
    pallas_call x1, Pallas kernels, outer_rows(): pl.pallas_call(outer_kernel, out_shape=pltpu.HBM((C, R, W), BF), in_specs...  4.58 us
    pallas_call x1, Pallas kernels, turned(): pl.pallas_call(kernel, out_shape=(kept((R * C, W)), pltpu.HBM((2 * C, W),...  3.63 us
    all_to_all x1, waiting for transfers between devices, local(): got = lax.all_to_all(msg, 'lon', split_axis=0, concat_axis=0, tiled=True)  3.37 us
    pallas_call x1, Pallas kernels, cond_tile(): pl.pallas_call(cond_kernel, out_shape=(kept((R * CP, WX)), kept((R * C, L...  3.29 us
    pallas_call x1, Pallas kernels, message(): pl.pallas_call(kernel, out_shape=kept((PEERS, MSG, LT)), in_specs=hbm(6),...  2.31 us
  transfers between devices with their start and end apart: 5, of which 1 were waited for; matrix products, arithmetic and copies ran while one was open for 0% of the time, Pallas kernels for 31%

profile of v8, /device:TPU:1, one launch (start us, length us, event | category | flops | bytes accessed | tf_op | source)
XLA Modules:
  0.0 41.4 jit_solution(5719754203075143076)
XLA Ops:
  0.0 2.3 %shard_map.118 = bf16[16,144,128]{2,1,0:T(8,128)(2,1)} custom-call(bf16[64,16,1280]{2,1,0:T(8,128)(2,1)} %noisy_ref.3, bf16[1,30,4,128]{3,2,1,0:T(4,128)(2,1)} %bitcast.6, s32[1,1,4,4]{3,2,1,0:T(4,128)} %owner.1, s32[1,1,4,4]{3,2,1,0:T(4,128)} %slot.1, s32[1,1,4,4]{3,2,1,0:T(4,128)} %weight.1, s32[1,1,4]{2,1,0:T(1,128)} %counts.1), custom_call_target="tpu_custom_call" | custom-call | tf_op jit(solution)/shard_map/pallas_call | solution.py:116
  2.3 8.6 %all-to-all-start = ((bf16[16,144,128]{2,1,0:T(8,128)(2,1)}), bf16[16,144,128]{2,1,0:T(8,128)(2,1)S(1)}, u32[]{:S(2)}, u32[]{:S(2)}) async-start(bf16[16,144,128]{2,1,0:T(8,128)(2,1)} %shard_map.118), calls=%async_computation | async-start | bytes 1179648 | tf_op jit(solution)/shard_map/all_to_all | solution.py:453
  10.9 3.6 %shard_map.119 = (bf16[1024,1280]{1,0:T(8,128)(2,1)S(1)}, bf16[128,1280]{1,0:T(8,128)(2,1)}, bf16[128,1280]{1,0:T(8,128)(2,1)}, bf16[128,1920]{1,0:T(8,128)(2,1)}, f32[128,256]{1,0:T(8,128)}) custom-call(bf16[64,16,1280]{2,1,0:T(8,128)(2,1)} %noisy_ref.3, bf16[3,3,64,64]{3,2,1,0:T(8,128)(2,1)} %refs_0_.1, bf16[3,3,30,64]{3,2,1,0:T(8,128)(2,1)} %bitcast.7, ...), custom_call_target="tpu_custom_call" | custom-call | flops 3000000000 | bytes 12000000 | tf_op jit(solution)/shard_map/pallas_call | solution.py:200
  14.6 4.0 %collective-permute-start = (bf16[128,1280]{1,0:T(8,128)(2,1)}, bf16[128,1280]{1,0:T(8,128)(2,1)}, u32[]{:S(2)}, u32[]{:S(2)}) collective-permute-start(bf16[128,1280]{1,0:T(8,128)(2,1)} %get-tuple-element.26), channel_id=1, source_target_pairs={{16,32},{32,16},{48,64},{64,48},{80,96},{96,80},{17,33},{33,17},{4... | collective-permute-start | bytes 983048 | tf_op jit(solution)/shard_map/ppermute | solution.py:444
  18.5 0.1 collective-permute-start.1
  18.6 3.4 %all-to-all-done.got = bf16[16,144,128]{2,1,0:T(8,128)(2,1)S(1)} async-done(((bf16[16,144,128]{2,1,0:T(8,128)(2,1)}), bf16[16,144,128]{2,1,0:T(8,128)(2,1)S(1)}, u32[]{:S(2)}, u32[]{:S(2)}) %all-to-all-start) | async-done | bytes 589856 | tf_op jit(solution)/shard_map/all_to_all | solution.py:453
  22.0 3.3 %shard_map.120 = (bf16[512,1408]{1,0:T(8,128)(2,1)S(1)}, bf16[1024,128]{1,0:T(8,128)(2,1)S(1)}, bf16[64,1664]{1,0:T(8,128)(2,1)S(1)}, bf16[64,1664]{1,0:T(8,128)...) custom-call(bf16[16,144,128]{2,1,0:T(8,128)(2,1)S(1)} %all-to-all-done.got, bf16[512,5120]{1,0:T(8,128)(2,1)} %bitcast.5, ...), custom_call_target="tpu_custom_call" | custom-call | tf_op jit(solution)/shard_map/pallas_call | solution.py:292
  25.3 2.2 %collective-permute-start.2 = (bf16[64,1664]{1,0:T(8,128)(2,1)S(1)}, bf16[64,1664]{1,0:T(8,128)(2,1)S(1)}, u32[]{:S(2)}, u32[]{:S(2)}) collective-permute-start(bf16[64,1664]{1,0:T(8,128)(2,1)S(1)} %get-tuple-element.31), channel_id=1, source_target_pairs={{0,16},{16,0},{32,48},{48,32},{64,80},{80,64},{96,112},{112,96},{1... | collective-permute-start | bytes 638984 | tf_op jit(solution)/shard_map/ppermute | solution.py:443
  27.5 3.0 %collective-permute-start.3 = (bf16[64,1664]{1,0:T(8,128)(2,1)S(1)}, bf16[64,1664]{1,0:T(8,128)(2,1)S(1)}, u32[]{:S(2)}, u32[]{:S(2)}) collective-permute-start(bf16[64,1664]{1,0:T(8,128)(2,1)S(1)} %get-tuple-element.32), channel_id=1, source_target_pairs={{16,32},{32,16},{48,64},{64,48},{80,96},{96,80},{17,33},{33,17},{4... | collective-permute-start | bytes 638984 | tf_op jit(solution)/shard_map/ppermute | solution.py:444
  30.5 0.0 collective-permute-done.noisy_hbm
  30.6 6.0 %shard_map.121 = (bf16[768,1280]{1,0:T(8,128)(2,1)S(1)}, bf16[256,1408]{1,0:T(8,128)(2,1)S(1)}, bf16[128,1280]{1,0:T(8,128)(2,1)S(1)}) custom-call(bf16[512,1408]{1,0:T(8,128)(2,1)S(1)} %get-tuple-element.21.cond, bf16[1024,128]{1,0:T(8,128)(2,1)S(1)} %get-tuple-element.22.halo, bf16[1024,1280]{1,0:T(8,128)(2,1)S(1)} %get-tuple-element.23.xs, ...), custom_call_target="tpu_custom_call" | custom-call | flops 6000000000 | bytes 12000000 | tf_op jit(solution)/shard_map/pallas_call | solution.py:366
  36.6 0.0 collective-permute-done.1.noisy_1
  36.6 0.0 collective-permute-done.2.got_1
  36.6 0.0 collective-permute-done.3.got_2
  36.6 4.6 %shard_map.122 = bf16[64,16,1280]{2,1,0:T(8,128)(2,1)} custom-call(bf16[768,1280]{1,0:T(8,128)(2,1)S(1)} %get-tuple-element.27.zi, bf16[256,1408]{1,0:T(8,128)(2,1)S(1)} %get-tuple-element.28.edge, bf16[512,1408]{1,0:T(8,128)(2,1)S(1)} %get-tuple-element.21.cond, bf16[1024,128]{1,0:T(8,128)(2,1)S(1)} %get-tuple-element.22.halo, ...), custom_call_target="tpu_custom_call" | custom-call | tf_op jit(solution)/shard_map/pallas_call | solution.py:426
Async XLA Ops:
  2.3 19.7 %all-to-all-start = ((bf16[16,144,128]{2,1,0:T(8,128)(2,1)}), bf16[16,144,128]{2,1,0:T(8,128)(2,1)S(1)}, u32[]{:S(2)}, u32[]{:S(2)}) async-start(bf16[16,144,128]{2,1,0:T(8,128)(2,1)} %shard_map.118), calls=%async_computation | async-start | bytes 1179648 | tf_op jit(solution)/shard_map/all_to_all | solution.py:453
  14.6 16.0 %collective-permute-start = (bf16[128,1280]{1,0:T(8,128)(2,1)}, bf16[128,1280]{1,0:T(8,128)(2,1)}, u32[]{:S(2)}, u32[]{:S(2)}) collective-permute-start(bf16[128,1280]{1,0:T(8,128)(2,1)} %get-tuple-element.26), channel_id=1, source_target_pairs={{16,32},{32,16},{48,64},{64,48},{80,96},{96,80},{17,33},{33,17},{4... | collective-permute-start | bytes 983048 | tf_op jit(solution)/shard_map/ppermute | solution.py:444
  18.5 18.1 %collective-permute-start.1 = (bf16[128,1280]{1,0:T(8,128)(2,1)}, bf16[128,1280]{1,0:T(8,128)(2,1)S(1)}, u32[]{:S(2)}, u32[]{:S(2)}) collective-permute-start(bf16[128,1280]{1,0:T(8,128)(2,1)} %get-tuple-element.29), channel_id=1, source_target_pairs={{0,16},{16,0},{32,48},{48,32},{64,80},{80,64},{96,112},{112,96},{1... | collective-permute-start | bytes 983048 | tf_op jit(solution)/shard_map/ppermute | solution.py:443
  25.3 11.3 %collective-permute-start.2 = (bf16[64,1664]{1,0:T(8,128)(2,1)S(1)}, bf16[64,1664]{1,0:T(8,128)(2,1)S(1)}, u32[]{:S(2)}, u32[]{:S(2)}) collective-permute-start(bf16[64,1664]{1,0:T(8,128)(2,1)S(1)} %get-tuple-element.31), channel_id=1, source_target_pairs={{0,16},{16,0},{32,48},{48,32},{64,80},{80,64},{96,112},{112,96},{1... | collective-permute-start | bytes 638984 | tf_op jit(solution)/shard_map/ppermute | solution.py:443
  27.5 9.1 %collective-permute-start.3 = (bf16[64,1664]{1,0:T(8,128)(2,1)S(1)}, bf16[64,1664]{1,0:T(8,128)(2,1)S(1)}, u32[]{:S(2)}, u32[]{:S(2)}) collective-permute-start(bf16[64,1664]{1,0:T(8,128)(2,1)S(1)} %get-tuple-element.32), channel_id=1, source_target_pairs={{16,32},{32,16},{48,64},{64,48},{80,96},{96,80},{17,33},{33,17},{4... | collective-permute-start | bytes 638984 | tf_op jit(solution)/shard_map/ppermute | solution.py:444
